TPU v7x, 256 devices: a whole 4x4x8 slice. The times are simulated.
256 devices in a mesh: seq: 32 (over x, z_hi, y), chan: 8 (over z_lo, core).
Axes of the slice: x: 4, y: 4, z: 8 (z_hi: 2, z_lo: 4; z = z_hi * 4 + z_lo), core: 2. Of those that a mesh axis runs over, the one named last changes fastest.
Arguments:
- hyena_gate: bfloat16 [16384, 4096], P('seq', 'chan'), may hold values from -6 to 6
- hyena_key: bfloat16 [16384, 4096], P('seq', 'chan'), may hold values from -6 to 6
- hyena_value: bfloat16 [16384, 4096], P('seq', 'chan'), may hold values from -6 to 6
- long_filter: bfloat16 [16384, 4096], P('seq', 'chan'), may hold values from -0.046875 to 0.046875
- skip_weight: float32 [4096], P('chan'), may hold values from -4 to 4
- attn_query: bfloat16 [16384, 8, 1024], P('seq', 'chan'), may hold values from -4.5 to 4.5
- attn_keys: bfloat16 [16384, 1024], P('seq', 'chan'), may hold values from -4.5 to 4.5
- attn_values: bfloat16 [16384, 1024], P('seq', 'chan'), may hold values from -6 to 6
Outputs:
- hyena_out: bfloat16 [16384, 4096], P('seq', 'chan')
- attn_out: bfloat16 [16384, 8, 1024], P('seq', 'chan')
- attn_lse: float32 [8, 8, 16384], P('chan', None, 'seq')
All inputs are finite; a program needn't handle non-finite values.
Results may differ from a plain program's by a relative error of at most 0.0045.
Values may be sent and summed in bfloat16 or wider, within the bound.
No kernel may reach another device: no remote copies, remote signals or barrier semaphores. Data moves between devices by JAX's collectives and lax.ppermute only.
A program may use at most 128 MiB of HBM per device.

v0:
```python
import math

import jax
import jax.numpy as jnp
from jax import lax
from jax.sharding import PartitionSpec as P

KVH = 8
HD = 128


PRECISE = lax.Precision.HIGHEST


def from_behind(x, axis, by):
    devices = lax.axis_size(axis)
    pairs = [(i, i + by) for i in range(devices) if 0 <= i + by < devices]
    return lax.ppermute(x, axis, pairs)


def wave_table(row_ids, col_ids, period):
    phase = row_ids[:, None] * col_ids[None, :] % period
    angles = phase.astype(jnp.float32) * (2.0 * math.pi / period)
    return (jnp.cos(angles), jnp.sin(angles))


def pair_order(shard_count):
    first_half = jnp.arange(shard_count, dtype=jnp.int32)
    partner = jnp.where(first_half == 0, shard_count, 2 * shard_count - first_half)
    return jnp.stack([first_half, partner], axis=1).reshape(-1)


def line_transform(real_part, imag_part, sign):
    length = real_part.shape[1]
    index = jnp.arange(length, dtype=jnp.int32)
    line_cos, line_sin = wave_table(index, index, length)
    cos_re = jnp.einsum("da,cak->cdk", line_cos, real_part, precision=PRECISE)
    cos_im = jnp.einsum("da,cak->cdk", line_cos, imag_part, precision=PRECISE)
    sin_re = jnp.einsum("da,cak->cdk", line_sin, real_part, precision=PRECISE)
    sin_im = jnp.einsum("da,cak->cdk", line_sin, imag_part, precision=PRECISE)
    return (cos_re + sign * sin_im, cos_im - sign * sin_re)


def long_conv(signal, kernel):
    shard_count = lax.axis_size("seq")
    my_index = lax.axis_index("seq")
    length, channels = signal.shape
    piece_len = length // shard_count
    full_span = 2 * shard_count * length
    freq_order = pair_order(shard_count)
    stacked = jnp.concatenate([signal, kernel], axis=1).reshape(
        shard_count, piece_len, 2 * channels
    )
    blocks = lax.all_to_all(stacked, "seq", split_axis=0, concat_axis=0, tiled=True)
    first_cos, first_sin = wave_table(
        freq_order, jnp.arange(shard_count, dtype=jnp.int32), 2 * shard_count
    )
    spread_re = jnp.einsum("cb,bwk->cwk", first_cos, blocks, precision=PRECISE)
    spread_im = -jnp.einsum("cb,bwk->cwk", first_sin, blocks, precision=PRECISE)
    positions = my_index * piece_len + jnp.arange(piece_len, dtype=jnp.int32)
    twist_cos, twist_sin = wave_table(freq_order, positions, full_span)
    twist_cos = twist_cos[:, :, None]
    twist_sin = twist_sin[:, :, None]
    turned_re = spread_re * twist_cos + spread_im * twist_sin
    turned_im = spread_im * twist_cos - spread_re * twist_sin
    recv_re, recv_im = (
        lax.all_to_all(turned_re, "seq", split_axis=0, concat_axis=1, tiled=True),
        lax.all_to_all(turned_im, "seq", split_axis=0, concat_axis=1, tiled=True),
    )
    full_re, full_im = line_transform(recv_re, recv_im, 1.0)
    sig_re = full_re[..., :channels]
    sig_im = full_im[..., :channels]
    ker_re = full_re[..., channels:]
    ker_im = full_im[..., channels:]
    prod_re = sig_re * ker_re - sig_im * ker_im
    prod_im = sig_re * ker_im + sig_im * ker_re
    back_re, back_im = line_transform(prod_re, prod_im, -1.0)
    slot_freq = jnp.stack(
        [my_index, jnp.where(my_index == 0, shard_count, 2 * shard_count - my_index)]
    )
    back_cos, back_sin = wave_table(slot_freq, jnp.arange(length, dtype=jnp.int32), full_span)
    back_cos = back_cos[:, :, None]
    back_sin = back_sin[:, :, None]
    reverted_re = back_re * back_cos - back_im * back_sin
    reverted_im = back_im * back_cos + back_re * back_sin
    final_re, final_im = (
        lax.all_to_all(reverted_re, "seq", split_axis=1, concat_axis=0, tiled=True),
        lax.all_to_all(reverted_im, "seq", split_axis=1, concat_axis=0, tiled=True),
    )
    last_cos, last_sin = wave_table(
        jnp.arange(shard_count, dtype=jnp.int32), freq_order, 2 * shard_count
    )
    values = jnp.einsum("bc,cwk->bwk", last_cos, final_re, precision=PRECISE)
    values = values - jnp.einsum("bc,cwk->bwk", last_sin, final_im, precision=PRECISE)
    values = values * (1.0 / full_span)
    placed = lax.all_to_all(values, "seq", split_axis=0, concat_axis=1, tiled=True)
    return placed.reshape(length, channels)


def attend(attn_query, window, my_index):
    tokens, groups, features = attn_query.shape
    queries = attn_query.reshape(tokens, groups, KVH, HD)
    key_rows = window[0].reshape(2 * tokens, KVH, HD)
    value_rows = window[1].reshape(2 * tokens, KVH, HD)
    scores = jnp.einsum(
        "tgjd,sjd->gjts", queries, key_rows, preferred_element_type=jnp.float32
    ) * HD ** (-0.5)
    key_pos = jnp.arange(2 * tokens, dtype=jnp.int32) - tokens
    query_pos = jnp.arange(tokens, dtype=jnp.int32)
    allowed = (key_pos[None, :] <= query_pos[:, None]) & ((key_pos[None, :] >= 0) | (my_index > 0))
    scores = jnp.where(allowed, scores, jnp.float32(-1e30))
    row_peak = jnp.max(scores, axis=-1)
    expd = jnp.exp(scores - row_peak[..., None])
    row_total = jnp.sum(expd, axis=-1)
    weights = expd.astype(jnp.bfloat16)
    mixed_sum = jnp.einsum(
        "gjts,sjd->tgjd", weights, value_rows, preferred_element_type=jnp.float32
    )
    normed = mixed_sum / row_total.transpose(2, 0, 1)[..., None]
    return (
        normed.astype(jnp.bfloat16).reshape(tokens, groups, features),
        row_peak + jnp.log(row_total),
    )


def local(
    hyena_gate, hyena_key, hyena_value, long_filter, skip_weight, attn_query, attn_keys, attn_values
):
    my_index = lax.axis_index("seq")
    signal = hyena_key.astype(jnp.float32) * hyena_value.astype(jnp.float32)
    kv_pair = jnp.stack([attn_keys, attn_values])
    all_heads = lax.all_gather(kv_pair, "chan", axis=2, tiled=True)
    behind = from_behind(all_heads, "seq", 1)
    window = jnp.concatenate([behind, all_heads], axis=1)
    conv = long_conv(signal, long_filter.astype(jnp.float32))
    hyena_out = (hyena_gate.astype(jnp.float32) * (conv + skip_weight * signal)).astype(
        jnp.bfloat16
    )
    attn_out, attn_lse = attend(attn_query, window, my_index)
    return (hyena_out, attn_out, attn_lse)


def solution(mesh):
    return jax.shard_map(
        local,
        mesh=mesh,
        in_specs=(
            P("seq", "chan"),
            P("seq", "chan"),
            P("seq", "chan"),
            P("seq", "chan"),
            P("chan"),
            P("seq", "chan", None),
            P("seq", "chan"),
            P("seq", "chan"),
        ),
        out_specs=(P("seq", "chan"), P("seq", "chan", None), P("chan", None, "seq")),
        check_vma=False,
    )
```

profile of v0, /device:TPU:224, one launch (start us, length us, event | category | flops | bytes accessed | tf_op | source)
XLA Modules:
  0.0 652.5 jit_solution(5925857923036416438)
XLA Ops:
  11.2 12.5 %all-to-all-start = ((f32[32,16,1024]{2,1,0:T(8,128)}), f32[32,16,1024]{2,1,0:T(8,128)S(1)}, u32[]{:S(2)}, u32[]{:S(2)}) async-start(f32[32,16,1024]{2,1,0:T(8,128)} %bitcast.130), calls=%async_computation | async-start | bytes 4194304 | tf_op jit(solution)/shard_map/all_to_all | solution.py:54
  24.0 43.7 %all-to-all-done = f32[32,16,1024]{2,1,0:T(8,128)S(1)} async-done(((f32[32,16,1024]{2,1,0:T(8,128)}), f32[32,16,1024]{2,1,0:T(8,128)S(1)}, u32[]{:S(2)}, u32[]{:S(2)}) %all-to-all-start) | async-done | bytes 2097184 | tf_op jit(solution)/shard_map/all_to_all | solution.py:54
  72.4 7.7 %multiply_add_fusion = (f32[64,16,1024]{2,0,1:T(8,128)S(1)}, f32[64,16,1024]{2,0,1:T(8,128)}) fusion(f32[64,16,1024]{2,0,1:T(8,128)S(1)} %fusion.9, f32[64,16]{0,1:T(8,128)S(1)} %get-tuple-element.24, f32[64,16]{0,1:T(8,128)S(1)} %get-tuple-element.23, f32[32,16,1024]{2,1,0:T(8,128)S(1)} %all-to-all-done, s32[64]{0:T(128)S(1)} %mul.302), kind=kOutput, calls=%fused_computation.11 | convolution fusion | flops 410021888 | bytes 14688512 | tf_op jit(solution)/shard_map/cb,bwk->cwk/dot_general | solution.py:58
  84.5 14.3 %all-to-all-start.1 = ((f32[64,16,1024]{2,1,0:T(8,128)}), f32[64,16,1024]{2,1,0:T(8,128)}, u32[]{:S(2)}, u32[]{:S(2)}) async-start(f32[64,16,1024]{2,1,0:T(8,128)} %copy.62), calls=%async_computation.1 | async-start | bytes 8388608 | tf_op jit(solution)/shard_map/all_to_all | solution.py:67
  105.3 33.0 %all-to-all-done.1 = f32[64,16,1024]{2,1,0:T(8,128)} async-done(((f32[64,16,1024]{2,1,0:T(8,128)}), f32[64,16,1024]{2,1,0:T(8,128)}, u32[]{:S(2)}, u32[]{:S(2)}) %all-to-all-start.1) | async-done | bytes 4194336 | tf_op jit(solution)/shard_map/all_to_all | solution.py:67
  138.3 70.3 %all-to-all-start.2 = ((f32[64,16,1024]{2,1,0:T(8,128)}), f32[64,16,1024]{2,1,0:T(8,128)}, u32[]{:S(2)}, u32[]{:S(2)}) async-start(f32[64,16,1024]{2,1,0:T(8,128)} %copy.65), calls=%async_computation.2 | async-start | bytes 8388608 | tf_op jit(solution)/shard_map/all_to_all | solution.py:68
  213.4 18.6 %fusion.31 = f32[2,1024,512]{2,1,0:T(8,128)} fusion(f32[2,512,1024]{2,1,0:T(8,128)S(1)} %bitcast.126), kind=kOutput, calls=%fused_computation.48 | convolution fusion | flops 6446120960 | bytes 8388608 | tf_op jit(solution)/shard_map/da,cak->cdk/dot_general | solution.py:37
  232.1 54.4 %all-to-all-done.2 = f32[64,16,1024]{2,1,0:T(8,128)} async-done(((f32[64,16,1024]{2,1,0:T(8,128)}), f32[64,16,1024]{2,1,0:T(8,128)}, u32[]{:S(2)}, u32[]{:S(2)}) %all-to-all-start.2) | async-done | bytes 4194336 | tf_op jit(solution)/shard_map/all_to_all | solution.py:68
  289.0 17.0 %fusion.29 = f32[2,1024,512]{2,1,0:T(8,128)S(1)} fusion(f32[2,512,1024]{2,1,0:T(8,128)S(1)} %bitcast.128), kind=kOutput, calls=%fused_computation.46 | convolution fusion | flops 6446120960 | bytes 8388608 | tf_op jit(solution)/shard_map/da,cak->cdk/dot_general | solution.py:38
  306.0 17.0 %add_bitcast_fusion = f32[2,512,1024]{1,2,0:T(8,128)S(1)} fusion(f32[2,1024,512]{2,1,0:T(8,128)S(1)} %copy-done.2, f32[2,512,1024]{2,1,0:T(8,128)S(1)} %bitcast.129), kind=kOutput, calls=%fused_computation.9 | convolution fusion | flops 6447169536 | bytes 12582912 | tf_op jit(solution)/shard_map/da,cak->cdk/dot_general | solution.py:40
  323.0 17.4 %subtract_bitcast_fusion = f32[2,512,1024]{1,2,0:T(8,128)S(1)} fusion(f32[2,1024,512]{2,1,0:T(8,128)S(1)} %fusion.29, f32[2,512,1024]{2,1,0:T(8,128)S(1)} %bitcast.127), kind=kOutput, calls=%fused_computation.8 | convolution fusion | flops 6447169536 | bytes 12582912 | tf_op jit(solution)/shard_map/da,cak->cdk/dot_general | solution.py:39
  341.5 8.4 %fusion.27 = f32[2,512,512]{2,1,0:T(8,128)S(1)} fusion(f32[2,512,512]{1,2,0:T(8,128)S(1)} %get-tuple-element.17), kind=kOutput, calls=%fused_computation.44 | convolution fusion | flops 3224895488 | bytes 4194304 | tf_op jit(solution)/shard_map/da,cak->cdk/dot_general | solution.py:37
  349.9 8.8 %fusion.25 = f32[2,512,512]{2,1,0:T(8,128)S(1)} fusion(f32[2,512,512]{1,2,0:T(8,128)S(1)} %get-tuple-element.18), kind=kOutput, calls=%fused_computation.42 | convolution fusion | flops 3224895488 | bytes 4194304 | tf_op jit(solution)/shard_map/da,cak->cdk/dot_general | solution.py:38
  358.7 8.5 %multiply_subtract_fusion.1 = f32[2,512,512]{2,1,0:T(8,128)S(1)} fusion(f32[2,512,512]{2,1,0:T(8,128)S(1)} %fusion.25, f32[2,512,512]{1,2,0:T(8,128)S(1)} %get-tuple-element.17), kind=kOutput, calls=%fused_computation.18 | convolution fusion | flops 3225944064 | bytes 6291456 | tf_op jit(solution)/shard_map/da,cak->cdk/dot_general | solution.py:39
  367.2 9.7 %add_bitcast_fusion.1 = (f32[2,512,512]{1,2,0:T(8,128)S(1)}, f32[2,512,512]{1,2,0:T(8,128)}) fusion(f32[2,512,512]{2,1,0:T(8,128)S(1)} %multiply_subtract_fusion.1, f32[2,512]{1,0:T(2,128)S(1)} %get-tuple-element.26, f32[2,512]{1,0:T(2,128)S(1)} %get-tuple-element.25, f32[2,512,512]{2,1,0:T(8,128)S(1)} %fusion.27, f32[2,512,512]{1,2,0:T(8,128)S(1)} %get-tuple-element.18), kind=kOutput, calls=%fused_computation.16 | convolution fusion | flops 3229089792 | bytes 10493952 | tf_op jit(solution)/shard_map/da,cak->cdk/dot_general | solution.py:40
  379.3 12.6 %all-to-all-start.4 = ((f32[2,512,512]{2,0,1:T(2,128)}), f32[2,512,512]{2,0,1:T(2,128)S(1)}, u32[]{:S(2)}, u32[]{:S(2)}) async-start(f32[2,512,512]{2,0,1:T(2,128)} %copy.73), calls=%async_computation.4 | async-start | bytes 4194304 | tf_op jit(solution)/shard_map/all_to_all | solution.py:88
  397.1 18.9 %all-to-all-done.4 = f32[2,512,512]{2,0,1:T(2,128)S(1)} async-done(((f32[2,512,512]{2,0,1:T(2,128)}), f32[2,512,512]{2,0,1:T(2,128)S(1)}, u32[]{:S(2)}, u32[]{:S(2)}) %all-to-all-start.4) | async-done | bytes 2097184 | tf_op jit(solution)/shard_map/all_to_all | solution.py:88
  416.0 14.3 %all-to-all-start.3 = ((f32[2,512,512]{2,0,1:T(2,128)}), f32[2,512,512]{2,0,1:T(2,128)}, u32[]{:S(2)}, u32[]{:S(2)}) async-start(f32[2,512,512]{2,0,1:T(2,128)} %copy.70), calls=%async_computation.3 | async-start | bytes 4194304 | tf_op jit(solution)/shard_map/all_to_all | solution.py:87
  430.3 24.8 %all-gather.2.cloned.1.call-done = bf16[2,512,1024]{1,2,0:T(8,128)(2,1)} async-done(((bf16[2,512,128]{1,2,0:T(8,128)(2,1)}), bf16[2,512,1024]{1,2,0:T(8,128)(2,1)}) %all-gather.2.cloned.1.call-update) | async-done | bytes 2097168 | tf_op jit(solution)/shard_map/all_gather | solution.py:132
  458.8 111.1 %collective-permute-done = bf16[2,512,1024]{1,2,0:T(8,128)(2,1)} collective-permute-done((bf16[2,512,1024]{1,2,0:T(8,128)(2,1)}, bf16[2,512,1024]{1,2,0:T(8,128)(2,1)}, u32[]{:S(2)}, u32[]{:S(2)}) %collective-permute-start) | collective-permute-done | bytes 2097184 | tf_op jit(solution)/shard_map/ppermute | solution.py:18
  573.8 7.6 %fusion.2 = (f32[8,512]{1,0:T(8,128)S(1)}, f32[8,1024,512]{2,1,0:T(8,128)}) fusion(pred[512,1024]{0,1:T(8,128)(4,1)S(1)} %fusion.8, bf16[1024,8,128]{0,2,1:T(8,128)(2,1)S(1)} %bitcast.131, bf16[512,8,128]{2,1,0:T(8,128)(2,1)S(1)} %bitcast.134), kind=kOutput, calls=%fused_computation.4 | convolution fusion | flops 1086320640 | bytes 20463616 | tf_op jit(solution)/shard_map/tgjd,sjd->gjts/dot_general | solution.py:105
  601.8 16.1 %all-to-all-start.5 = ((f32[32,16,512]{2,1,0:T(8,128)}), f32[32,16,512]{2,1,0:T(8,128)S(1)}, u32[]{:S(2)}, u32[]{:S(2)}) async-start(f32[32,16,512]{2,1,0:T(8,128)} %copy.76), calls=%async_computation.5 | async-start | bytes 2097152 | tf_op jit(solution)/shard_map/all_to_all | solution.py:96
  617.8 9.2 %fusion = f32[8,512]{1,0:T(8,128)S(1)} fusion(f32[8,1024,512]{2,1,0:T(8,128)} %get-tuple-element.28, f32[8,512]{1,0:T(8,128)S(1)} %get-tuple-element.27, pred[512,1024]{0,1:T(8,128)(4,1)S(1)} %fusion.8), kind=kLoop, calls=%fused_computation.2 | loop fusion | flops 16773120 | bytes 17334272 | tf_op jit(solution)/shard_map/reduce_sum | solution.py:114
  627.0 11.8 %fusion.7 = bf16[512,1,8,128]{0,3,2,1:T(8,128)(2,1)} fusion(bf16[1024,8,128]{0,2,1:T(8,128)(2,1)} %bitcast.135, f32[8,1024,512]{2,1,0:T(8,128)} %get-tuple-element.28, f32[8,512]{1,0:T(8,128)S(1)} %get-tuple-element.27, pred[512,1024]{0,1:T(8,128)(4,1)S(1)} %fusion.8, f32[512,8]{0,1:T(8,128)S(1)} %bitcast.140), kind=kOutput, calls=%fused_computation.14 | convolution fusion | flops 1091567616 | bytes 20480000 | tf_op jit(solution)/shard_map/gjts,sjd->tgjd/dot_general | solution.py:116
  (69 shorter events, 70.3 us)
Async XLA Ops:
  11.2 56.5 %all-to-all-start = ((f32[32,16,1024]{2,1,0:T(8,128)}), f32[32,16,1024]{2,1,0:T(8,128)S(1)}, u32[]{:S(2)}, u32[]{:S(2)}) async-start(f32[32,16,1024]{2,1,0:T(8,128)} %bitcast.130), calls=%async_computation | async-start | bytes 4194304 | tf_op jit(solution)/shard_map/all_to_all | solution.py:54
  84.5 53.9 %all-to-all-start.1 = ((f32[64,16,1024]{2,1,0:T(8,128)}), f32[64,16,1024]{2,1,0:T(8,128)}, u32[]{:S(2)}, u32[]{:S(2)}) async-start(f32[64,16,1024]{2,1,0:T(8,128)} %copy.62), calls=%async_computation.1 | async-start | bytes 8388608 | tf_op jit(solution)/shard_map/all_to_all | solution.py:67
  138.3 148.1 %all-to-all-start.2 = ((f32[64,16,1024]{2,1,0:T(8,128)}), f32[64,16,1024]{2,1,0:T(8,128)}, u32[]{:S(2)}, u32[]{:S(2)}) async-start(f32[64,16,1024]{2,1,0:T(8,128)} %copy.65), calls=%async_computation.2 | async-start | bytes 8388608 | tf_op jit(solution)/shard_map/all_to_all | solution.py:68
  211.4 2.0 copy-start
  289.0 17.0 %copy-start.2 = (f32[2,1024,512]{2,1,0:T(8,128)S(1)}, f32[2,1024,512]{2,1,0:T(8,128)}, u32[]{:S(2)}) copy-start(f32[2,1024,512]{2,1,0:T(8,128)} %fusion.31) | copy-start | bytes 12582916
  306.0 17.1 %copy-start.1 = (f32[2,32,16,1024]{3,2,1,0:T(8,128)S(1)}, f32[2,32,16,1024]{3,2,1,0:T(8,128)}, u32[]{:S(2)}) copy-start(f32[2,32,16,1024]{3,2,1,0:T(8,128)} %copy-done) | copy-start | bytes 12582916
  379.3 12.6 %copy-start.8 = (bf16[512,128]{1,0:T(8,128)(2,1)S(1)}, bf16[512,128]{1,0:T(8,128)(2,1)}, u32[]{:S(2)}) copy-start(bf16[512,128]{1,0:T(8,128)(2,1)} %param.14) | copy-start | bytes 393220
  379.3 12.8 %copy-start.9 = (bf16[512,128]{1,0:T(8,128)(2,1)S(1)}, bf16[512,128]{1,0:T(8,128)(2,1)}, u32[]{:S(2)}) copy-start(bf16[512,128]{1,0:T(8,128)(2,1)} %param.15) | copy-start | bytes 393220
  379.3 36.7 %all-to-all-start.4 = ((f32[2,512,512]{2,0,1:T(2,128)}), f32[2,512,512]{2,0,1:T(2,128)S(1)}, u32[]{:S(2)}, u32[]{:S(2)}) async-start(f32[2,512,512]{2,0,1:T(2,128)} %copy.73), calls=%async_computation.4 | async-start | bytes 4194304 | tf_op jit(solution)/shard_map/all_to_all | solution.py:88
  391.9 63.2 %all-gather.2.cloned.1.call-start = ((), (), s32[]{:S(2)}) async-start(), calls=%async_computation.6 | async-start | bytes 2359296 | tf_op jit(solution)/shard_map/all_gather | solution.py:132
  397.1 60.4 %copy-start.6 = (bf16[512,1,1024]{2,0,1:T(8,128)(2,1)S(1)}, bf16[512,1,1024]{2,0,1:T(8,128)(2,1)}, u32[]{:S(2)}) copy-start(bf16[512,1,1024]{2,0,1:T(8,128)(2,1)} %param.13) | copy-start | bytes 3145732
  416.0 171.6 %all-to-all-start.3 = ((f32[2,512,512]{2,0,1:T(2,128)}), f32[2,512,512]{2,0,1:T(2,128)}, u32[]{:S(2)}, u32[]{:S(2)}) async-start(f32[2,512,512]{2,0,1:T(2,128)} %copy.70), calls=%async_computation.3 | async-start | bytes 4194304 | tf_op jit(solution)/shard_map/all_to_all | solution.py:87
  455.1 114.8 %collective-permute-start = (bf16[2,512,1024]{1,2,0:T(8,128)(2,1)}, bf16[2,512,1024]{1,2,0:T(8,128)(2,1)}, u32[]{:S(2)}, u32[]{:S(2)}) collective-permute-start(bf16[2,512,1024]{1,2,0:T(8,128)(2,1)} %all-gather.2.cloned.1.call-done), channel_id=1, source_target_pairs={{0,8},{8,16},{16,24},{24,32},{32,40},{40,48},{48,56},{56,64},{64,7... | collective-permute-start | bytes 6291464 | tf_op jit(solution)/shard_map/ppermute | solution.py:18
  458.8 112.9 %copy-start.3 = (bf16[2,512,1024]{1,2,0:T(8,128)(2,1)S(1)}, bf16[2,512,1024]{1,2,0:T(8,128)(2,1)}, u32[]{:S(2)}) copy-start(bf16[2,512,1024]{1,2,0:T(8,128)(2,1)} %all-gather.2.cloned.1.call-done) | copy-start | bytes 6291460
  601.8 42.5 %all-to-all-start.5 = ((f32[32,16,512]{2,1,0:T(8,128)}), f32[32,16,512]{2,1,0:T(8,128)S(1)}, u32[]{:S(2)}, u32[]{:S(2)}) async-start(f32[32,16,512]{2,1,0:T(8,128)} %copy.76), calls=%async_computation.5 | async-start | bytes 2097152 | tf_op jit(solution)/shard_map/all_to_all | solution.py:96
  638.8 5.5 copy-start.4
  638.8 5.5 copy-start.5
  638.8 5.5 copy-start.7
  638.8 5.5 copy-start.10
Sparse Core Ops, SparseCore 0:
  395.1 59.9 all-gather.1
where the time goes:
time: 662 us; the launch traced here: 652 us
  waiting for transfers between devices  288 us (44%)
  starting transfers between devices  142 us (21%)
  matrix products  141 us (21%)
  local copies, waits for them, and re-layouts  47.9 us (7%)
  other arithmetic  18.1 us (3%)
  between operations  14.7 us (2%)
    ppermute x1, waiting for transfers between devices, from_behind(): return lax.ppermute(x, axis, pairs)  111 us
    all_to_all x1, starting transfers between devices, long_conv(): lax.all_to_all(turned_im, 'seq', split_axis=0, concat_axis=1, tiled=True)  70.3 us
    all_to_all x1, waiting for transfers between devices, long_conv(): lax.all_to_all(turned_im, 'seq', split_axis=0, concat_axis=1, tiled=True)  54.4 us
    all_to_all x1, waiting for transfers between devices, long_conv(): lax.all_to_all(stacked, 'seq', split_axis=0, concat_axis=0, tiled=True)  43.7 us
    all_to_all x1, waiting for transfers between devices, long_conv(): lax.all_to_all(turned_re, 'seq', split_axis=0, concat_axis=1, tiled=True)  33 us
    dot_general x2, matrix products, line_transform(): cos_re = jnp.einsum('da,cak->cdk', line_cos, real_part, precision=PRECISE)  27 us
    dot_general x2, matrix products, line_transform(): sin_im = jnp.einsum('da,cak->cdk', line_sin, imag_part, precision=PRECISE)  26.7 us
    dot_general x2, matrix products, line_transform(): sin_re = jnp.einsum('da,cak->cdk', line_sin, real_part, precision=PRECISE)  25.9 us
  transfers between devices with their start and end apart: 8, of which 7 were waited for; matrix products, arithmetic and copies ran while one was open for 11% of the time, Pallas kernels for 0%

commit v1 on v0

v1 whole, which is shorter than its diff:
```python
import functools
import math

import jax
import jax.numpy as jnp
import ml_dtypes
import numpy as np
from jax import lax
from jax.experimental import pallas as pl
from jax.experimental.pallas import tpu as pltpu
from jax.sharding import PartitionSpec as P

KVH = 8
HD = 128
TOK = 512
SEQ = 32
CHAN = 8
CH = 512
MINE = CH // SEQ
LINES = 128
COLS = 128
SIZE = 2 * LINES * COLS
BF = jnp.bfloat16
F32 = jnp.float32
MASKED = -1e30

ONES = (((1,), (1,)), ((), ()))
PLAIN = (((1,), (0,)), ((), ()))
FIRST = (((0,), (0,)), ((), ()))


def dot(a, b, dims=PLAIN):
    return lax.dot_general(a, b, dims, preferred_element_type=F32)


def split(x):
    high = x.astype(BF)
    return high, (x - high.astype(F32)).astype(BF)


def np_split(x):
    high = x.astype(ml_dtypes.bfloat16)
    low = (x - high.astype(np.float64)).astype(ml_dtypes.bfloat16)
    return high, low


def tables():
    rows = np.arange(LINES)
    line = 4 * (rows % SEQ) + rows // SEQ
    freq = np.arange(LINES) + 0.5
    angle = 2 * np.pi * np.outer(freq, line) / (2 * LINES)
    first = np.concatenate([np.cos(angle), -np.sin(angle)], axis=0)
    first_hi, first_lo = np_split(first)
    first_both = np.concatenate([first_hi, first_lo], axis=1)
    last_hi, last_lo = np_split(first.T * (2.0 / SIZE))
    turn = 2 * np.pi * np.outer(freq, np.arange(COLS)) / SIZE
    turn_cos, turn_sin = np.cos(turn).astype(np.float32), np.sin(turn).astype(np.float32)
    angle = 2 * np.pi * np.outer(np.arange(COLS), np.arange(COLS)) / COLS
    cos, sin = np.cos(angle), np.sin(angle)
    there = np.block([[cos, -sin], [sin, cos]])
    back = np.block([[cos, sin], [-sin, cos]])
    return (first_both, last_hi, last_lo, turn_cos, turn_sin, *np_split(there), *np_split(back))


def eye(n):
    at = lax.broadcasted_iota(jnp.int32, (n, n), 0) == lax.broadcasted_iota(jnp.int32, (n, n), 1)
    return at.astype(F32).astype(BF)


def turn_kernel(key_ref, value_ref, filter_ref, out_ref):
    unit = eye(256)
    for half in range(2):
        cols = slice(half * 256, half * 256 + 256)
        groups = slice(half * 16, half * 16 + 16)
        signal = (key_ref[:, cols].astype(F32) * value_ref[:, cols].astype(F32)).astype(BF)
        out_ref[groups, 0] = dot(unit, signal, ONES).astype(BF).reshape(16, MINE, TOK)
        out_ref[groups, 1] = dot(unit, filter_ref[:, cols], ONES).astype(BF).reshape(16, MINE, TOK)


def turn_call(key, value, long_filter):
    return pl.pallas_call(
        turn_kernel,
        out_shape=jax.ShapeDtypeStruct((SEQ, 2, MINE, TOK), BF),
        compiler_params=pltpu.CompilerParams(vmem_limit_bytes=32 * 2**20),
        cost_estimate=pl.CostEstimate(flops=2**29, bytes_accessed=5 * 2**19, transcendentals=0),
        name="turn",
    )(key, value, long_filter)


def conv_kernel(
    in_ref,
    first_ref,
    last_hi_ref,
    last_lo_ref,
    cos_ref,
    sin_ref,
    there_hi_ref,
    there_lo_ref,
    back_hi_ref,
    back_lo_ref,
    out_ref,
    wide,
    spec_hi,
    spec_lo,
    result,
):
    for which in range(2):
        for q in range(4):
            part = in_ref[:, which, :, q * 128 : q * 128 + 128].astype(F32)
            wide[which, q * 512 : q * 512 + 512, :] = part.reshape(512, 128)

    def spread(ch, carry):
        both = jnp.concatenate(
            [wide[which, pl.ds(ch, LINES, stride=MINE), :] for which in range(2)], axis=1
        ).astype(BF)
        both = jnp.concatenate([both, both], axis=0)
        lines = dot(first_ref[...], both)
        cos, sin = cos_ref[...], sin_ref[...]
        for which in range(2):
            re = lines[:LINES, which * COLS : which * COLS + COLS]
            im = lines[LINES:, which * COLS : which * COLS + COLS]
            turned = jnp.concatenate([re * cos + im * sin, im * cos - re * sin], axis=1)
            high, low = split(turned)
            rows = pl.ds(pl.multiple_of(ch * LINES, LINES), LINES)
            spec_hi[which, rows, :] = high
            spec_lo[which, rows, :] = low
        return carry

    lax.fori_loop(0, MINE, spread, 0, unroll=2)

    many = 4

    def multiply(step, carry):
        rows = pl.ds(pl.multiple_of(step * (many * LINES), many * LINES), many * LINES)
        spectra = []
        for which in range(2):
            high, low = spec_hi[which, rows, :], spec_lo[which, rows, :]
            spectra.append(
                dot(high, there_hi_ref[...])
                + (dot(low, there_hi_ref[...]) + dot(high, there_lo_ref[...]))
            )
        sig, ker = spectra
        sig_re, sig_im, ker_re, ker_im = sig[:, :COLS], sig[:, COLS:], ker[:, :COLS], ker[:, COLS:]
        product = jnp.concatenate(
            [sig_re * ker_re - sig_im * ker_im, sig_re * ker_im + sig_im * ker_re], axis=1
        )
        high, low = split(product)
        lines = dot(high, back_hi_ref[...]) + (
            dot(low, back_hi_ref[...]) + dot(high, back_lo_ref[...])
        )
        cos, sin = cos_ref[...], sin_ref[...]
        turned = []
        for k in range(many):
            re = lines[k * LINES : k * LINES + LINES, :COLS]
            im = lines[k * LINES : k * LINES + LINES, COLS:]
            turned.append(jnp.concatenate([re * cos - im * sin, im * cos + re * sin], axis=0))
        high, low = split(jnp.concatenate(turned, axis=1))
        values = dot(last_hi_ref[...], high) + (
            dot(last_hi_ref[...], low) + dot(last_lo_ref[...], high)
        )
        for k in range(many):
            result[pl.ds(step * many + k, LINES, stride=MINE), :] = values[
                :, k * COLS : k * COLS + COLS
            ]
        return carry

    lax.fori_loop(0, MINE // many, multiply, 0)
    for q in range(4):
        out_ref[:, :, q * 128 : q * 128 + 128] = (
            result[q * 512 : q * 512 + 512, :].reshape(SEQ, MINE, 128).astype(BF)
        )


def conv_call(received):
    consts = [jnp.asarray(t) for t in tables()]
    return pl.pallas_call(
        conv_kernel,
        out_shape=jax.ShapeDtypeStruct((SEQ, MINE, TOK), BF),
        scratch_shapes=[
            pltpu.VMEM((2, MINE * LINES, 128), F32),
            pltpu.VMEM((2, MINE * LINES, 2 * COLS), BF),
            pltpu.VMEM((2, MINE * LINES, 2 * COLS), BF),
            pltpu.VMEM((MINE * LINES, 128), F32),
        ],
        compiler_params=pltpu.CompilerParams(vmem_limit_bytes=40 * 2**20),
        cost_estimate=pl.CostEstimate(flops=5 * 10**9, bytes_accessed=2 * 2**20, transcendentals=0),
        name="conv",
    )(received, *consts)


def gate_kernel(conv_ref, gate_ref, key_ref, value_ref, skip_ref, out_ref):
    unit = eye(256)
    for half in range(2):
        rows = slice(half * 256, half * 256 + 256)
        conv = dot(unit, conv_ref[:, rows], ONES)
        signal = key_ref[rows, :].astype(F32) * value_ref[rows, :].astype(F32)
        gate = gate_ref[rows, :].astype(F32)
        out_ref[rows, :] = (gate * (conv + skip_ref[...] * signal)).astype(BF)


def gate_call(conv, gate, key, value, skip):
    return pl.pallas_call(
        gate_kernel,
        out_shape=jax.ShapeDtypeStruct((TOK, CH), BF),
        compiler_params=pltpu.CompilerParams(vmem_limit_bytes=32 * 2**20),
        cost_estimate=pl.CostEstimate(flops=2**28, bytes_accessed=5 * 2**19, transcendentals=0),
        name="gate",
    )(conv, gate, key, value, skip)


def pick_kernel(where_ref, query_ref, key_ref, value_ref, query_out, kv_out):
    core = where_ref[2]
    for k in range(4):
        cols = pl.ds(pl.multiple_of((2 * k + 1 - core) * HD, HD), HD)
        query_out[:, k * HD : k * HD + HD] = query_ref[:, cols]
    kv_out[:TOK, :] = key_ref[...]
    kv_out[TOK:, :] = value_ref[...]


def pick_call(where, query, keys, values):
    whole = pl.BlockSpec(memory_space=pltpu.VMEM)
    return pl.pallas_call(
        pick_kernel,
        out_shape=(
            jax.ShapeDtypeStruct((TOK, 4 * HD), BF),
            jax.ShapeDtypeStruct((2 * TOK, HD), BF),
        ),
        in_specs=[pl.BlockSpec(memory_space=pltpu.SMEM), whole, whole, whole],
        out_specs=(whole, whole),
        compiler_params=pltpu.CompilerParams(vmem_limit_bytes=16 * 2**20),
        cost_estimate=pl.CostEstimate(flops=0, bytes_accessed=2 * 2**20, transcendentals=0),
        name="pick",
    )(where, query, keys, values)


def attend_kernel(where_ref, query_ref, other_ref, *refs):
    own, behind = refs[0:4], refs[4:8]
    mine_out, other_out, mine_lse, other_lse = refs[8:]
    seq, line, core = where_ref[0], where_ref[1], where_ref[2]
    scale = HD**-0.5
    to_two = scale * math.log2(math.e)
    unit = eye(256)
    key_at = lax.broadcasted_iota(jnp.int32, (256, 256), 0)
    query_at = lax.broadcasted_iota(jnp.int32, (256, 256), 1)
    later = key_at > query_at
    for k in range(4):
        place = lax.rem(line + 4 - k, 4)
        value_t = jnp.concatenate(
            [behind[k][TOK:, :], own[k][TOK:, :]], axis=0
        ).T
        for member in range(2):
            if member == 0:
                cols = pl.ds(pl.multiple_of((2 * place + core) * HD, HD), HD)
                source, target, lse = query_ref, mine_out, mine_lse
            else:
                cols = pl.ds(pl.multiple_of(place * HD, HD), HD)
                source, target, lse = other_ref, other_out, other_lse
            out_cols = pl.ds(pl.multiple_of(place * HD, HD), HD)
            for half in range(2):
                rows = slice(half * 256, half * 256 + 256)
                query = source[rows, cols]
                back = dot(behind[k][:TOK, :], query, ONES)
                back = jnp.where(seq > 0, back, MASKED)
                tiles = [back]
                if half == 1:
                    tiles.append(dot(own[k][:256, :], query, ONES))
                last = dot(own[k][half * 256 : half * 256 + 256, :], query, ONES)
                tiles.append(jnp.where(later, MASKED, last))
                scores = jnp.concatenate(tiles, axis=0)
                peak = jnp.max(scores, axis=0, keepdims=True)
                expd = jnp.exp2(scores * to_two - peak * to_two)
                total = jnp.sum(expd, axis=0, keepdims=True)
                n_keys = scores.shape[0]
                mixed = dot(value_t[:, :n_keys], expd.astype(BF))
                normed = (mixed / total).astype(BF)
                target[rows, out_cols] = dot(unit, normed, ONES).astype(BF)
                lse[pl.ds(place, 1), rows] = peak * scale + jnp.log(total)


def attend_call(where, query, other, own, behind):
    whole = pl.BlockSpec(memory_space=pltpu.VMEM)
    return pl.pallas_call(
        attend_kernel,
        out_shape=(
            jax.ShapeDtypeStruct((TOK, 4 * HD), BF),
            jax.ShapeDtypeStruct((TOK, 4 * HD), BF),
            jax.ShapeDtypeStruct((4, TOK), F32),
            jax.ShapeDtypeStruct((4, TOK), F32),
        ),
        in_specs=[pl.BlockSpec(memory_space=pltpu.SMEM)] + [whole] * 10,
        out_specs=(whole,) * 4,
        compiler_params=pltpu.CompilerParams(vmem_limit_bytes=40 * 2**20),
        cost_estimate=pl.CostEstimate(
            flops=4 * 10**9, bytes_accessed=5 * 2**20, transcendentals=4 * 2**20
        ),
        name="attend",
    )(where, query, other, *own, *behind)


def merge_kernel(where_ref, mine_ref, got_ref, mine_lse, got_lse, out_ref, lse_ref):
    core = where_ref[2]
    for k in range(4):
        cols = slice(k * HD, k * HD + HD)
        at = pl.ds(pl.multiple_of((2 * k + core) * HD, HD), HD)
        out_ref[:, at] = mine_ref[:, cols]
        lse_ref[pl.ds(2 * k + core, 1), :] = mine_lse[k : k + 1, :]
        at = pl.ds(pl.multiple_of((2 * k + 1 - core) * HD, HD), HD)
        out_ref[:, at] = got_ref[:, cols]
        lse_ref[pl.ds(2 * k + 1 - core, 1), :] = got_lse[k : k + 1, :]


def merge_call(where, mine, got, mine_lse, got_lse):
    whole = pl.BlockSpec(memory_space=pltpu.VMEM)
    return pl.pallas_call(
        merge_kernel,
        out_shape=(
            jax.ShapeDtypeStruct((TOK, KVH * HD), BF),
            jax.ShapeDtypeStruct((KVH, TOK), F32),
        ),
        in_specs=[pl.BlockSpec(memory_space=pltpu.SMEM)] + [whole] * 4,
        out_specs=(whole, whole),
        compiler_params=pltpu.CompilerParams(vmem_limit_bytes=16 * 2**20),
        cost_estimate=pl.CostEstimate(flops=0, bytes_accessed=2 * 2**20, transcendentals=0),
        name="merge",
    )(where, mine, got, mine_lse, got_lse)


def to_line(x, chips):
    return lax.ppermute(x, "chan", [(c, (c + 2 * chips) % CHAN) for c in range(CHAN)])


def to_next(x, chips):
    pairs = [
        (s * CHAN + c, (s + 1) * CHAN + (c + 2 * chips) % CHAN)
        for s in range(SEQ - 1)
        for c in range(CHAN)
    ]
    return lax.ppermute(x, ("seq", "chan"), pairs)


def swap(x):
    return lax.ppermute(x, "chan", [(c, c ^ 1) for c in range(CHAN)])


def exchange(x):
    return lax.all_to_all(x, "seq", split_axis=0, concat_axis=0, tiled=True)


def local(
    hyena_gate, hyena_key, hyena_value, long_filter, skip_weight, attn_query, attn_keys, attn_values
):
    seq, chan = lax.axis_index("seq"), lax.axis_index("chan")
    where = jnp.stack([seq, chan // 2, chan % 2]).astype(jnp.int32)
    query = attn_query.reshape(TOK, KVH * HD)
    query_given, kv = pick_call(where, query, attn_keys, attn_values)
    own = [kv] + [to_line(kv, k) for k in (1, 2, 3)]
    behind = [to_next(kv, k) for k in (0, 1, 2, 3)]
    query_got = swap(query_given)
    turned = turn_call(hyena_key, hyena_value, long_filter)
    received = exchange(turned.reshape(2 * SEQ, MINE, TOK)).reshape(SEQ, 2, MINE, TOK)
    conv = conv_call(received)
    placed = exchange(conv)
    mine, given, mine_lse, given_lse = attend_call(where, query, query_got, own, behind)
    got, got_lse = swap(given), swap(given_lse)
    hyena_out = gate_call(
        placed.reshape(CH, TOK), hyena_gate, hyena_key, hyena_value, skip_weight.reshape(1, CH)
    )
    attn_out, attn_lse = merge_call(where, mine, got, mine_lse, got_lse)
    return (
        hyena_out,
        attn_out.reshape(TOK, 1, KVH * HD),
        attn_lse.reshape(1, KVH, TOK),
    )


def solution(mesh):
    return jax.shard_map(
        local,
        mesh=mesh,
        in_specs=(
            P("seq", "chan"),
            P("seq", "chan"),
            P("seq", "chan"),
            P("seq", "chan"),
            P("chan"),
            P("seq", "chan", None),
            P("seq", "chan"),
            P("seq", "chan"),
        ),
        out_specs=(P("seq", "chan"), P("seq", "chan", None), P("chan", None, "seq")),
        check_vma=False,
    )
```

time: 662 us -> 143 us (0.22)
  the two profiles are of different devices: /device:TPU:224 before, /device:TPU:1 now
where the time goes in v1:
time: 143 us
  starting transfers between devices  95.7 us (67%)
  Pallas kernels  28.6 us (20%)
  local copies, waits for them, and re-layouts  14.1 us (10%)
  waiting for transfers between devices  3.25 us (2%)
    all_to_all x2, starting transfers between devices, exchange(): return lax.all_to_all(x, 'seq', split_axis=0, concat_axis=0, tiled=True)  55.8 us
    ppermute x3, starting transfers between devices, to_line(): lax.ppermute(x, 'chan', [(c, (c + 2 * chips) % CHAN) for c in range(CHAN)])  20.5 us
    ppermute x4, starting transfers between devices, to_next(): return lax.ppermute(x, ('seq', 'chan'), pairs)  17.6 us
    unnamed x46, local copies, waits for them, and re-layouts  14.1 us
    pallas_call x1, Pallas kernels, attend_call(): pl.pallas_call(attend_kernel, out_shape=(jax.ShapeDtypeStruct((TOK, 4 * H...  13.2 us
    pallas_call x1, Pallas kernels, conv_call(): pl.pallas_call(conv_kernel, out_shape=jax.ShapeDtypeStruct((SEQ, MINE, TO...  9.57 us
  transfers between devices with their start and end apart: 12, of which 2 were waited for; matrix products, arithmetic and copies ran while one was open for 0% of the time, Pallas kernels for 18%

profile of v1, /device:TPU:1, one launch (start us, length us, event | category | flops | bytes accessed | tf_op | source)
XLA Modules:
  0.0 142.5 jit_solution(4747059920415432602)
XLA Ops:
  0.6 1.0 copy-done
  1.7 1.0 copy-done.2
  2.7 1.0 copy-done.5
  3.8 1.4 %turn.1 = bf16[32,2,16,512]{3,2,1,0:T(8,128)(2,1)} custom-call(bf16[512,512]{1,0:T(8,128)(2,1)S(1)} %copy-done, bf16[512,512]{1,0:T(8,128)(2,1)S(1)} %copy-done.2, bf16[512,512]{1,0:T(8,128)(2,1)S(1)} %copy-done.5), custom_call_target="tpu_custom_call" | custom-call | flops 536870912 | bytes 2621440 | tf_op jit(solution)/shard_map/turn/pallas_call | solution.py:81
  5.2 14.6 %all-to-all-start = ((bf16[64,16,512]{2,1,0:T(8,128)(2,1)}), bf16[64,16,512]{2,1,0:T(8,128)(2,1)S(1)}, u32[]{:S(2)}, u32[]{:S(2)}) async-start(bf16[64,16,512]{2,1,0:T(8,128)(2,1)} %bitcast), calls=%async_computation | async-start | bytes 2097152 | tf_op jit(solution)/shard_map/all_to_all | solution.py:346
  20.0 1.4 pick.1
  21.4 4.5 %collective-permute-start.7 = (bf16[1024,128]{1,0:T(8,128)(2,1)}, bf16[1024,128]{1,0:T(8,128)(2,1)S(1)}, u32[]{:S(2)}, u32[]{:S(2)}) collective-permute-start(bf16[1024,128]{1,0:T(8,128)(2,1)} %get-tuple-element.12.refs_0_), channel_id=1, source_target_pairs={{0,14},{1,15},{2,8},{3,9},{4,10},{5,11},{6,12},{7,13},{8,22},{9,23... | collective-permute-start | bytes 786440 | tf_op jit(solution)/shard_map/ppermute | solution.py:338
  25.9 3.1 %collective-permute-start.6 = (bf16[1024,128]{1,0:T(8,128)(2,1)}, bf16[1024,128]{1,0:T(8,128)(2,1)S(1)}, u32[]{:S(2)}, u32[]{:S(2)}) collective-permute-start(bf16[1024,128]{1,0:T(8,128)(2,1)} %get-tuple-element.12.refs_0_), channel_id=1, source_target_pairs={{0,12},{1,13},{2,14},{3,15},{4,8},{5,9},{6,10},{7,11},{8,20},{9,21... | collective-permute-start | bytes 786440 | tf_op jit(solution)/shard_map/ppermute | solution.py:338
  29.0 3.3 %collective-permute-start.5 = (bf16[1024,128]{1,0:T(8,128)(2,1)}, bf16[1024,128]{1,0:T(8,128)(2,1)S(1)}, u32[]{:S(2)}, u32[]{:S(2)}) collective-permute-start(bf16[1024,128]{1,0:T(8,128)(2,1)} %get-tuple-element.12.refs_0_), channel_id=1, source_target_pairs={{0,10},{1,11},{2,12},{3,13},{4,14},{5,15},{6,8},{7,9},{8,18},{9,19... | collective-permute-start | bytes 786440 | tf_op jit(solution)/shard_map/ppermute | solution.py:338
  32.2 6.8 %collective-permute-start.4 = (bf16[1024,128]{1,0:T(8,128)(2,1)}, bf16[1024,128]{1,0:T(8,128)(2,1)}, u32[]{:S(2)}, u32[]{:S(2)}) collective-permute-start(bf16[1024,128]{1,0:T(8,128)(2,1)} %get-tuple-element.12.refs_0_), channel_id=1, source_target_pairs={{0,8},{1,9},{2,10},{3,11},{4,12},{5,13},{6,14},{7,15},{8,16},{9,17... | collective-permute-start | bytes 786440 | tf_op jit(solution)/shard_map/ppermute | solution.py:338
  39.0 2.5 %collective-permute-start.3 = (bf16[1024,128]{1,0:T(8,128)(2,1)}, bf16[1024,128]{1,0:T(8,128)(2,1)}, u32[]{:S(2)}, u32[]{:S(2)}) collective-permute-start(bf16[1024,128]{1,0:T(8,128)(2,1)} %get-tuple-element.12.refs_0_), channel_id=1, source_target_pairs={{0,6},{1,7},{2,0},{3,1},{4,2},{5,3},{6,4},{7,5},{8,14},{9,15},{10,... | collective-permute-start | bytes 786440 | tf_op jit(solution)/shard_map/ppermute | solution.py:329
  41.5 9.9 %collective-permute-start.2 = (bf16[1024,128]{1,0:T(8,128)(2,1)}, bf16[1024,128]{1,0:T(8,128)(2,1)}, u32[]{:S(2)}, u32[]{:S(2)}) collective-permute-start(bf16[1024,128]{1,0:T(8,128)(2,1)} %get-tuple-element.12.refs_0_), channel_id=1, source_target_pairs={{0,4},{1,5},{2,6},{3,7},{4,0},{5,1},{6,2},{7,3},{8,12},{9,13},{10,... | collective-permute-start | bytes 786440 | tf_op jit(solution)/shard_map/ppermute | solution.py:329
  51.4 1.8 %collective-permute-done.6.refs_6_ = bf16[1024,128]{1,0:T(8,128)(2,1)S(1)} collective-permute-done((bf16[1024,128]{1,0:T(8,128)(2,1)}, bf16[1024,128]{1,0:T(8,128)(2,1)S(1)}, u32[]{:S(2)}, u32[]{:S(2)}) %collective-permute-start.6) | collective-permute-done | bytes 262176 | tf_op jit(solution)/shard_map/ppermute | solution.py:338
  53.9 8.1 %collective-permute-start.1 = (bf16[1024,128]{1,0:T(8,128)(2,1)}, bf16[1024,128]{1,0:T(8,128)(2,1)}, u32[]{:S(2)}, u32[]{:S(2)}) collective-permute-start(bf16[1024,128]{1,0:T(8,128)(2,1)} %get-tuple-element.12.refs_0_), channel_id=1, source_target_pairs={{0,2},{1,3},{2,4},{3,5},{4,6},{5,7},{6,0},{7,1},{8,10},{9,11},{10,... | collective-permute-start | bytes 786440 | tf_op jit(solution)/shard_map/ppermute | solution.py:329
  62.7 1.2 collective-permute-start
  63.9 0.9 copy-done.15
  70.9 9.6 %conv.1 = bf16[32,16,512]{2,1,0:T(8,128)(2,1)} custom-call(bf16[32,2,16,512]{3,2,1,0:T(8,128)(2,1)S(1)} %bitcast.13, bf16[256,256]{1,0:T(8,128)(2,1)S(1)} %copy-done.18, bf16[128,256]{1,0:T(8,128)(2,1)S(1)} %copy-done.22, bf16[128,256]{1,0:T(8,128)(2,1)S(1)} %copy-done.21, f32[128,128]{1,0:T(8,128)S(1)} %copy-done.20, f32[128,128]{1,0:T(8,128)S(1)} %copy-done.19, ...), custom_call_target="tpu_custom_call" | custom-call | flops 5000000000 | bytes 2097152 | tf_op jit(solution)/shard_map/conv/pallas_call | solution.py:176
  80.5 41.2 %all-to-all-start.1 = ((bf16[32,16,512]{2,1,0:T(8,128)(2,1)}), bf16[32,16,512]{2,1,0:T(8,128)(2,1)S(1)}, u32[]{:S(2)}, u32[]{:S(2)}) async-start(bf16[32,16,512]{2,1,0:T(8,128)(2,1)} %conv.1), calls=%async_computation.1 | async-start | bytes 1048576 | tf_op jit(solution)/shard_map/all_to_all | solution.py:346
  121.7 0.9 copy-done.11
  122.7 0.9 copy-done.13
  123.6 13.2 %attend.1 = (bf16[512,512]{1,0:T(8,128)(2,1)S(1)}, bf16[512,512]{1,0:T(8,128)(2,1)S(1)}, f32[4,512]{1,0:T(4,128)S(1)}, f32[4,512]{1,0:T(4,128)S(1)}) custom-call(s32[3]{0:T(128)S(1)} %pad_add_fusion.where_ref, bf16[512,1024]{1,0:T(8,128)(2,1)S(1)} %bitcast.12, bf16[512,512]{1,0:T(8,128)(2,1)S(1)} %collective-permute-done.other_ref, ...), custom_call_target="tpu_custom_call" | custom-call | flops 4000000000 | bytes 5242880 | tf_op jit(solution)/shard_map/attend/pallas_call | solution.py:282
  137.4 1.4 collective-permute-done.9.got_lse
  138.8 1.8 %merge.1 = (bf16[512,1024]{1,0:T(8,128)(2,1)}, f32[8,512]{1,0:T(8,128)}) custom-call(s32[3]{0:T(128)S(1)} %pad_add_fusion.where_ref, bf16[512,512]{1,0:T(8,128)(2,1)S(1)} %get-tuple-element.13.mine_ref, bf16[512,512]{1,0:T(8,128)(2,1)S(1)} %collective-permute-done.8.got_ref, f32[4,512]{1,0:T(4,128)S(1)} %get-tuple-element.15.mine_lse, ...), custom_call_target="tpu_custom_call" | custom-call | bytes 2097152 | tf_op jit(solution)/shard_map/merge/pallas_call | solution.py:314
  141.3 1.2 gate.1
  (53 shorter events, 8.9 us)
Async XLA Ops:
  0.6 1.0 copy-start
  1.7 1.0 copy-start.2
  2.7 1.0 copy-start.5
  5.2 14.7 %copy-start.4 = (bf16[512,1,1024]{2,0,1:T(8,128)(2,1)S(1)}, bf16[512,1,1024]{2,0,1:T(8,128)(2,1)}, u32[]{:S(2)}) copy-start(bf16[512,1,1024]{2,0,1:T(8,128)(2,1)} %param.22) | copy-start | bytes 3145732
  5.2 14.7 %copy-start.7 = (bf16[512,128]{1,0:T(8,128)(2,1)S(1)}, bf16[512,128]{1,0:T(8,128)(2,1)}, u32[]{:S(2)}) copy-start(bf16[512,128]{1,0:T(8,128)(2,1)} %key_ref.5) | copy-start | bytes 393220
  5.2 14.7 %copy-start.8 = (bf16[512,128]{1,0:T(8,128)(2,1)S(1)}, bf16[512,128]{1,0:T(8,128)(2,1)}, u32[]{:S(2)}) copy-start(bf16[512,128]{1,0:T(8,128)(2,1)} %value_ref.5) | copy-start | bytes 393220
  5.2 58.7 %all-to-all-start = ((bf16[64,16,512]{2,1,0:T(8,128)(2,1)}), bf16[64,16,512]{2,1,0:T(8,128)(2,1)S(1)}, u32[]{:S(2)}, u32[]{:S(2)}) async-start(bf16[64,16,512]{2,1,0:T(8,128)(2,1)} %bitcast), calls=%async_computation | async-start | bytes 2097152 | tf_op jit(solution)/shard_map/all_to_all | solution.py:346
  20.0 44.0 %copy-start.14 = (bf16[256,256]{1,0:T(8,128)(2,1)S(1)}, bf16[256,256]{1,0:T(8,128)(2,1)}, u32[]{:S(2)}) copy-start(bf16[256,256]{1,0:T(8,128)(2,1)} %constant.59.clone.back_lo_ref) | copy-start | bytes 393220
  21.4 20.2 %collective-permute-start.7 = (bf16[1024,128]{1,0:T(8,128)(2,1)}, bf16[1024,128]{1,0:T(8,128)(2,1)S(1)}, u32[]{:S(2)}, u32[]{:S(2)}) collective-permute-start(bf16[1024,128]{1,0:T(8,128)(2,1)} %get-tuple-element.12.refs_0_), channel_id=1, source_target_pairs={{0,14},{1,15},{2,8},{3,9},{4,10},{5,11},{6,12},{7,13},{8,22},{9,23... | collective-permute-start | bytes 786440 | tf_op jit(solution)/shard_map/ppermute | solution.py:338
  25.9 27.3 %collective-permute-start.6 = (bf16[1024,128]{1,0:T(8,128)(2,1)}, bf16[1024,128]{1,0:T(8,128)(2,1)S(1)}, u32[]{:S(2)}, u32[]{:S(2)}) collective-permute-start(bf16[1024,128]{1,0:T(8,128)(2,1)} %get-tuple-element.12.refs_0_), channel_id=1, source_target_pairs={{0,12},{1,13},{2,14},{3,15},{4,8},{5,9},{6,10},{7,11},{8,20},{9,21... | collective-permute-start | bytes 786440 | tf_op jit(solution)/shard_map/ppermute | solution.py:338
  29.0 33.1 %collective-permute-start.5 = (bf16[1024,128]{1,0:T(8,128)(2,1)}, bf16[1024,128]{1,0:T(8,128)(2,1)S(1)}, u32[]{:S(2)}, u32[]{:S(2)}) collective-permute-start(bf16[1024,128]{1,0:T(8,128)(2,1)} %get-tuple-element.12.refs_0_), channel_id=1, source_target_pairs={{0,10},{1,11},{2,12},{3,13},{4,14},{5,15},{6,8},{7,9},{8,18},{9,19... | collective-permute-start | bytes 786440 | tf_op jit(solution)/shard_map/ppermute | solution.py:338
  32.2 89.4 %collective-permute-start.4 = (bf16[1024,128]{1,0:T(8,128)(2,1)}, bf16[1024,128]{1,0:T(8,128)(2,1)}, u32[]{:S(2)}, u32[]{:S(2)}) collective-permute-start(bf16[1024,128]{1,0:T(8,128)(2,1)} %get-tuple-element.12.refs_0_), channel_id=1, source_target_pairs={{0,8},{1,9},{2,10},{3,11},{4,12},{5,13},{6,14},{7,15},{8,16},{9,17... | collective-permute-start | bytes 786440 | tf_op jit(solution)/shard_map/ppermute | solution.py:338
  39.0 82.7 %collective-permute-start.3 = (bf16[1024,128]{1,0:T(8,128)(2,1)}, bf16[1024,128]{1,0:T(8,128)(2,1)}, u32[]{:S(2)}, u32[]{:S(2)}) collective-permute-start(bf16[1024,128]{1,0:T(8,128)(2,1)} %get-tuple-element.12.refs_0_), channel_id=1, source_target_pairs={{0,6},{1,7},{2,0},{3,1},{4,2},{5,3},{6,4},{7,5},{8,14},{9,15},{10,... | collective-permute-start | bytes 786440 | tf_op jit(solution)/shard_map/ppermute | solution.py:329
  41.5 80.1 %collective-permute-start.2 = (bf16[1024,128]{1,0:T(8,128)(2,1)}, bf16[1024,128]{1,0:T(8,128)(2,1)}, u32[]{:S(2)}, u32[]{:S(2)}) collective-permute-start(bf16[1024,128]{1,0:T(8,128)(2,1)} %get-tuple-element.12.refs_0_), channel_id=1, source_target_pairs={{0,4},{1,5},{2,6},{3,7},{4,0},{5,1},{6,2},{7,3},{8,12},{9,13},{10,... | collective-permute-start | bytes 786440 | tf_op jit(solution)/shard_map/ppermute | solution.py:329
  53.9 67.8 %collective-permute-start.1 = (bf16[1024,128]{1,0:T(8,128)(2,1)}, bf16[1024,128]{1,0:T(8,128)(2,1)}, u32[]{:S(2)}, u32[]{:S(2)}) collective-permute-start(bf16[1024,128]{1,0:T(8,128)(2,1)} %get-tuple-element.12.refs_0_), channel_id=1, source_target_pairs={{0,2},{1,3},{2,4},{3,5},{4,6},{5,7},{6,0},{7,1},{8,10},{9,11},{10,... | collective-permute-start | bytes 786440 | tf_op jit(solution)/shard_map/ppermute | solution.py:329
  62.7 59.0 %collective-permute-start = (bf16[512,512]{1,0:T(8,128)(2,1)S(1)}, bf16[512,512]{1,0:T(8,128)(2,1)S(1)}, u32[]{:S(2)}, u32[]{:S(2)}) collective-permute-start(bf16[512,512]{1,0:T(8,128)(2,1)S(1)} %get-tuple-element.11), channel_id=1, source_target_pairs={{0,1},{1,0},{2,3},{3,2},{4,5},{5,4},{6,7},{7,6},{8,9},{9,8},{10,11... | collective-permute-start | bytes 1572872 | tf_op jit(solution)/shard_map/ppermute | solution.py:342
  80.5 60.1 %all-to-all-start.1 = ((bf16[32,16,512]{2,1,0:T(8,128)(2,1)}), bf16[32,16,512]{2,1,0:T(8,128)(2,1)S(1)}, u32[]{:S(2)}, u32[]{:S(2)}) async-start(bf16[32,16,512]{2,1,0:T(8,128)(2,1)} %conv.1), calls=%async_computation.1 | async-start | bytes 1048576 | tf_op jit(solution)/shard_map/all_to_all | solution.py:346
  121.7 1.0 copy-start.11
  122.7 0.9 copy-start.13
  123.6 17.0 %copy-start.6 = (bf16[512,512]{1,0:T(8,128)(2,1)S(1)}, bf16[512,512]{1,0:T(8,128)(2,1)}, u32[]{:S(2)}) copy-start(bf16[512,512]{1,0:T(8,128)(2,1)} %gate_ref.1) | copy-start | bytes 1572868
  136.8 2.0 %collective-permute-start.8 = (bf16[512,512]{1,0:T(8,128)(2,1)S(1)}, bf16[512,512]{1,0:T(8,128)(2,1)S(1)}, u32[]{:S(2)}, u32[]{:S(2)}) collective-permute-start(bf16[512,512]{1,0:T(8,128)(2,1)S(1)} %get-tuple-element.14), channel_id=1, source_target_pairs={{0,1},{1,0},{2,3},{3,2},{4,5},{5,4},{6,7},{7,6},{8,9},{9,8},{10,11... | collective-permute-start | bytes 1572872 | tf_op jit(solution)/shard_map/ppermute | solution.py:342
  137.2 1.6 %collective-permute-start.9 = (f32[4,512]{1,0:T(4,128)S(1)}, f32[4,512]{1,0:T(4,128)S(1)}, u32[]{:S(2)}, u32[]{:S(2)}) collective-permute-start(f32[4,512]{1,0:T(4,128)S(1)} %get-tuple-element.16), channel_id=1, source_target_pairs={{0,1},{1,0},{2,3},{3,2},{4,5},{5,4},{6,7},{7,6},{8,9},{9,8},{10,11... | collective-permute-start | bytes 24584 | tf_op jit(solution)/shard_map/ppermute | solution.py:342
  138.8 1.9 %copy-start.1 = (bf16[512,512]{1,0:T(8,128)(2,1)S(1)}, bf16[512,512]{1,0:T(8,128)(2,1)}, u32[]{:S(2)}) copy-start(bf16[512,512]{1,0:T(8,128)(2,1)} %key_ref.4) | copy-start | bytes 1572868
  138.8 1.9 %copy-start.3 = (bf16[512,512]{1,0:T(8,128)(2,1)S(1)}, bf16[512,512]{1,0:T(8,128)(2,1)}, u32[]{:S(2)}) copy-start(bf16[512,512]{1,0:T(8,128)(2,1)} %value_ref.4) | copy-start | bytes 1572868
  (11 other events, 9.1 us)

commit v2 on v1

v2 whole, which is shorter than its diff:
```python
import functools
import math

import jax
import jax.numpy as jnp
import ml_dtypes
import numpy as np
from jax import lax
from jax.experimental import pallas as pl
from jax.experimental.pallas import tpu as pltpu
from jax.sharding import PartitionSpec as P

KVH = 8
HD = 128
TOK = 512
SEQ = 32
CHAN = 8
CH = 512
MINE = CH // SEQ
LINES = 128
COLS = 128
SIZE = 2 * LINES * COLS
BF = jnp.bfloat16
F32 = jnp.float32
MASKED = -1e30
ROOM = 58 * 2**20

ONES = (((1,), (1,)), ((), ()))
PLAIN = (((1,), (0,)), ((), ()))
FIRST = (((0,), (0,)), ((), ()))


def dot(a, b, dims=PLAIN):
    return lax.dot_general(a, b, dims, preferred_element_type=F32)


def split(x):
    high = x.astype(BF)
    return high, (x - high.astype(F32)).astype(BF)


def np_split(x):
    high = x.astype(ml_dtypes.bfloat16)
    low = (x - high.astype(np.float64)).astype(ml_dtypes.bfloat16)
    return high, low


def tables():
    rows = np.arange(LINES)
    line = 4 * (rows % SEQ) + rows // SEQ
    freq = np.arange(LINES) + 0.5
    angle = 2 * np.pi * np.outer(freq, line) / (2 * LINES)
    first = np.concatenate([np.cos(angle), -np.sin(angle)], axis=0)
    first_hi, first_lo = np_split(first)
    first_both = np.concatenate([first_hi, first_lo], axis=1)
    last_hi, last_lo = np_split(first.T * (2.0 / SIZE))
    turn = 2 * np.pi * np.outer(freq, np.arange(COLS)) / SIZE
    turn_cos, turn_sin = np.cos(turn).astype(np.float32), np.sin(turn).astype(np.float32)
    angle = 2 * np.pi * np.outer(np.arange(COLS), np.arange(COLS)) / COLS
    cos, sin = np.cos(angle), np.sin(angle)
    there = np.block([[cos, -sin], [sin, cos]])
    back = np.block([[cos, sin], [-sin, cos]])
    there_hi, there_lo = np_split(there)
    back_hi, back_lo = np_split(back)
    return (
        first_both,
        np.concatenate([last_hi, last_hi, last_lo], axis=1),
        turn_cos,
        turn_sin,
        np.concatenate([there_hi, there_hi, there_lo], axis=0),
        np.concatenate([back_hi, back_hi, back_lo], axis=0),
    )


def eye(n):
    at = lax.broadcasted_iota(jnp.int32, (n, n), 0) == lax.broadcasted_iota(jnp.int32, (n, n), 1)
    return at.astype(F32).astype(BF)


def turn_kernel(key_ref, value_ref, filter_ref, after_ref, out_ref):
    unit = eye(256)
    for half in range(2):
        cols = slice(half * 256, half * 256 + 256)
        groups = slice(half * 16, half * 16 + 16)
        signal = (key_ref[:, cols].astype(F32) * value_ref[:, cols].astype(F32)).astype(BF)
        out_ref[groups, 0] = dot(unit, signal, ONES).astype(BF).reshape(16, MINE, TOK)
        out_ref[groups, 1] = dot(unit, filter_ref[:, cols], ONES).astype(BF).reshape(16, MINE, TOK)


def turn_call(key, value, long_filter, after):
    whole = pl.BlockSpec(memory_space=pltpu.VMEM)
    return pl.pallas_call(
        turn_kernel,
        in_specs=[whole, whole, whole, pl.BlockSpec(memory_space=pl.ANY)],
        out_shape=jax.ShapeDtypeStruct((SEQ, 2, MINE, TOK), BF),
        compiler_params=pltpu.CompilerParams(vmem_limit_bytes=ROOM),
        cost_estimate=pl.CostEstimate(flops=2**29, bytes_accessed=5 * 2**19, transcendentals=0),
        name="turn",
    )(key, value, long_filter, after)


def conv_kernel(
    in_ref,
    first_ref,
    last_ref,
    cos_ref,
    sin_ref,
    there_ref,
    back_ref,
    out_ref,
    wide,
    spec,
    result,
):
    for which in range(2):
        for q in range(4):
            part = in_ref[:, which, :, q * 128 : q * 128 + 128].astype(F32)
            wide[which, q * 512 : q * 512 + 512, :] = part.reshape(512, 128)

    def spread(ch, carry):
        both = jnp.concatenate(
            [wide[which, pl.ds(ch, LINES, stride=MINE), :] for which in range(2)], axis=1
        ).astype(BF)
        both = jnp.concatenate([both, both], axis=0)
        lines = dot(first_ref[...], both)
        cos, sin = cos_ref[...], sin_ref[...]
        for which in range(2):
            re = lines[:LINES, which * COLS : which * COLS + COLS]
            im = lines[LINES:, which * COLS : which * COLS + COLS]
            turned = jnp.concatenate([re * cos + im * sin, im * cos - re * sin], axis=1)
            high, low = split(turned)
            rows = pl.ds(pl.multiple_of(ch * LINES, LINES), LINES)
            spec[which, rows, : 2 * COLS] = high
            spec[which, rows, 2 * COLS :] = low
        return carry

    lax.fori_loop(0, MINE, spread, 0, unroll=8)

    many = MINE

    def multiply(step, carry):
        rows = pl.ds(pl.multiple_of(step * (many * LINES), many * LINES), many * LINES)
        spectra = []
        for which in range(2):
            both = spec[which, rows, :]
            high = both[:, : 2 * COLS]
            spectra.append(dot(jnp.concatenate([both, high], axis=1), there_ref[...]))
        sig, ker = spectra
        sig_re, sig_im, ker_re, ker_im = sig[:, :COLS], sig[:, COLS:], ker[:, :COLS], ker[:, COLS:]
        product = jnp.concatenate(
            [sig_re * ker_re - sig_im * ker_im, sig_re * ker_im + sig_im * ker_re], axis=1
        )
        high, low = split(product)
        lines = dot(jnp.concatenate([high, low, high], axis=1), back_ref[...])
        cos, sin = cos_ref[...], sin_ref[...]
        turned = []
        for k in range(many):
            re = lines[k * LINES : k * LINES + LINES, :COLS]
            im = lines[k * LINES : k * LINES + LINES, COLS:]
            turned.append(jnp.concatenate([re * cos - im * sin, im * cos + re * sin], axis=0))
        high, low = split(jnp.concatenate(turned, axis=1))
        values = dot(last_ref[...], jnp.concatenate([high, low, high], axis=0))
        for k in range(many):
            result[pl.ds(step * many + k, LINES, stride=MINE), :] = values[
                :, k * COLS : k * COLS + COLS
            ]
        return carry

    lax.fori_loop(0, MINE // many, multiply, 0)
    for q in range(4):
        out_ref[:, :, q * 128 : q * 128 + 128] = (
            result[q * 512 : q * 512 + 512, :].reshape(SEQ, MINE, 128).astype(BF)
        )


def conv_call(received):
    consts = [jnp.asarray(t) for t in tables()]
    return pl.pallas_call(
        conv_kernel,
        out_shape=jax.ShapeDtypeStruct((SEQ, MINE, TOK), BF),
        scratch_shapes=[
            pltpu.VMEM((2, MINE * LINES, 128), F32),
            pltpu.VMEM((2, MINE * LINES, 4 * COLS), BF),
            pltpu.VMEM((MINE * LINES, 128), F32),
        ],
        compiler_params=pltpu.CompilerParams(vmem_limit_bytes=58 * 2**20),
        cost_estimate=pl.CostEstimate(flops=5 * 10**9, bytes_accessed=2 * 2**20, transcendentals=0),
        name="conv",
    )(received, *consts)


def gate_kernel(conv_ref, gate_ref, key_ref, value_ref, skip_ref, out_ref):
    unit = eye(256)
    for half in range(2):
        rows = slice(half * 256, half * 256 + 256)
        conv = dot(unit, conv_ref[:, rows], ONES)
        signal = key_ref[rows, :].astype(F32) * value_ref[rows, :].astype(F32)
        gate = gate_ref[rows, :].astype(F32)
        out_ref[rows, :] = (gate * (conv + skip_ref[...] * signal)).astype(BF)


def gate_call(conv, gate, key, value, skip):
    return pl.pallas_call(
        gate_kernel,
        out_shape=jax.ShapeDtypeStruct((TOK, CH), BF),
        compiler_params=pltpu.CompilerParams(vmem_limit_bytes=14 * 2**20),
        cost_estimate=pl.CostEstimate(flops=2**28, bytes_accessed=5 * 2**19, transcendentals=0),
        name="gate",
    )(conv, gate, key, value, skip)


def pack_kernel(key_ref, value_ref, out_ref):
    out_ref[:TOK, :] = key_ref[...]
    out_ref[TOK:, :] = value_ref[...]


def pack_call(keys, values):
    return pl.pallas_call(
        pack_kernel,
        out_shape=jax.ShapeDtypeStruct((2 * TOK, HD), BF),
        compiler_params=pltpu.CompilerParams(vmem_limit_bytes=ROOM),
        cost_estimate=pl.CostEstimate(flops=0, bytes_accessed=2**19, transcendentals=0),
        name="pack",
    )(keys, values)


SCALE = HD**-0.5
TO_TWO = SCALE * math.log2(math.e)
TILE = 256
HALVES = TOK // TILE


def pipelined(jobs, first, second):
    ahead = first(jobs[0])
    for i, job in enumerate(jobs):
        now = ahead
        if i + 1 < len(jobs):
            ahead = first(jobs[i + 1])
        second(job, now)


def tile_rows(h):
    return slice(h * TILE, h * TILE + TILE)


def own_kernel(where_ref, query_ref, other_ref, *refs):
    pieces = refs[0:4]
    mine_acc, other_acc, peak_ref, total_ref, keys = refs[4:]
    line, core = where_ref[1], where_ref[2]
    for k in range(4):
        keys[lax.rem(line + 4 - k, 4), :, :HD] = pieces[k][...]
        keys[k, TOK:, HD:] = jnp.ones((TOK, HD), BF)
    at_query = lax.broadcasted_iota(jnp.int32, (TILE, TILE), 0)
    at_key = lax.broadcasted_iota(jnp.int32, (TILE, TILE), 1)
    later = at_key > at_query
    lane = lax.broadcasted_iota(jnp.int32, (TILE, HD), 1)
    peaks = [jnp.zeros((TILE, HD), F32) for _ in range(HALVES)]
    totals = [jnp.zeros((TILE, HD), F32) for _ in range(HALVES)]

    def score(job):
        place, member, h = job
        cols = pl.ds(pl.multiple_of((2 * place + core) * HD, HD), HD)
        query = (query_ref, other_ref)[member][tile_rows(h), cols]
        here = dot(query, keys[place, : (h + 1) * TILE, :HD], ONES)
        last = jnp.where(later, MASKED, here[:, h * TILE :])
        return jnp.concatenate([here[:, : h * TILE], last], axis=1) if h else last

    def finish(job, scores):
        place, member, h = job
        peak = jnp.max(scores, axis=1, keepdims=True)
        weights = jnp.exp2(scores * TO_TWO - peak * TO_TWO).astype(BF)
        mixed = dot(weights, keys[place, TOK : TOK + (h + 1) * TILE, :])
        (mine_acc, other_acc)[member][place, tile_rows(h), :] = mixed[:, :HD]
        at = lane == member * 4 + place
        peaks[h] = jnp.where(at, peak, peaks[h])
        totals[h] = jnp.where(at, mixed[:, HD:], totals[h])

    jobs = [(p, m, h) for p in range(4) for m in range(2) for h in range(HALVES)]
    pipelined(jobs, score, finish)
    for h in range(HALVES):
        peak_ref[tile_rows(h), :] = peaks[h]
        total_ref[tile_rows(h), :] = totals[h]


def own_call(where, query, other, pieces):
    whole = pl.BlockSpec(memory_space=pltpu.VMEM)
    acc = jax.ShapeDtypeStruct((4, TOK, HD), F32)
    stat = jax.ShapeDtypeStruct((TOK, HD), F32)
    return pl.pallas_call(
        own_kernel,
        out_shape=(acc, acc, stat, stat),
        in_specs=[pl.BlockSpec(memory_space=pltpu.SMEM)] + [whole] * 6,
        out_specs=(whole,) * 4,
        scratch_shapes=[pltpu.VMEM((4, 2 * TOK, 2 * HD), BF)],
        compiler_params=pltpu.CompilerParams(vmem_limit_bytes=14 * 2**20),
        cost_estimate=pl.CostEstimate(
            flops=4 * 10**10, bytes_accessed=4 * 2**20, transcendentals=2 * 2**20
        ),
        name="own",
    )(where, query, other, *pieces)


def back_kernel(member, where_ref, query_ref, *refs):
    pieces = refs[0:4]
    acc_ref, peak_ref, total_ref, out_ref, lse_ref, keys = refs[4:]
    seq, line, core = where_ref[0], where_ref[1], where_ref[2]
    crossed = lax.rem(seq, 4) == 0
    for k in range(4):
        place = lax.rem(line + 4 - k, 4)
        keys[jnp.where(crossed, 3 - place, place), :, :HD] = pieces[k][...]
        keys[k, TOK:, HD:] = jnp.ones((TOK, HD), BF)
    lane = lax.broadcasted_iota(jnp.int32, (TILE, HD), 1)
    lses = [jnp.zeros((TILE, HD), F32) for _ in range(HALVES)]

    def score(job):
        place, h = job
        cols = pl.ds(pl.multiple_of((2 * place + core) * HD, HD), HD)
        scores = dot(query_ref[tile_rows(h), cols], keys[place, :TOK, :HD], ONES)
        return jnp.where(seq > 0, scores, MASKED)

    def finish(job, scores):
        place, h = job
        column = member * 4 + place
        own_peak = peak_ref[tile_rows(h), column : column + 1]
        own_total = total_ref[tile_rows(h), column : column + 1]
        peak = jnp.maximum(jnp.max(scores, axis=1, keepdims=True), own_peak)
        weights = jnp.exp2(scores * TO_TWO - peak * TO_TWO).astype(BF)
        mixed = dot(weights, keys[place, TOK:, :])
        keep = jnp.exp2((own_peak - peak) * TO_TWO)
        total = mixed[:, HD:] + keep * own_total
        out = (mixed[:, :HD] + keep * acc_ref[place, tile_rows(h), :]) / total
        out_ref[tile_rows(h), place * HD : place * HD + HD] = out.astype(BF)
        lses[h] = jnp.where(lane == place, peak * SCALE + jnp.log(total), lses[h])

    pipelined([(p, h) for p in range(4) for h in range(HALVES)], score, finish)
    for h in range(HALVES):
        lse_ref[:, tile_rows(h)] = lses[h].T[:4]


def back_call(member, where, query, pieces, acc, peak, total):
    whole = pl.BlockSpec(memory_space=pltpu.VMEM)

    def kernel(*refs):
        back_kernel(member, *refs)

    return pl.pallas_call(
        kernel,
        out_shape=(
            jax.ShapeDtypeStruct((TOK, 4 * HD), BF),
            jax.ShapeDtypeStruct((4, TOK), F32),
        ),
        in_specs=[pl.BlockSpec(memory_space=pltpu.SMEM)] + [whole] * 8,
        out_specs=(whole,) * 2,
        scratch_shapes=[pltpu.VMEM((4, 2 * TOK, 2 * HD), BF)],
        compiler_params=pltpu.CompilerParams(vmem_limit_bytes=14 * 2**20),
        cost_estimate=pl.CostEstimate(
            flops=10**11, bytes_accessed=4 * 2**20, transcendentals=2 * 2**20
        ),
        name="back",
    )(where, query, *pieces, acc, peak, total)


def merge_kernel(where_ref, mine_ref, got_ref, mine_lse, got_lse, out_ref, lse_ref):
    core = where_ref[2]
    for k in range(4):
        cols = slice(k * HD, k * HD + HD)
        at = pl.ds(pl.multiple_of((2 * k + core) * HD, HD), HD)
        out_ref[:, at] = mine_ref[:, cols]
        lse_ref[pl.ds(2 * k + core, 1), :] = mine_lse[k : k + 1, :]
        at = pl.ds(pl.multiple_of((2 * k + 1 - core) * HD, HD), HD)
        out_ref[:, at] = got_ref[:, cols]
        lse_ref[pl.ds(2 * k + 1 - core, 1), :] = got_lse[k : k + 1, :]


def merge_call(where, mine, got, mine_lse, got_lse):
    whole = pl.BlockSpec(memory_space=pltpu.VMEM)
    return pl.pallas_call(
        merge_kernel,
        out_shape=(
            jax.ShapeDtypeStruct((TOK, KVH * HD), BF),
            jax.ShapeDtypeStruct((KVH, TOK), F32),
        ),
        in_specs=[pl.BlockSpec(memory_space=pltpu.SMEM)] + [whole] * 4,
        out_specs=(whole, whole),
        compiler_params=pltpu.CompilerParams(vmem_limit_bytes=14 * 2**20),
        cost_estimate=pl.CostEstimate(flops=0, bytes_accessed=2 * 2**20, transcendentals=0),
        name="merge",
    )(where, mine, got, mine_lse, got_lse)


def to_line(x, chips):
    return lax.ppermute(x, "chan", [(c, (c + 2 * chips) % CHAN) for c in range(CHAN)])


def to_next(x):
    pairs = [
        (s * CHAN + c, (s + 1) * CHAN + (c if s % 4 != 3 else 2 * (3 - c // 2) + c % 2))
        for s in range(SEQ - 1)
        for c in range(CHAN)
    ]
    return lax.ppermute(x, ("seq", "chan"), pairs)


def swap(x):
    return lax.ppermute(x, "chan", [(c, c ^ 1) for c in range(CHAN)])


def exchange(x):
    return lax.all_to_all(x, "seq", split_axis=0, concat_axis=0, tiled=True)


def local(
    hyena_gate, hyena_key, hyena_value, long_filter, skip_weight, attn_query, attn_keys, attn_values
):
    seq, chan = lax.axis_index("seq"), lax.axis_index("chan")
    where = jnp.stack([seq, chan // 2, chan % 2]).astype(jnp.int32)
    query = attn_query.reshape(TOK, KVH * HD)
    kv = pack_call(attn_keys, attn_values)
    query_got = swap(query)
    kv_behind = to_next(kv)
    own = [kv] + [to_line(kv, k) for k in (1, 2, 3)]
    turned = turn_call(hyena_key, hyena_value, long_filter, kv)
    received = exchange(turned.reshape(2 * SEQ, MINE, TOK)).reshape(SEQ, 2, MINE, TOK)
    mine_acc, given_acc, peak, total = own_call(where, query, query_got, own)
    received, kv_behind, peak = lax.optimization_barrier((received, kv_behind, peak))
    behind = [kv_behind] + [to_line(kv_behind, k) for k in (1, 2, 3)]
    conv = conv_call(received)
    placed = exchange(conv)
    given, given_lse = back_call(1, where, query_got, behind, given_acc, peak, total)
    got, got_lse = swap(given), swap(given_lse)
    mine, mine_lse = back_call(0, where, query, behind, mine_acc, peak, total)
    hyena_out = gate_call(
        placed.reshape(CH, TOK), hyena_gate, hyena_key, hyena_value, skip_weight.reshape(1, CH)
    )
    attn_out, attn_lse = merge_call(where, mine, got, mine_lse, got_lse)
    return (
        hyena_out,
        attn_out.reshape(TOK, 1, KVH * HD),
        attn_lse.reshape(1, KVH, TOK),
    )


def solution(mesh):
    return jax.shard_map(
        local,
        mesh=mesh,
        in_specs=(
            P("seq", "chan"),
            P("seq", "chan"),
            P("seq", "chan"),
            P("seq", "chan"),
            P("chan"),
            P("seq", "chan", None),
            P("seq", "chan"),
            P("seq", "chan"),
        ),
        out_specs=(P("seq", "chan"), P("seq", "chan", None), P("chan", None, "seq")),
        check_vma=False,
    )
```

time: 143 us -> 110 us (0.77)
  the two profiles are of different devices: /device:TPU:1 before, /device:TPU:9 now
where the time goes in v2:
time: 110 us
  starting transfers between devices  56.2 us (51%)
  Pallas kernels  27.7 us (25%)
  waiting for transfers between devices  18.9 us (17%)
  local copies, waits for them, and re-layouts  6.21 us (6%)
    ppermute x6, starting transfers between devices, to_line(): lax.ppermute(x, 'chan', [(c, (c + 2 * chips) % CHAN) for c in range(CHAN)])  22.1 us
    all_to_all x2, starting transfers between devices, exchange(): return lax.all_to_all(x, 'seq', split_axis=0, concat_axis=0, tiled=True)  21.2 us
    ppermute x6, waiting for transfers between devices, to_line(): lax.ppermute(x, 'chan', [(c, (c + 2 * chips) % CHAN) for c in range(CHAN)])  18.9 us
    ppermute x3, starting transfers between devices, swap(): return lax.ppermute(x, 'chan', [(c, c ^ 1) for c in range(CHAN)])  9.74 us
    pallas_call x1, Pallas kernels, conv_call(): pl.pallas_call(conv_kernel, out_shape=jax.ShapeDtypeStruct((SEQ, MINE, TO...  8.61 us
    pallas_call x2, Pallas kernels, back_call(): pl.pallas_call(kernel, out_shape=(jax.ShapeDtypeStruct((TOK, 4 * HD), BF)...  7.43 us
    unnamed x30, local copies, waits for them, and re-layouts  6.21 us
    ppermute x1, starting transfers between devices, to_next(): return lax.ppermute(x, ('seq', 'chan'), pairs)  3.19 us
  transfers between devices with their start and end apart: 12, of which 2 were waited for; matrix products, arithmetic and copies ran while one was open for 0% of the time, Pallas kernels for 23%

profile of v2, /device:TPU:9, one launch (start us, length us, event | category | flops | bytes accessed | tf_op | source)
XLA Modules:
  0.0 109.9 jit_solution(6903073259675471604)
XLA Ops:
  0.6 0.8 collective-permute-start.1
  1.4 1.7 %pack.1.after_ref.refs_0_ = bf16[1024,128]{1,0:T(8,128)(2,1)} custom-call(bf16[512,128]{1,0:T(8,128)(2,1)} %key_ref.3, bf16[512,128]{1,0:T(8,128)(2,1)} %value_ref.3), custom_call_target="tpu_custom_call" | custom-call | bytes 524288 | tf_op jit(solution)/shard_map/pack/pallas_call | solution.py:218
  3.1 4.3 %collective-permute-start.4 = (bf16[1024,128]{1,0:T(8,128)(2,1)}, bf16[1024,128]{1,0:T(8,128)(2,1)S(1)}, u32[]{:S(2)}, u32[]{:S(2)}) collective-permute-start(bf16[1024,128]{1,0:T(8,128)(2,1)} %pack.1.after_ref.refs_0_), channel_id=1, source_target_pairs={{0,6},{1,7},{2,0},{3,1},{4,2},{5,3},{6,4},{7,5},{8,14},{9,15},{10,... | collective-permute-start | bytes 786440 | tf_op jit(solution)/shard_map/ppermute | solution.py:392
  7.7 3.2 %collective-permute-start = (bf16[1024,128]{1,0:T(8,128)(2,1)}, bf16[1024,128]{1,0:T(8,128)(2,1)S(1)}, u32[]{:S(2)}, u32[]{:S(2)}) collective-permute-start(bf16[1024,128]{1,0:T(8,128)(2,1)} %pack.1.after_ref.refs_0_), channel_id=1, source_target_pairs={{0,8},{1,9},{2,10},{3,11},{4,12},{5,13},{6,14},{7,15},{8,16},{9,17... | collective-permute-start | bytes 786440 | tf_op jit(solution)/shard_map/ppermute | solution.py:401
  10.9 2.8 %turn.1 = bf16[32,2,16,512]{3,2,1,0:T(8,128)(2,1)} custom-call(bf16[512,512]{1,0:T(8,128)(2,1)} %key_ref.5, bf16[512,512]{1,0:T(8,128)(2,1)} %value_ref.5, bf16[512,512]{1,0:T(8,128)(2,1)} %filter_ref.1, bf16[1024,128]{1,0:T(8,128)(2,1)} %pack.1.after_ref.refs_0_), custom_call_target="tpu_custom_call" | custom-call | flops 536870912 | bytes 2621440 | tf_op jit(solution)/shard_map/turn/pallas_call | solution.py:92
  13.7 11.5 %all-to-all-start = ((bf16[64,16,512]{2,1,0:T(8,128)(2,1)}), bf16[64,16,512]{2,1,0:T(8,128)(2,1)}, u32[]{:S(2)}, u32[]{:S(2)}) async-start(bf16[64,16,512]{2,1,0:T(8,128)(2,1)} %bitcast.14), calls=%async_computation | async-start | bytes 2097152 | tf_op jit(solution)/shard_map/all_to_all | solution.py:409
  25.3 15.9 %collective-permute-done.3.refs_2_ = bf16[1024,128]{1,0:T(8,128)(2,1)S(1)} collective-permute-done((bf16[1024,128]{1,0:T(8,128)(2,1)}, bf16[1024,128]{1,0:T(8,128)(2,1)S(1)}, u32[]{:S(2)}, u32[]{:S(2)}) %collective-permute-start.3) | collective-permute-done | bytes 262176 | tf_op jit(solution)/shard_map/ppermute | solution.py:392
  41.2 3.1 %own.1 = (f32[4,512,128]{2,1,0:T(8,128)S(1)}, f32[4,512,128]{2,1,0:T(8,128)S(1)}, f32[512,128]{1,0:T(8,128)S(1)}, f32[512,128]{1,0:T(8,128)S(1)}) custom-call(s32[3]{0:T(128)S(1)} %pad_add_fusion.where_ref.refs_0_, bf16[512,1024]{1,0:T(8,128)(2,1)S(1)} %bitcast.12, bf16[512,1024]{1,0:T(8,128)(2,1)S(1)} %collective-permute-done.1.other_ref.refs_1_, ...), custom_call_target="tpu_custom_call" | custom-call | flops 40000000000 | bytes 4194304 | tf_op jit(solution)/shard_map/own/pallas_call | solution.py:289
  44.4 1.0 copy-done.6
  45.3 1.0 copy-done.8
  47.0 0.7 copy-done.13
  47.7 2.6 %collective-permute-start.7 = (bf16[1024,128]{1,0:T(8,128)(2,1)S(1)}, bf16[1024,128]{1,0:T(8,128)(2,1)S(1)}, u32[]{:S(2)}, u32[]{:S(2)}) collective-permute-start(bf16[1024,128]{1,0:T(8,128)(2,1)S(1)} %collective-permute-done.refs_2_), channel_id=1, source_target_pairs={{0,6},{1,7},{2,0},{3,1},{4,2},{5,3},{6,4},{7,5},{8,14},{9,15},{10,... | collective-permute-start | bytes 786440 | tf_op jit(solution)/shard_map/ppermute | solution.py:392
  50.3 13.4 %collective-permute-start.6 = (bf16[1024,128]{1,0:T(8,128)(2,1)S(1)}, bf16[1024,128]{1,0:T(8,128)(2,1)S(1)}, u32[]{:S(2)}, u32[]{:S(2)}) collective-permute-start(bf16[1024,128]{1,0:T(8,128)(2,1)S(1)} %collective-permute-done.refs_2_), channel_id=1, source_target_pairs={{0,4},{1,5},{2,6},{3,7},{4,0},{5,1},{6,2},{7,3},{8,12},{9,13},{10,... | collective-permute-start | bytes 786440 | tf_op jit(solution)/shard_map/ppermute | solution.py:392
  63.7 1.5 %collective-permute-start.5 = (bf16[1024,128]{1,0:T(8,128)(2,1)S(1)}, bf16[1024,128]{1,0:T(8,128)(2,1)S(1)}, u32[]{:S(2)}, u32[]{:S(2)}) collective-permute-start(bf16[1024,128]{1,0:T(8,128)(2,1)S(1)} %collective-permute-done.refs_2_), channel_id=1, source_target_pairs={{0,2},{1,3},{2,4},{3,5},{4,6},{5,7},{6,0},{7,1},{8,10},{9,11},{10,... | collective-permute-start | bytes 786440 | tf_op jit(solution)/shard_map/ppermute | solution.py:392
  65.2 8.6 %conv.1 = bf16[32,16,512]{2,1,0:T(8,128)(2,1)} custom-call(bf16[32,2,16,512]{3,2,1,0:T(8,128)(2,1)} %bitcast.1.in_ref, bf16[256,256]{1,0:T(8,128)(2,1)} %constant.45.clone.first_ref, bf16[128,768]{1,0:T(8,128)(2,1)} %constant.46.clone.last_ref, f32[128,128]{1,0:T(8,128)} %constant.47.clone.cos_ref, f32[128,128]{1,0:T(8,128)} %constant.48.clone.sin_ref, ...), custom_call_target="tpu_custom_call" | custom-call | flops 5000000000 | bytes 2097152 | tf_op jit(solution)/shard_map/conv/pallas_call | solution.py:178
  73.8 9.7 %all-to-all-start.1 = ((bf16[32,16,512]{2,1,0:T(8,128)(2,1)}), bf16[32,16,512]{2,1,0:T(8,128)(2,1)}, u32[]{:S(2)}, u32[]{:S(2)}) async-start(bf16[32,16,512]{2,1,0:T(8,128)(2,1)} %conv.1), calls=%async_computation.1 | async-start | bytes 1048576 | tf_op jit(solution)/shard_map/all_to_all | solution.py:409
  83.5 3.0 %collective-permute-done.6.refs_4_ = bf16[1024,128]{1,0:T(8,128)(2,1)S(1)} collective-permute-done((bf16[1024,128]{1,0:T(8,128)(2,1)S(1)}, bf16[1024,128]{1,0:T(8,128)(2,1)S(1)}, u32[]{:S(2)}, u32[]{:S(2)}) %collective-permute-start.6) | collective-permute-done | bytes 262176 | tf_op jit(solution)/shard_map/ppermute | solution.py:392
  86.5 1.2 %copy-done.9 = f32[4,512,128]{2,1,0:T(8,128)S(1)} copy-done((f32[4,512,128]{2,1,0:T(8,128)S(1)}, f32[4,512,128]{2,1,0:T(8,128)}, u32[]{:S(2)}) %copy-start.9) | copy-done | bytes 1048600
  87.7 0.9 copy-done.14
  88.7 3.7 %back.3 = (bf16[512,512]{1,0:T(8,128)(2,1)S(1)}, f32[4,512]{1,0:T(4,128)S(1)}) custom-call(s32[3]{0:T(128)S(1)} %pad_add_fusion.where_ref.refs_0_, bf16[512,1024]{1,0:T(8,128)(2,1)S(1)} %collective-permute-done.1.other_ref.refs_1_, bf16[1024,128]{1,0:T(8,128)(2,1)S(1)} %collective-permute-done.refs_2_, bf16[1024,128]{1,0:T(8,128)(2,1)S(1)} %collective-permute-done.5.refs_3_, ...), custom_call_target="tpu_custom_call" | custom-call | flops 99999997952 | bytes 4194304 | tf_op jit(solution)/shard_map/back/pallas_call | solution.py:346
  92.4 8.7 %collective-permute-start.9 = (f32[4,512]{1,0:T(4,128)S(1)}, f32[4,512]{1,0:T(4,128)S(1)}, u32[]{:S(2)}, u32[]{:S(2)}) collective-permute-start(f32[4,512]{1,0:T(4,128)S(1)} %get-tuple-element.26), channel_id=1, source_target_pairs={{0,1},{1,0},{2,3},{3,2},{4,5},{5,4},{6,7},{7,6},{8,9},{9,8},{10,11... | collective-permute-start | bytes 24584 | tf_op jit(solution)/shard_map/ppermute | solution.py:405
  101.3 3.7 %back.2 = (bf16[512,512]{1,0:T(8,128)(2,1)S(1)}, f32[4,512]{1,0:T(4,128)S(1)}) custom-call(s32[3]{0:T(128)S(1)} %pad_add_fusion.where_ref.refs_0_, bf16[512,1024]{1,0:T(8,128)(2,1)S(1)} %bitcast.13, bf16[1024,128]{1,0:T(8,128)(2,1)S(1)} %collective-permute-done.refs_2_, bf16[1024,128]{1,0:T(8,128)(2,1)S(1)} %collective-permute-done.5.refs_3_, ...), custom_call_target="tpu_custom_call" | custom-call | flops 99999997952 | bytes 4194304 | tf_op jit(solution)/shard_map/back/pallas_call | solution.py:346
  105.1 1.8 %merge.1 = (bf16[512,1024]{1,0:T(8,128)(2,1)}, f32[8,512]{1,0:T(8,128)}) custom-call(s32[3]{0:T(128)S(1)} %pad_add_fusion.where_ref.refs_0_, bf16[512,512]{1,0:T(8,128)(2,1)S(1)} %get-tuple-element.22.mine_ref, bf16[512,512]{1,0:T(8,128)(2,1)S(1)} %collective-permute-done.8.got_ref, f32[4,512]{1,0:T(4,128)S(1)} %get-tuple-element.25.mine_lse, ...), custom_call_target="tpu_custom_call" | custom-call | bytes 2097152 | tf_op jit(solution)/shard_map/merge/pallas_call | solution.py:377
  107.6 2.2 %gate.1 = bf16[512,512]{1,0:T(8,128)(2,1)} custom-call(bf16[512,512]{1,0:T(8,128)(2,1)} %bitcast.6.conv_ref, bf16[512,512]{1,0:T(8,128)(2,1)S(1)} %copy-done.3, bf16[512,512]{1,0:T(8,128)(2,1)S(1)} %copy-done, bf16[512,512]{1,0:T(8,128)(2,1)S(1)} %copy-done.1, f32[1,512]{1,0:T(1,128)S(1)} %bitcast.10), custom_call_target="tpu_custom_call" | custom-call | flops 268435456 | bytes 2621440 | tf_op jit(solution)/shard_map/gate/pallas_call | solution.py:203
  (39 shorter events, 2.1 us)
Async XLA Ops:
  0.6 40.6 %collective-permute-start.1 = (bf16[512,1024]{1,0:T(8,128)(2,1)}, bf16[512,1024]{1,0:T(8,128)(2,1)S(1)}, u32[]{:S(2)}, u32[]{:S(2)}) collective-permute-start(bf16[512,1024]{1,0:T(8,128)(2,1)} %bitcast.11), channel_id=1, source_target_pairs={{0,1},{1,0},{2,3},{3,2},{4,5},{5,4},{6,7},{7,6},{8,9},{9,8},{10,11... | collective-permute-start | bytes 3145736 | tf_op jit(solution)/shard_map/ppermute | solution.py:405
  3.1 22.3 %collective-permute-start.4 = (bf16[1024,128]{1,0:T(8,128)(2,1)}, bf16[1024,128]{1,0:T(8,128)(2,1)S(1)}, u32[]{:S(2)}, u32[]{:S(2)}) collective-permute-start(bf16[1024,128]{1,0:T(8,128)(2,1)} %pack.1.after_ref.refs_0_), channel_id=1, source_target_pairs={{0,6},{1,7},{2,0},{3,1},{4,2},{5,3},{6,4},{7,5},{8,14},{9,15},{10,... | collective-permute-start | bytes 786440 | tf_op jit(solution)/shard_map/ppermute | solution.py:392
  7.4 33.8 %collective-permute-start.3 = (bf16[1024,128]{1,0:T(8,128)(2,1)}, bf16[1024,128]{1,0:T(8,128)(2,1)S(1)}, u32[]{:S(2)}, u32[]{:S(2)}) collective-permute-start(bf16[1024,128]{1,0:T(8,128)(2,1)} %pack.1.after_ref.refs_0_), channel_id=1, source_target_pairs={{0,4},{1,5},{2,6},{3,7},{4,0},{5,1},{6,2},{7,3},{8,12},{9,13},{10,... | collective-permute-start | bytes 786440 | tf_op jit(solution)/shard_map/ppermute | solution.py:392
  7.4 33.8 %collective-permute-start.2 = (bf16[1024,128]{1,0:T(8,128)(2,1)}, bf16[1024,128]{1,0:T(8,128)(2,1)S(1)}, u32[]{:S(2)}, u32[]{:S(2)}) collective-permute-start(bf16[1024,128]{1,0:T(8,128)(2,1)} %pack.1.after_ref.refs_0_), channel_id=1, source_target_pairs={{0,2},{1,3},{2,4},{3,5},{4,6},{5,7},{6,0},{7,1},{8,10},{9,11},{10,... | collective-permute-start | bytes 786440 | tf_op jit(solution)/shard_map/ppermute | solution.py:392
  7.7 40.0 %collective-permute-start = (bf16[1024,128]{1,0:T(8,128)(2,1)}, bf16[1024,128]{1,0:T(8,128)(2,1)S(1)}, u32[]{:S(2)}, u32[]{:S(2)}) collective-permute-start(bf16[1024,128]{1,0:T(8,128)(2,1)} %pack.1.after_ref.refs_0_), channel_id=1, source_target_pairs={{0,8},{1,9},{2,10},{3,11},{4,12},{5,13},{6,14},{7,15},{8,16},{9,17... | collective-permute-start | bytes 786440 | tf_op jit(solution)/shard_map/ppermute | solution.py:401
  13.7 27.5 %copy-start.2 = (bf16[1024,128]{1,0:T(8,128)(2,1)S(1)}, bf16[1024,128]{1,0:T(8,128)(2,1)}, u32[]{:S(2)}) copy-start(bf16[1024,128]{1,0:T(8,128)(2,1)} %pack.1.after_ref.refs_0_) | copy-start | bytes 786436
  13.7 27.5 %copy-start.5 = (bf16[512,1,1024]{2,0,1:T(8,128)(2,1)S(1)}, bf16[512,1,1024]{2,0,1:T(8,128)(2,1)}, u32[]{:S(2)}) copy-start(bf16[512,1,1024]{2,0,1:T(8,128)(2,1)} %param.19) | copy-start | bytes 3145732
  13.7 34.0 %all-to-all-start = ((bf16[64,16,512]{2,1,0:T(8,128)(2,1)}), bf16[64,16,512]{2,1,0:T(8,128)(2,1)}, u32[]{:S(2)}, u32[]{:S(2)}) async-start(bf16[64,16,512]{2,1,0:T(8,128)(2,1)} %bitcast.14), calls=%async_computation | async-start | bytes 2097152 | tf_op jit(solution)/shard_map/all_to_all | solution.py:409
  44.4 1.0 copy-start.6
  45.3 1.0 copy-start.8
  47.7 35.7 %collective-permute-start.7 = (bf16[1024,128]{1,0:T(8,128)(2,1)S(1)}, bf16[1024,128]{1,0:T(8,128)(2,1)S(1)}, u32[]{:S(2)}, u32[]{:S(2)}) collective-permute-start(bf16[1024,128]{1,0:T(8,128)(2,1)S(1)} %collective-permute-done.refs_2_), channel_id=1, source_target_pairs={{0,6},{1,7},{2,0},{3,1},{4,2},{5,3},{6,4},{7,5},{8,14},{9,15},{10,... | collective-permute-start | bytes 786440 | tf_op jit(solution)/shard_map/ppermute | solution.py:392
  50.3 36.2 %collective-permute-start.6 = (bf16[1024,128]{1,0:T(8,128)(2,1)S(1)}, bf16[1024,128]{1,0:T(8,128)(2,1)S(1)}, u32[]{:S(2)}, u32[]{:S(2)}) collective-permute-start(bf16[1024,128]{1,0:T(8,128)(2,1)S(1)} %collective-permute-done.refs_2_), channel_id=1, source_target_pairs={{0,4},{1,5},{2,6},{3,7},{4,0},{5,1},{6,2},{7,3},{8,12},{9,13},{10,... | collective-permute-start | bytes 786440 | tf_op jit(solution)/shard_map/ppermute | solution.py:392
  63.7 22.8 %collective-permute-start.5 = (bf16[1024,128]{1,0:T(8,128)(2,1)S(1)}, bf16[1024,128]{1,0:T(8,128)(2,1)S(1)}, u32[]{:S(2)}, u32[]{:S(2)}) collective-permute-start(bf16[1024,128]{1,0:T(8,128)(2,1)S(1)} %collective-permute-done.refs_2_), channel_id=1, source_target_pairs={{0,2},{1,3},{2,4},{3,5},{4,6},{5,7},{6,0},{7,1},{8,10},{9,11},{10,... | collective-permute-start | bytes 786440 | tf_op jit(solution)/shard_map/ppermute | solution.py:392
  73.8 12.7 %copy-start.11 = (f32[512,128]{1,0:T(8,128)S(1)}, f32[512,128]{1,0:T(8,128)}, u32[]{:S(2)}) copy-start(f32[512,128]{1,0:T(8,128)} %copy-done.10) | copy-start | bytes 786436
  73.8 33.2 %all-to-all-start.1 = ((bf16[32,16,512]{2,1,0:T(8,128)(2,1)}), bf16[32,16,512]{2,1,0:T(8,128)(2,1)}, u32[]{:S(2)}, u32[]{:S(2)}) async-start(bf16[32,16,512]{2,1,0:T(8,128)(2,1)} %conv.1), calls=%async_computation.1 | async-start | bytes 1048576 | tf_op jit(solution)/shard_map/all_to_all | solution.py:409
  86.5 1.2 %copy-start.9 = (f32[4,512,128]{2,1,0:T(8,128)S(1)}, f32[4,512,128]{2,1,0:T(8,128)}, u32[]{:S(2)}) copy-start(f32[4,512,128]{2,1,0:T(8,128)} %copy-done.8) | copy-start | bytes 3145732
  87.7 0.9 copy-start.14
  88.6 12.7 %copy-start.7 = (f32[4,512,128]{2,1,0:T(8,128)S(1)}, f32[4,512,128]{2,1,0:T(8,128)}, u32[]{:S(2)}) copy-start(f32[4,512,128]{2,1,0:T(8,128)} %copy-done.6) | copy-start | bytes 3145732
  88.7 12.7 %copy-start.12 = (f32[512,128]{1,0:T(8,128)S(1)}, f32[512,128]{1,0:T(8,128)}, u32[]{:S(2)}) copy-start(f32[512,128]{1,0:T(8,128)} %copy-done.10) | copy-start | bytes 786436
  92.4 12.7 %collective-permute-start.9 = (f32[4,512]{1,0:T(4,128)S(1)}, f32[4,512]{1,0:T(4,128)S(1)}, u32[]{:S(2)}, u32[]{:S(2)}) collective-permute-start(f32[4,512]{1,0:T(4,128)S(1)} %get-tuple-element.26), channel_id=1, source_target_pairs={{0,1},{1,0},{2,3},{3,2},{4,5},{5,4},{6,7},{7,6},{8,9},{9,8},{10,11... | collective-permute-start | bytes 24584 | tf_op jit(solution)/shard_map/ppermute | solution.py:405
  101.0 4.1 %collective-permute-start.8 = (bf16[512,512]{1,0:T(8,128)(2,1)S(1)}, bf16[512,512]{1,0:T(8,128)(2,1)S(1)}, u32[]{:S(2)}, u32[]{:S(2)}) collective-permute-start(bf16[512,512]{1,0:T(8,128)(2,1)S(1)} %get-tuple-element.24), channel_id=1, source_target_pairs={{0,1},{1,0},{2,3},{3,2},{4,5},{5,4},{6,7},{7,6},{8,9},{9,8},{10,11... | collective-permute-start | bytes 1572872 | tf_op jit(solution)/shard_map/ppermute | solution.py:405
  101.3 5.6 %copy-start.3 = (bf16[512,512]{1,0:T(8,128)(2,1)S(1)}, bf16[512,512]{1,0:T(8,128)(2,1)}, u32[]{:S(2)}) copy-start(bf16[512,512]{1,0:T(8,128)(2,1)} %gate_ref.1) | copy-start | bytes 1572868
  105.1 1.9 %copy-start = (bf16[512,512]{1,0:T(8,128)(2,1)S(1)}, bf16[512,512]{1,0:T(8,128)(2,1)}, u32[]{:S(2)}) copy-start(bf16[512,512]{1,0:T(8,128)(2,1)} %key_ref.5) | copy-start | bytes 1572868
  105.1 1.9 %copy-start.1 = (bf16[512,512]{1,0:T(8,128)(2,1)S(1)}, bf16[512,512]{1,0:T(8,128)(2,1)}, u32[]{:S(2)}) copy-start(bf16[512,512]{1,0:T(8,128)(2,1)} %value_ref.5) | copy-start | bytes 1572868
  (3 other events, 2.1 us)

commit v3 on v2

--- a/solution.py
+++ b/solution.py
@@ -62,14 +62,9 @@
     back = np.block([[cos, sin], [-sin, cos]])
     there_hi, there_lo = np_split(there)
     back_hi, back_lo = np_split(back)
-    return (
-        first_both,
-        np.concatenate([last_hi, last_hi, last_lo], axis=1),
-        turn_cos,
-        turn_sin,
-        np.concatenate([there_hi, there_hi, there_lo], axis=0),
-        np.concatenate([back_hi, back_hi, back_lo], axis=0),
-    )
+    factors = [first_both, there_hi, there_hi, there_lo, back_hi, back_hi, back_lo]
+    factors += [last_hi, last_hi, last_lo]
+    return np.concatenate(factors, axis=0), np.concatenate([turn_cos, turn_sin], axis=1)
 
 
 def eye(n):
@@ -101,17 +96,17 @@
 
 def conv_kernel(
     in_ref,
-    first_ref,
-    last_ref,
-    cos_ref,
-    sin_ref,
-    there_ref,
-    back_ref,
+    factor_ref,
+    turn_ref,
     out_ref,
     wide,
     spec,
     result,
 ):
+    def factor(start, size):
+        return factor_ref[start : start + size, :]
+
+    cos, sin = turn_ref[:, :COLS], turn_ref[:, COLS:]
     for which in range(2):
         for q in range(4):
             part = in_ref[:, which, :, q * 128 : q * 128 + 128].astype(F32)
@@ -122,8 +117,7 @@
             [wide[which, pl.ds(ch, LINES, stride=MINE), :] for which in range(2)], axis=1
         ).astype(BF)
         both = jnp.concatenate([both, both], axis=0)
-        lines = dot(first_ref[...], both)
-        cos, sin = cos_ref[...], sin_ref[...]
+        lines = dot(factor(0, 256), both)
         for which in range(2):
             re = lines[:LINES, which * COLS : which * COLS + COLS]
             im = lines[LINES:, which * COLS : which * COLS + COLS]
@@ -144,22 +138,22 @@
         for which in range(2):
             both = spec[which, rows, :]
             high = both[:, : 2 * COLS]
-            spectra.append(dot(jnp.concatenate([both, high], axis=1), there_ref[...]))
+            spectra.append(dot(jnp.concatenate([both, high], axis=1), factor(256, 768)))
         sig, ker = spectra
         sig_re, sig_im, ker_re, ker_im = sig[:, :COLS], sig[:, COLS:], ker[:, :COLS], ker[:, COLS:]
         product = jnp.concatenate(
             [sig_re * ker_re - sig_im * ker_im, sig_re * ker_im + sig_im * ker_re], axis=1
         )
         high, low = split(product)
-        lines = dot(jnp.concatenate([high, low, high], axis=1), back_ref[...])
-        cos, sin = cos_ref[...], sin_ref[...]
+        lines = dot(jnp.concatenate([high, low, high], axis=1), factor(1024, 768))
         turned = []
         for k in range(many):
             re = lines[k * LINES : k * LINES + LINES, :COLS]
             im = lines[k * LINES : k * LINES + LINES, COLS:]
             turned.append(jnp.concatenate([re * cos - im * sin, im * cos + re * sin], axis=0))
         high, low = split(jnp.concatenate(turned, axis=1))
-        values = dot(last_ref[...], jnp.concatenate([high, low, high], axis=0))
+        last = jnp.concatenate([factor(1792 + LINES * i, LINES) for i in range(3)], axis=1)
+        values = dot(last, jnp.concatenate([high, low, high], axis=0))
         for k in range(many):
             result[pl.ds(step * many + k, LINES, stride=MINE), :] = values[
                 :, k * COLS : k * COLS + COLS
@@ -243,13 +237,21 @@
     return slice(h * TILE, h * TILE + TILE)
 
 
+def lay_out(keys, pieces, line):
+    kept, below, above, across, far = pieces
+    keys[line, :, :HD] = kept[...]
+    keys[lax.rem(line + 2, 4), :, :HD] = across[...]
+    keys[lax.rem(line + 3, 4), :, :HD] = jnp.where(line > 0, below[...], far[...])
+    keys[lax.rem(line + 1, 4), :, :HD] = jnp.where(line < 3, above[...], far[...])
+    for k in range(4):
+        keys[k, TOK:, HD:] = jnp.ones((TOK, HD), BF)
+
+
 def own_kernel(where_ref, query_ref, other_ref, *refs):
-    pieces = refs[0:4]
-    mine_acc, other_acc, peak_ref, total_ref, keys = refs[4:]
+    pieces = refs[0:5]
+    mine_acc, other_acc, peak_ref, total_ref, keys = refs[5:]
     line, core = where_ref[1], where_ref[2]
-    for k in range(4):
-        keys[lax.rem(line + 4 - k, 4), :, :HD] = pieces[k][...]
-        keys[k, TOK:, HD:] = jnp.ones((TOK, HD), BF)
+    lay_out(keys, pieces, line)
     at_query = lax.broadcasted_iota(jnp.int32, (TILE, TILE), 0)
     at_key = lax.broadcasted_iota(jnp.int32, (TILE, TILE), 1)
     later = at_key > at_query
@@ -289,7 +291,7 @@
     return pl.pallas_call(
         own_kernel,
         out_shape=(acc, acc, stat, stat),
-        in_specs=[pl.BlockSpec(memory_space=pltpu.SMEM)] + [whole] * 6,
+        in_specs=[pl.BlockSpec(memory_space=pltpu.SMEM)] + [whole] * 7,
         out_specs=(whole,) * 4,
         scratch_shapes=[pltpu.VMEM((4, 2 * TOK, 2 * HD), BF)],
         compiler_params=pltpu.CompilerParams(vmem_limit_bytes=14 * 2**20),
@@ -388,8 +390,24 @@
     )(where, mine, got, mine_lse, got_lse)
 
 
-def to_line(x, chips):
-    return lax.ppermute(x, "chan", [(c, (c + 2 * chips) % CHAN) for c in range(CHAN)])
+def one_line(x, moves):
+    pairs = [(2 * i + core, 2 * j + core) for i, j in moves for core in range(2)]
+    return lax.ppermute(x, "chan", pairs)
+
+
+def gather_near(x):
+    below = one_line(x, [(0, 1), (1, 2), (2, 3)])
+    above = one_line(x, [(1, 0), (2, 1), (3, 2)])
+    across = one_line(x, [(0, 2), (1, 3), (2, 0), (3, 1)])
+    return [x, below, above, across]
+
+
+def around(x, chips):
+    return one_line(x, [(i, (i + chips) % 4) for i in range(4)])
+
+
+def gather_far(across):
+    return one_line(across, [(2, 3), (1, 0)])
 
 
 def to_next(x):
@@ -418,12 +436,15 @@
     kv = pack_call(attn_keys, attn_values)
     query_got = swap(query)
     kv_behind = to_next(kv)
-    own = [kv] + [to_line(kv, k) for k in (1, 2, 3)]
+    own = gather_near(kv)
     turned = turn_call(hyena_key, hyena_value, long_filter, kv)
+    across, _, kv_behind = lax.optimization_barrier((own[3], turned, kv_behind))
+    own.append(gather_far(across))
     received = exchange(turned.reshape(2 * SEQ, MINE, TOK)).reshape(SEQ, 2, MINE, TOK)
     mine_acc, given_acc, peak, total = own_call(where, query, query_got, own)
-    received, kv_behind, peak = lax.optimization_barrier((received, kv_behind, peak))
-    behind = [kv_behind] + [to_line(kv_behind, k) for k in (1, 2, 3)]
+    kv_behind, peak = lax.optimization_barrier((kv_behind, peak))
+    behind = [kv_behind] + [around(kv_behind, k) for k in (1, 2, 3)]
+    received, peak = lax.optimization_barrier((received, peak))
     conv = conv_call(received)
     placed = exchange(conv)
     given, given_lse = back_call(1, where, query_got, behind, given_acc, peak, total)

time: 110 us -> 105 us (0.955)
  the two profiles are of different devices: /device:TPU:9 before, /device:TPU:1 now
where the time goes in v3:
time: 105 us; the launch traced here: 104 us
  starting transfers between devices  41.3 us (39%)
  waiting for transfers between devices  28.4 us (27%)
  Pallas kernels  28.2 us (27%)
  local copies, waits for them, and re-layouts  5.54 us (5%)
    ppermute x7, waiting for transfers between devices, one_line(): return lax.ppermute(x, 'chan', pairs)  21.4 us
    all_to_all x2, starting transfers between devices, exchange(): return lax.all_to_all(x, 'seq', split_axis=0, concat_axis=0, tiled=True)  17.7 us
    ppermute x7, starting transfers between devices, one_line(): return lax.ppermute(x, 'chan', pairs)  14.5 us
    pallas_call x1, Pallas kernels, conv_call(): pl.pallas_call(conv_kernel, out_shape=jax.ShapeDtypeStruct((SEQ, MINE, TO...  8.6 us
    ppermute x3, starting transfers between devices, swap(): return lax.ppermute(x, 'chan', [(c, c ^ 1) for c in range(CHAN)])  7.65 us
    pallas_call x2, Pallas kernels, back_call(): pl.pallas_call(kernel, out_shape=(jax.ShapeDtypeStruct((TOK, 4 * HD), BF)...  7.43 us
    all_to_all x2, waiting for transfers between devices, exchange(): return lax.all_to_all(x, 'seq', split_axis=0, concat_axis=0, tiled=True)  6.99 us
    unnamed x30, local copies, waits for them, and re-layouts  5.54 us
  transfers between devices with their start and end apart: 13, of which 3 were waited for; matrix products, arithmetic and copies ran while one was open for 0% of the time, Pallas kernels for 25%

profile of v3, /device:TPU:1, one launch (start us, length us, event | category | flops | bytes accessed | tf_op | source)
XLA Modules:
  0.0 104.4 jit_solution(4034116729880475479)
XLA Ops:
  0.6 3.3 %collective-permute-start.2 = (bf16[512,1024]{1,0:T(8,128)(2,1)}, bf16[512,1024]{1,0:T(8,128)(2,1)S(1)}, u32[]{:S(2)}, u32[]{:S(2)}) collective-permute-start(bf16[512,1024]{1,0:T(8,128)(2,1)} %bitcast.11), channel_id=1, source_target_pairs={{0,1},{1,0},{2,3},{3,2},{4,5},{5,4},{6,7},{7,6},{8,9},{9,8},{10,11... | collective-permute-start | bytes 3145736 | tf_op jit(solution)/shard_map/ppermute | solution.py:423
  4.0 1.7 %pack.1.after_ref.refs_0_ = bf16[1024,128]{1,0:T(8,128)(2,1)} custom-call(bf16[512,128]{1,0:T(8,128)(2,1)} %key_ref.3, bf16[512,128]{1,0:T(8,128)(2,1)} %value_ref.3), custom_call_target="tpu_custom_call" | custom-call | bytes 524288 | tf_op jit(solution)/shard_map/pack/pallas_call | solution.py:212
  5.6 1.5 %collective-permute-start.1 = (bf16[1024,128]{1,0:T(8,128)(2,1)}, bf16[1024,128]{1,0:T(8,128)(2,1)S(1)}, u32[]{:S(2)}, u32[]{:S(2)}) collective-permute-start(bf16[1024,128]{1,0:T(8,128)(2,1)} %pack.1.after_ref.refs_0_), channel_id=1, source_target_pairs={{0,8},{1,9},{2,10},{3,11},{4,12},{5,13},{6,14},{7,15},{8,16},{9,17... | collective-permute-start | bytes 786440 | tf_op jit(solution)/shard_map/ppermute | solution.py:419
  7.1 3.1 %collective-permute-start = (bf16[1024,128]{1,0:T(8,128)(2,1)}, bf16[1024,128]{1,0:T(8,128)(2,1)S(1)}, u32[]{:S(2)}, u32[]{:S(2)}) collective-permute-start(bf16[1024,128]{1,0:T(8,128)(2,1)} %pack.1.after_ref.refs_0_), channel_id=1, source_target_pairs={{0,4},{1,5},{2,6},{3,7},{4,0},{5,1},{6,2},{7,3},{8,12},{9,13},{10,... | collective-permute-start | bytes 786440 | tf_op jit(solution)/shard_map/ppermute | solution.py:395
  10.2 1.3 %collective-permute-start.4 = (bf16[1024,128]{1,0:T(8,128)(2,1)}, bf16[1024,128]{1,0:T(8,128)(2,1)S(1)}, u32[]{:S(2)}, u32[]{:S(2)}) collective-permute-start(bf16[1024,128]{1,0:T(8,128)(2,1)} %pack.1.after_ref.refs_0_), channel_id=1, source_target_pairs={{2,0},{3,1},{4,2},{5,3},{6,4},{7,5},{10,8},{11,9},{12,10},{13,11},... | collective-permute-start | bytes 786440 | tf_op jit(solution)/shard_map/ppermute | solution.py:395
  11.5 4.2 %collective-permute-start.3 = (bf16[1024,128]{1,0:T(8,128)(2,1)}, bf16[1024,128]{1,0:T(8,128)(2,1)S(1)}, u32[]{:S(2)}, u32[]{:S(2)}) collective-permute-start(bf16[1024,128]{1,0:T(8,128)(2,1)} %pack.1.after_ref.refs_0_), channel_id=1, source_target_pairs={{0,2},{1,3},{2,4},{3,5},{4,6},{5,7},{8,10},{9,11},{10,12},{11,13},... | collective-permute-start | bytes 786440 | tf_op jit(solution)/shard_map/ppermute | solution.py:395
  15.7 2.8 %turn.1 = bf16[32,2,16,512]{3,2,1,0:T(8,128)(2,1)} custom-call(bf16[512,512]{1,0:T(8,128)(2,1)} %key_ref.5, bf16[512,512]{1,0:T(8,128)(2,1)} %value_ref.5, bf16[512,512]{1,0:T(8,128)(2,1)} %filter_ref.1, bf16[1024,128]{1,0:T(8,128)(2,1)} %pack.1.after_ref.refs_0_), custom_call_target="tpu_custom_call" | custom-call | flops 536870912 | bytes 2621440 | tf_op jit(solution)/shard_map/turn/pallas_call | solution.py:87
  18.5 4.0 %collective-permute-done.refs_3_ = bf16[1024,128]{1,0:T(8,128)(2,1)S(1)} collective-permute-done((bf16[1024,128]{1,0:T(8,128)(2,1)}, bf16[1024,128]{1,0:T(8,128)(2,1)S(1)}, u32[]{:S(2)}, u32[]{:S(2)}) %collective-permute-start) | collective-permute-done | bytes 262176 | tf_op jit(solution)/shard_map/ppermute | solution.py:395
  22.5 1.3 %collective-permute-start.5 = (bf16[1024,128]{1,0:T(8,128)(2,1)S(1)}, bf16[1024,128]{1,0:T(8,128)(2,1)}, u32[]{:S(2)}, u32[]{:S(2)}) collective-permute-start(bf16[1024,128]{1,0:T(8,128)(2,1)S(1)} %collective-permute-done.refs_3_), channel_id=1, source_target_pairs={{4,6},{5,7},{2,0},{3,1},{12,14},{13,15},{10,8},{11,9},{20,22},{21,... | collective-permute-start | bytes 786440 | tf_op jit(solution)/shard_map/ppermute | solution.py:395
  23.8 12.8 %all-to-all-start = ((bf16[64,16,512]{2,1,0:T(8,128)(2,1)}), bf16[64,16,512]{2,1,0:T(8,128)(2,1)}, u32[]{:S(2)}, u32[]{:S(2)}) async-start(bf16[64,16,512]{2,1,0:T(8,128)(2,1)} %bitcast.14), calls=%async_computation | async-start | bytes 2097152 | tf_op jit(solution)/shard_map/all_to_all | solution.py:427
  36.7 3.6 %own.1 = (f32[4,512,128]{2,1,0:T(8,128)S(1)}, f32[4,512,128]{2,1,0:T(8,128)S(1)}, f32[512,128]{1,0:T(8,128)S(1)}, f32[512,128]{1,0:T(8,128)S(1)}) custom-call(s32[3]{0:T(128)S(1)} %pad_add_fusion.where_ref.refs_0_, bf16[512,1024]{1,0:T(8,128)(2,1)S(1)} %bitcast.12, bf16[512,1024]{1,0:T(8,128)(2,1)S(1)} %collective-permute-done.2.other_ref.refs_1_, ...), custom_call_target="tpu_custom_call" | custom-call | flops 40000000000 | bytes 4194304 | tf_op jit(solution)/shard_map/own/pallas_call | solution.py:291
  41.3 1.0 copy-done.8
  43.7 1.7 %collective-permute-start.8 = (bf16[1024,128]{1,0:T(8,128)(2,1)S(1)}, bf16[1024,128]{1,0:T(8,128)(2,1)S(1)}, u32[]{:S(2)}, u32[]{:S(2)}) collective-permute-start(bf16[1024,128]{1,0:T(8,128)(2,1)S(1)} %collective-permute-done.1.refs_2_), channel_id=1, source_target_pairs={{0,6},{1,7},{2,0},{3,1},{4,2},{5,3},{6,4},{7,5},{8,14},{9,15},{10,... | collective-permute-start | bytes 786440 | tf_op jit(solution)/shard_map/ppermute | solution.py:395
  45.4 2.3 %collective-permute-start.7 = (bf16[1024,128]{1,0:T(8,128)(2,1)S(1)}, bf16[1024,128]{1,0:T(8,128)(2,1)S(1)}, u32[]{:S(2)}, u32[]{:S(2)}) collective-permute-start(bf16[1024,128]{1,0:T(8,128)(2,1)S(1)} %collective-permute-done.1.refs_2_), channel_id=1, source_target_pairs={{0,4},{1,5},{2,6},{3,7},{4,0},{5,1},{6,2},{7,3},{8,12},{9,13},{10,... | collective-permute-start | bytes 786440 | tf_op jit(solution)/shard_map/ppermute | solution.py:395
  48.4 7.0 %all-to-all-done = bf16[64,16,512]{2,1,0:T(8,128)(2,1)} async-done(((bf16[64,16,512]{2,1,0:T(8,128)(2,1)}), bf16[64,16,512]{2,1,0:T(8,128)(2,1)}, u32[]{:S(2)}, u32[]{:S(2)}) %all-to-all-start) | async-done | bytes 1048608 | tf_op jit(solution)/shard_map/all_to_all | solution.py:427
  55.4 8.6 %conv.1 = bf16[32,16,512]{2,1,0:T(8,128)(2,1)} custom-call(bf16[32,2,16,512]{3,2,1,0:T(8,128)(2,1)} %bitcast.1.in_ref, bf16[2176,256]{1,0:T(8,128)(2,1)} %constant.37.clone.factor_ref, f32[128,256]{1,0:T(8,128)} %constant.38.clone.turn_ref), custom_call_target="tpu_custom_call" | custom-call | flops 5000000000 | bytes 2097152 | tf_op jit(solution)/shard_map/conv/pallas_call | solution.py:172
  64.0 4.9 %all-to-all-start.1 = ((bf16[32,16,512]{2,1,0:T(8,128)(2,1)}), bf16[32,16,512]{2,1,0:T(8,128)(2,1)}, u32[]{:S(2)}, u32[]{:S(2)}) async-start(bf16[32,16,512]{2,1,0:T(8,128)(2,1)} %conv.1), calls=%async_computation.1 | async-start | bytes 1048576 | tf_op jit(solution)/shard_map/all_to_all | solution.py:427
  68.9 17.4 %collective-permute-done.7.refs_4_ = bf16[1024,128]{1,0:T(8,128)(2,1)S(1)} collective-permute-done((bf16[1024,128]{1,0:T(8,128)(2,1)S(1)}, bf16[1024,128]{1,0:T(8,128)(2,1)S(1)}, u32[]{:S(2)}, u32[]{:S(2)}) %collective-permute-start.7) | collective-permute-done | bytes 262176 | tf_op jit(solution)/shard_map/ppermute | solution.py:395
  86.3 1.2 %copy-done.9 = f32[4,512,128]{2,1,0:T(8,128)S(1)} copy-done((f32[4,512,128]{2,1,0:T(8,128)S(1)}, f32[4,512,128]{2,1,0:T(8,128)}, u32[]{:S(2)}) %copy-start.9) | copy-done | bytes 1048600
  88.5 3.7 %back.3 = (bf16[512,512]{1,0:T(8,128)(2,1)S(1)}, f32[4,512]{1,0:T(4,128)S(1)}) custom-call(s32[3]{0:T(128)S(1)} %pad_add_fusion.where_ref.refs_0_, bf16[512,1024]{1,0:T(8,128)(2,1)S(1)} %collective-permute-done.2.other_ref.refs_1_, bf16[1024,128]{1,0:T(8,128)(2,1)S(1)} %collective-permute-done.1.refs_2_, ...), custom_call_target="tpu_custom_call" | custom-call | flops 99999997952 | bytes 4194304 | tf_op jit(solution)/shard_map/back/pallas_call | solution.py:348
  92.2 4.2 %collective-permute-start.10 = (f32[4,512]{1,0:T(4,128)S(1)}, f32[4,512]{1,0:T(4,128)S(1)}, u32[]{:S(2)}, u32[]{:S(2)}) collective-permute-start(f32[4,512]{1,0:T(4,128)S(1)} %get-tuple-element.32), channel_id=1, source_target_pairs={{0,1},{1,0},{2,3},{3,2},{4,5},{5,4},{6,7},{7,6},{8,9},{9,8},{10,11... | collective-permute-start | bytes 24584 | tf_op jit(solution)/shard_map/ppermute | solution.py:423
  96.5 3.7 %back.2 = (bf16[512,512]{1,0:T(8,128)(2,1)S(1)}, f32[4,512]{1,0:T(4,128)S(1)}) custom-call(s32[3]{0:T(128)S(1)} %pad_add_fusion.where_ref.refs_0_, bf16[512,1024]{1,0:T(8,128)(2,1)S(1)} %bitcast.13, bf16[1024,128]{1,0:T(8,128)(2,1)S(1)} %collective-permute-done.1.refs_2_, bf16[1024,128]{1,0:T(8,128)(2,1)S(1)} %collective-permute-done.6.refs_3_, ...), custom_call_target="tpu_custom_call" | custom-call | flops 99999997952 | bytes 4194304 | tf_op jit(solution)/shard_map/back/pallas_call | solution.py:348
  100.2 1.8 %merge.1 = (bf16[512,1024]{1,0:T(8,128)(2,1)}, f32[8,512]{1,0:T(8,128)}) custom-call(s32[3]{0:T(128)S(1)} %pad_add_fusion.where_ref.refs_0_, bf16[512,512]{1,0:T(8,128)(2,1)S(1)} %get-tuple-element.28.mine_ref, bf16[512,512]{1,0:T(8,128)(2,1)S(1)} %collective-permute-done.9.got_ref, f32[4,512]{1,0:T(4,128)S(1)} %get-tuple-element.31.mine_lse, ...), custom_call_target="tpu_custom_call" | custom-call | bytes 2097152 | tf_op jit(solution)/shard_map/merge/pallas_call | solution.py:379
  102.1 2.3 %gate.1 = bf16[512,512]{1,0:T(8,128)(2,1)} custom-call(bf16[512,512]{1,0:T(8,128)(2,1)} %bitcast.6.conv_ref, bf16[512,512]{1,0:T(8,128)(2,1)S(1)} %copy-done.3, bf16[512,512]{1,0:T(8,128)(2,1)S(1)} %copy-done, bf16[512,512]{1,0:T(8,128)(2,1)S(1)} %copy-done.1, f32[1,512]{1,0:T(1,128)S(1)} %bitcast.10), custom_call_target="tpu_custom_call" | custom-call | flops 268435456 | bytes 2621440 | tf_op jit(solution)/shard_map/gate/pallas_call | solution.py:197
  (41 shorter events, 4.3 us)
Async XLA Ops:
  0.6 36.1 %collective-permute-start.2 = (bf16[512,1024]{1,0:T(8,128)(2,1)}, bf16[512,1024]{1,0:T(8,128)(2,1)S(1)}, u32[]{:S(2)}, u32[]{:S(2)}) collective-permute-start(bf16[512,1024]{1,0:T(8,128)(2,1)} %bitcast.11), channel_id=1, source_target_pairs={{0,1},{1,0},{2,3},{3,2},{4,5},{5,4},{6,7},{7,6},{8,9},{9,8},{10,11... | collective-permute-start | bytes 3145736 | tf_op jit(solution)/shard_map/ppermute | solution.py:423
  5.6 12.8 %collective-permute-start.1 = (bf16[1024,128]{1,0:T(8,128)(2,1)}, bf16[1024,128]{1,0:T(8,128)(2,1)S(1)}, u32[]{:S(2)}, u32[]{:S(2)}) collective-permute-start(bf16[1024,128]{1,0:T(8,128)(2,1)} %pack.1.after_ref.refs_0_), channel_id=1, source_target_pairs={{0,8},{1,9},{2,10},{3,11},{4,12},{5,13},{6,14},{7,15},{8,16},{9,17... | collective-permute-start | bytes 786440 | tf_op jit(solution)/shard_map/ppermute | solution.py:419
  7.1 15.4 %collective-permute-start = (bf16[1024,128]{1,0:T(8,128)(2,1)}, bf16[1024,128]{1,0:T(8,128)(2,1)S(1)}, u32[]{:S(2)}, u32[]{:S(2)}) collective-permute-start(bf16[1024,128]{1,0:T(8,128)(2,1)} %pack.1.after_ref.refs_0_), channel_id=1, source_target_pairs={{0,4},{1,5},{2,6},{3,7},{4,0},{5,1},{6,2},{7,3},{8,12},{9,13},{10,... | collective-permute-start | bytes 786440 | tf_op jit(solution)/shard_map/ppermute | solution.py:395
  10.2 26.5 %collective-permute-start.4 = (bf16[1024,128]{1,0:T(8,128)(2,1)}, bf16[1024,128]{1,0:T(8,128)(2,1)S(1)}, u32[]{:S(2)}, u32[]{:S(2)}) collective-permute-start(bf16[1024,128]{1,0:T(8,128)(2,1)} %pack.1.after_ref.refs_0_), channel_id=1, source_target_pairs={{2,0},{3,1},{4,2},{5,3},{6,4},{7,5},{10,8},{11,9},{12,10},{13,11},... | collective-permute-start | bytes 786440 | tf_op jit(solution)/shard_map/ppermute | solution.py:395
  11.5 25.2 %collective-permute-start.3 = (bf16[1024,128]{1,0:T(8,128)(2,1)}, bf16[1024,128]{1,0:T(8,128)(2,1)S(1)}, u32[]{:S(2)}, u32[]{:S(2)}) collective-permute-start(bf16[1024,128]{1,0:T(8,128)(2,1)} %pack.1.after_ref.refs_0_), channel_id=1, source_target_pairs={{0,2},{1,3},{2,4},{3,5},{4,6},{5,7},{8,10},{9,11},{10,12},{11,13},... | collective-permute-start | bytes 786440 | tf_op jit(solution)/shard_map/ppermute | solution.py:395
  18.5 18.2 %copy-start.2 = (bf16[1024,128]{1,0:T(8,128)(2,1)S(1)}, bf16[1024,128]{1,0:T(8,128)(2,1)}, u32[]{:S(2)}) copy-start(bf16[1024,128]{1,0:T(8,128)(2,1)} %pack.1.after_ref.refs_0_) | copy-start | bytes 786436
  18.5 18.2 %copy-start.5 = (bf16[512,1,1024]{2,0,1:T(8,128)(2,1)S(1)}, bf16[512,1,1024]{2,0,1:T(8,128)(2,1)}, u32[]{:S(2)}) copy-start(bf16[512,1,1024]{2,0,1:T(8,128)(2,1)} %param.15) | copy-start | bytes 3145732
  22.5 14.2 %collective-permute-start.5 = (bf16[1024,128]{1,0:T(8,128)(2,1)S(1)}, bf16[1024,128]{1,0:T(8,128)(2,1)}, u32[]{:S(2)}, u32[]{:S(2)}) collective-permute-start(bf16[1024,128]{1,0:T(8,128)(2,1)S(1)} %collective-permute-done.refs_3_), channel_id=1, source_target_pairs={{4,6},{5,7},{2,0},{3,1},{12,14},{13,15},{10,8},{11,9},{20,22},{21,... | collective-permute-start | bytes 786440 | tf_op jit(solution)/shard_map/ppermute | solution.py:395
  23.8 31.5 %all-to-all-start = ((bf16[64,16,512]{2,1,0:T(8,128)(2,1)}), bf16[64,16,512]{2,1,0:T(8,128)(2,1)}, u32[]{:S(2)}, u32[]{:S(2)}) async-start(bf16[64,16,512]{2,1,0:T(8,128)(2,1)} %bitcast.14), calls=%async_computation | async-start | bytes 2097152 | tf_op jit(solution)/shard_map/all_to_all | solution.py:427
  41.3 1.0 copy-start.8
  43.7 25.2 %collective-permute-start.8 = (bf16[1024,128]{1,0:T(8,128)(2,1)S(1)}, bf16[1024,128]{1,0:T(8,128)(2,1)S(1)}, u32[]{:S(2)}, u32[]{:S(2)}) collective-permute-start(bf16[1024,128]{1,0:T(8,128)(2,1)S(1)} %collective-permute-done.1.refs_2_), channel_id=1, source_target_pairs={{0,6},{1,7},{2,0},{3,1},{4,2},{5,3},{6,4},{7,5},{8,14},{9,15},{10,... | collective-permute-start | bytes 786440 | tf_op jit(solution)/shard_map/ppermute | solution.py:395
  45.4 40.9 %collective-permute-start.7 = (bf16[1024,128]{1,0:T(8,128)(2,1)S(1)}, bf16[1024,128]{1,0:T(8,128)(2,1)S(1)}, u32[]{:S(2)}, u32[]{:S(2)}) collective-permute-start(bf16[1024,128]{1,0:T(8,128)(2,1)S(1)} %collective-permute-done.1.refs_2_), channel_id=1, source_target_pairs={{0,4},{1,5},{2,6},{3,7},{4,0},{5,1},{6,2},{7,3},{8,12},{9,13},{10,... | collective-permute-start | bytes 786440 | tf_op jit(solution)/shard_map/ppermute | solution.py:395
  47.6 38.6 %collective-permute-start.6 = (bf16[1024,128]{1,0:T(8,128)(2,1)S(1)}, bf16[1024,128]{1,0:T(8,128)(2,1)S(1)}, u32[]{:S(2)}, u32[]{:S(2)}) collective-permute-start(bf16[1024,128]{1,0:T(8,128)(2,1)S(1)} %collective-permute-done.1.refs_2_), channel_id=1, source_target_pairs={{0,2},{1,3},{2,4},{3,5},{4,6},{5,7},{6,0},{7,1},{8,10},{9,11},{10,... | collective-permute-start | bytes 786440 | tf_op jit(solution)/shard_map/ppermute | solution.py:395
  55.4 30.9 %copy-start.11 = (f32[512,128]{1,0:T(8,128)S(1)}, f32[512,128]{1,0:T(8,128)}, u32[]{:S(2)}) copy-start(f32[512,128]{1,0:T(8,128)} %copy-done.10) | copy-start | bytes 786436
  64.0 38.1 %all-to-all-start.1 = ((bf16[32,16,512]{2,1,0:T(8,128)(2,1)}), bf16[32,16,512]{2,1,0:T(8,128)(2,1)}, u32[]{:S(2)}, u32[]{:S(2)}) async-start(bf16[32,16,512]{2,1,0:T(8,128)(2,1)} %conv.1), calls=%async_computation.1 | async-start | bytes 1048576 | tf_op jit(solution)/shard_map/all_to_all | solution.py:427
  86.3 1.2 %copy-start.9 = (f32[4,512,128]{2,1,0:T(8,128)S(1)}, f32[4,512,128]{2,1,0:T(8,128)}, u32[]{:S(2)}) copy-start(f32[4,512,128]{2,1,0:T(8,128)} %copy-done.8) | copy-start | bytes 3145732
  88.5 8.0 %copy-start.7 = (f32[4,512,128]{2,1,0:T(8,128)S(1)}, f32[4,512,128]{2,1,0:T(8,128)}, u32[]{:S(2)}) copy-start(f32[4,512,128]{2,1,0:T(8,128)} %copy-done.6) | copy-start | bytes 3145732
  88.5 8.0 %copy-start.12 = (f32[512,128]{1,0:T(8,128)S(1)}, f32[512,128]{1,0:T(8,128)}, u32[]{:S(2)}) copy-start(f32[512,128]{1,0:T(8,128)} %copy-done.10) | copy-start | bytes 786436
  92.2 8.1 %collective-permute-start.10 = (f32[4,512]{1,0:T(4,128)S(1)}, f32[4,512]{1,0:T(4,128)S(1)}, u32[]{:S(2)}, u32[]{:S(2)}) collective-permute-start(f32[4,512]{1,0:T(4,128)S(1)} %get-tuple-element.32), channel_id=1, source_target_pairs={{0,1},{1,0},{2,3},{3,2},{4,5},{5,4},{6,7},{7,6},{8,9},{9,8},{10,11... | collective-permute-start | bytes 24584 | tf_op jit(solution)/shard_map/ppermute | solution.py:423
  96.4 3.9 %collective-permute-start.9 = (bf16[512,512]{1,0:T(8,128)(2,1)S(1)}, bf16[512,512]{1,0:T(8,128)(2,1)S(1)}, u32[]{:S(2)}, u32[]{:S(2)}) collective-permute-start(bf16[512,512]{1,0:T(8,128)(2,1)S(1)} %get-tuple-element.30), channel_id=1, source_target_pairs={{0,1},{1,0},{2,3},{3,2},{4,5},{5,4},{6,7},{7,6},{8,9},{9,8},{10,11... | collective-permute-start | bytes 1572872 | tf_op jit(solution)/shard_map/ppermute | solution.py:423
  96.5 5.6 %copy-start.3 = (bf16[512,512]{1,0:T(8,128)(2,1)S(1)}, bf16[512,512]{1,0:T(8,128)(2,1)}, u32[]{:S(2)}) copy-start(bf16[512,512]{1,0:T(8,128)(2,1)} %gate_ref.1) | copy-start | bytes 1572868
  96.5 5.6 %copy-start.4 = (f32[512]{0:T(512)S(1)}, f32[512]{0:T(512)}, u32[]{:S(2)}) copy-start(f32[512]{0:T(512)} %param.14) | copy-start | bytes 6148
  100.2 1.9 %copy-start = (bf16[512,512]{1,0:T(8,128)(2,1)S(1)}, bf16[512,512]{1,0:T(8,128)(2,1)}, u32[]{:S(2)}) copy-start(bf16[512,512]{1,0:T(8,128)(2,1)} %key_ref.5) | copy-start | bytes 1572868
  100.2 1.9 %copy-start.1 = (bf16[512,512]{1,0:T(8,128)(2,1)S(1)}, bf16[512,512]{1,0:T(8,128)(2,1)}, u32[]{:S(2)}) copy-start(bf16[512,512]{1,0:T(8,128)(2,1)} %value_ref.5) | copy-start | bytes 1572868
  (4 other events, 3.3 us)

commit v4 on v3

--- a/solution.py
+++ b/solution.py
@@ -62,8 +62,7 @@
     back = np.block([[cos, sin], [-sin, cos]])
     there_hi, there_lo = np_split(there)
     back_hi, back_lo = np_split(back)
-    factors = [first_both, there_hi, there_hi, there_lo, back_hi, back_hi, back_lo]
-    factors += [last_hi, last_hi, last_lo]
+    factors = [first_both, there_hi, there_lo, back_hi, back_lo, last_hi, last_lo]
     return np.concatenate(factors, axis=0), np.concatenate([turn_cos, turn_sin], axis=1)
 
 
@@ -105,6 +104,10 @@
 ):
     def factor(start, size):
         return factor_ref[start : start + size, :]
+
+    def three(start, size, axis):
+        high, low = factor(start, size), factor(start + size, size)
+        return jnp.concatenate([high, high, low], axis=axis)
 
     cos, sin = turn_ref[:, :COLS], turn_ref[:, COLS:]
     for which in range(2):
@@ -138,22 +141,21 @@
         for which in range(2):
             both = spec[which, rows, :]
             high = both[:, : 2 * COLS]
-            spectra.append(dot(jnp.concatenate([both, high], axis=1), factor(256, 768)))
+            spectra.append(dot(jnp.concatenate([both, high], axis=1), three(256, 256, 0)))
         sig, ker = spectra
         sig_re, sig_im, ker_re, ker_im = sig[:, :COLS], sig[:, COLS:], ker[:, :COLS], ker[:, COLS:]
         product = jnp.concatenate(
             [sig_re * ker_re - sig_im * ker_im, sig_re * ker_im + sig_im * ker_re], axis=1
         )
         high, low = split(product)
-        lines = dot(jnp.concatenate([high, low, high], axis=1), factor(1024, 768))
+        lines = dot(jnp.concatenate([high, low, high], axis=1), three(768, 256, 0))
         turned = []
         for k in range(many):
             re = lines[k * LINES : k * LINES + LINES, :COLS]
             im = lines[k * LINES : k * LINES + LINES, COLS:]
             turned.append(jnp.concatenate([re * cos - im * sin, im * cos + re * sin], axis=0))
         high, low = split(jnp.concatenate(turned, axis=1))
-        last = jnp.concatenate([factor(1792 + LINES * i, LINES) for i in range(3)], axis=1)
-        values = dot(last, jnp.concatenate([high, low, high], axis=0))
+        values = dot(three(1280, LINES, 1), jnp.concatenate([high, low, high], axis=0))
         for k in range(many):
             result[pl.ds(step * many + k, LINES, stride=MINE), :] = values[
                 :, k * COLS : k * COLS + COLS
@@ -184,20 +186,27 @@
 
 
 def gate_kernel(conv_ref, gate_ref, key_ref, value_ref, skip_ref, out_ref):
-    unit = eye(256)
-    for half in range(2):
-        rows = slice(half * 256, half * 256 + 256)
-        conv = dot(unit, conv_ref[:, rows], ONES)
-        signal = key_ref[rows, :].astype(F32) * value_ref[rows, :].astype(F32)
-        gate = gate_ref[rows, :].astype(F32)
-        out_ref[rows, :] = (gate * (conv + skip_ref[...] * signal)).astype(BF)
+    conv = dot(eye(256), conv_ref[...], ONES)
+    signal = key_ref[...].astype(F32) * value_ref[...].astype(F32)
+    gate = gate_ref[...].astype(F32)
+    out_ref[...] = (gate * (conv + skip_ref[...] * signal)).astype(BF)
 
 
 def gate_call(conv, gate, key, value, skip):
+    rows = pl.BlockSpec((256, CH), lambda i: (i, 0))
     return pl.pallas_call(
         gate_kernel,
+        grid=(2,),
+        in_specs=[
+            pl.BlockSpec((CH, 256), lambda i: (0, i)),
+            rows,
+            rows,
+            rows,
+            pl.BlockSpec((1, CH), lambda i: (0, 0)),
+        ],
+        out_specs=rows,
         out_shape=jax.ShapeDtypeStruct((TOK, CH), BF),
-        compiler_params=pltpu.CompilerParams(vmem_limit_bytes=14 * 2**20),
+        compiler_params=pltpu.CompilerParams(vmem_limit_bytes=ROOM),
         cost_estimate=pl.CostEstimate(flops=2**28, bytes_accessed=5 * 2**19, transcendentals=0),
         name="gate",
     )(conv, gate, key, value, skip)
@@ -304,7 +313,9 @@
 
 def back_kernel(member, where_ref, query_ref, *refs):
     pieces = refs[0:4]
-    acc_ref, peak_ref, total_ref, out_ref, lse_ref, keys = refs[4:]
+    acc_in, peak_ref, total_ref, out_ref, lse_ref, keys, acc_ref, sem = refs[4:]
+    copy = pltpu.make_async_copy(acc_in, acc_ref, sem)
+    copy.start()
     seq, line, core = where_ref[0], where_ref[1], where_ref[2]
     crossed = lax.rem(seq, 4) == 0
     for k in range(4):
@@ -322,6 +333,8 @@
 
     def finish(job, scores):
         place, h = job
+        if job == (0, 0):
+            copy.wait()
         column = member * 4 + place
         own_peak = peak_ref[tile_rows(h), column : column + 1]
         own_total = total_ref[tile_rows(h), column : column + 1]
@@ -351,9 +364,14 @@
             jax.ShapeDtypeStruct((TOK, 4 * HD), BF),
             jax.ShapeDtypeStruct((4, TOK), F32),
         ),
-        in_specs=[pl.BlockSpec(memory_space=pltpu.SMEM)] + [whole] * 8,
+        in_specs=[pl.BlockSpec(memory_space=pltpu.SMEM)] + [whole] * 5
+        + [pl.BlockSpec(memory_space=pl.ANY), whole, whole],
         out_specs=(whole,) * 2,
-        scratch_shapes=[pltpu.VMEM((4, 2 * TOK, 2 * HD), BF)],
+        scratch_shapes=[
+            pltpu.VMEM((4, 2 * TOK, 2 * HD), BF),
+            pltpu.VMEM((4, TOK, HD), F32),
+            pltpu.SemaphoreType.DMA,
+        ],
         compiler_params=pltpu.CompilerParams(vmem_limit_bytes=14 * 2**20),
         cost_estimate=pl.CostEstimate(
             flops=10**11, bytes_accessed=4 * 2**20, transcendentals=2 * 2**20

time: 105 us -> 105 us (level)
    unnamed x30 -> x20, local copies, waits for them, and re-layouts: 5.54 us -> 5.56 us
  transfers between devices with their start and end apart: 13 -> 13, of which waited for: 3 -> 3; matrix products, arithmetic and copies ran while one was open for 0% -> 0% of each run, Pallas kernels for 25% -> 24%
where the time goes in v4:
time: 105 us; the launch traced here: 104 us
  starting transfers between devices  41.6 us (40%)
  waiting for transfers between devices  28.4 us (27%)
  Pallas kernels  28 us (27%)
  local copies, waits for them, and re-layouts  5.56 us (5%)
    ppermute x7, waiting for transfers between devices, one_line(): return lax.ppermute(x, 'chan', pairs)  21.4 us
    all_to_all x2, starting transfers between devices, exchange(): return lax.all_to_all(x, 'seq', split_axis=0, concat_axis=0, tiled=True)  17.9 us
    ppermute x7, starting transfers between devices, one_line(): return lax.ppermute(x, 'chan', pairs)  14.5 us
    pallas_call x1, Pallas kernels, conv_call(): pl.pallas_call(conv_kernel, out_shape=jax.ShapeDtypeStruct((SEQ, MINE, TO...  8.46 us
    ppermute x3, starting transfers between devices, swap(): return lax.ppermute(x, 'chan', [(c, c ^ 1) for c in range(CHAN)])  7.68 us
    pallas_call x2, Pallas kernels, back_call(): pl.pallas_call(kernel, out_shape=(jax.ShapeDtypeStruct((TOK, 4 * HD), BF)...  7.11 us
    all_to_all x2, waiting for transfers between devices, exchange(): return lax.all_to_all(x, 'seq', split_axis=0, concat_axis=0, tiled=True)  6.97 us
    unnamed x20, local copies, waits for them, and re-layouts  5.56 us
  transfers between devices with their start and end apart: 13, of which 3 were waited for; matrix products, arithmetic and copies ran while one was open for 0% of the time, Pallas kernels for 24%

profile of v4, /device:TPU:1, one launch (start us, length us, event | category | flops | bytes accessed | tf_op | source)
XLA Modules:
  0.0 104.5 jit_solution(11242125248896481962)
XLA Ops:
  0.6 3.3 %collective-permute-start.2 = (bf16[512,1024]{1,0:T(8,128)(2,1)}, bf16[512,1024]{1,0:T(8,128)(2,1)S(1)}, u32[]{:S(2)}, u32[]{:S(2)}) collective-permute-start(bf16[512,1024]{1,0:T(8,128)(2,1)} %bitcast.10), channel_id=1, source_target_pairs={{0,1},{1,0},{2,3},{3,2},{4,5},{5,4},{6,7},{7,6},{8,9},{9,8},{10,11... | collective-permute-start | bytes 3145736 | tf_op jit(solution)/shard_map/ppermute | solution.py:441
  4.0 1.7 %pack.1.after_ref.refs_0_ = bf16[1024,128]{1,0:T(8,128)(2,1)} custom-call(bf16[512,128]{1,0:T(8,128)(2,1)} %key_ref.3, bf16[512,128]{1,0:T(8,128)(2,1)} %value_ref.3), custom_call_target="tpu_custom_call" | custom-call | bytes 524288 | tf_op jit(solution)/shard_map/pack/pallas_call | solution.py:221
  5.6 1.5 %collective-permute-start.1 = (bf16[1024,128]{1,0:T(8,128)(2,1)}, bf16[1024,128]{1,0:T(8,128)(2,1)S(1)}, u32[]{:S(2)}, u32[]{:S(2)}) collective-permute-start(bf16[1024,128]{1,0:T(8,128)(2,1)} %pack.1.after_ref.refs_0_), channel_id=1, source_target_pairs={{0,8},{1,9},{2,10},{3,11},{4,12},{5,13},{6,14},{7,15},{8,16},{9,17... | collective-permute-start | bytes 786440 | tf_op jit(solution)/shard_map/ppermute | solution.py:437
  7.1 3.1 %collective-permute-start = (bf16[1024,128]{1,0:T(8,128)(2,1)}, bf16[1024,128]{1,0:T(8,128)(2,1)S(1)}, u32[]{:S(2)}, u32[]{:S(2)}) collective-permute-start(bf16[1024,128]{1,0:T(8,128)(2,1)} %pack.1.after_ref.refs_0_), channel_id=1, source_target_pairs={{0,4},{1,5},{2,6},{3,7},{4,0},{5,1},{6,2},{7,3},{8,12},{9,13},{10,... | collective-permute-start | bytes 786440 | tf_op jit(solution)/shard_map/ppermute | solution.py:413
  10.2 1.3 %collective-permute-start.4 = (bf16[1024,128]{1,0:T(8,128)(2,1)}, bf16[1024,128]{1,0:T(8,128)(2,1)S(1)}, u32[]{:S(2)}, u32[]{:S(2)}) collective-permute-start(bf16[1024,128]{1,0:T(8,128)(2,1)} %pack.1.after_ref.refs_0_), channel_id=1, source_target_pairs={{2,0},{3,1},{4,2},{5,3},{6,4},{7,5},{10,8},{11,9},{12,10},{13,11},... | collective-permute-start | bytes 786440 | tf_op jit(solution)/shard_map/ppermute | solution.py:413
  11.5 4.2 %collective-permute-start.3 = (bf16[1024,128]{1,0:T(8,128)(2,1)}, bf16[1024,128]{1,0:T(8,128)(2,1)S(1)}, u32[]{:S(2)}, u32[]{:S(2)}) collective-permute-start(bf16[1024,128]{1,0:T(8,128)(2,1)} %pack.1.after_ref.refs_0_), channel_id=1, source_target_pairs={{0,2},{1,3},{2,4},{3,5},{4,6},{5,7},{8,10},{9,11},{10,12},{11,13},... | collective-permute-start | bytes 786440 | tf_op jit(solution)/shard_map/ppermute | solution.py:413
  15.7 2.8 %turn.1 = bf16[32,2,16,512]{3,2,1,0:T(8,128)(2,1)} custom-call(bf16[512,512]{1,0:T(8,128)(2,1)} %key_ref.5, bf16[512,512]{1,0:T(8,128)(2,1)} %value_ref.5, bf16[512,512]{1,0:T(8,128)(2,1)} %filter_ref.1, bf16[1024,128]{1,0:T(8,128)(2,1)} %pack.1.after_ref.refs_0_), custom_call_target="tpu_custom_call" | custom-call | flops 536870912 | bytes 2621440 | tf_op jit(solution)/shard_map/turn/pallas_call | solution.py:86
  18.5 4.1 %collective-permute-done.refs_3_ = bf16[1024,128]{1,0:T(8,128)(2,1)S(1)} collective-permute-done((bf16[1024,128]{1,0:T(8,128)(2,1)}, bf16[1024,128]{1,0:T(8,128)(2,1)S(1)}, u32[]{:S(2)}, u32[]{:S(2)}) %collective-permute-start) | collective-permute-done | bytes 262176 | tf_op jit(solution)/shard_map/ppermute | solution.py:413
  22.5 1.3 %collective-permute-start.5 = (bf16[1024,128]{1,0:T(8,128)(2,1)S(1)}, bf16[1024,128]{1,0:T(8,128)(2,1)}, u32[]{:S(2)}, u32[]{:S(2)}) collective-permute-start(bf16[1024,128]{1,0:T(8,128)(2,1)S(1)} %collective-permute-done.refs_3_), channel_id=1, source_target_pairs={{4,6},{5,7},{2,0},{3,1},{12,14},{13,15},{10,8},{11,9},{20,22},{21,... | collective-permute-start | bytes 786440 | tf_op jit(solution)/shard_map/ppermute | solution.py:413
  23.9 12.9 %all-to-all-start = ((bf16[64,16,512]{2,1,0:T(8,128)(2,1)}), bf16[64,16,512]{2,1,0:T(8,128)(2,1)}, u32[]{:S(2)}, u32[]{:S(2)}) async-start(bf16[64,16,512]{2,1,0:T(8,128)(2,1)} %bitcast.13), calls=%async_computation | async-start | bytes 2097152 | tf_op jit(solution)/shard_map/all_to_all | solution.py:445
  36.9 3.6 %own.1 = (f32[4,512,128]{2,1,0:T(8,128)S(1)}, f32[4,512,128]{2,1,0:T(8,128)S(1)}, f32[512,128]{1,0:T(8,128)S(1)}, f32[512,128]{1,0:T(8,128)S(1)}) custom-call(s32[3]{0:T(128)S(1)} %pad_add_fusion.where_ref.refs_0_, bf16[512,1024]{1,0:T(8,128)(2,1)S(1)} %bitcast.11, bf16[512,1024]{1,0:T(8,128)(2,1)S(1)} %collective-permute-done.2.other_ref.refs_1_, ...), custom_call_target="tpu_custom_call" | custom-call | flops 40000000000 | bytes 4194304 | tf_op jit(solution)/shard_map/own/pallas_call | solution.py:300
  41.5 1.0 copy-done.4
  43.9 1.7 %collective-permute-start.8 = (bf16[1024,128]{1,0:T(8,128)(2,1)S(1)}, bf16[1024,128]{1,0:T(8,128)(2,1)S(1)}, u32[]{:S(2)}, u32[]{:S(2)}) collective-permute-start(bf16[1024,128]{1,0:T(8,128)(2,1)S(1)} %collective-permute-done.1.refs_2_), channel_id=1, source_target_pairs={{0,6},{1,7},{2,0},{3,1},{4,2},{5,3},{6,4},{7,5},{8,14},{9,15},{10,... | collective-permute-start | bytes 786440 | tf_op jit(solution)/shard_map/ppermute | solution.py:413
  45.5 2.3 %collective-permute-start.7 = (bf16[1024,128]{1,0:T(8,128)(2,1)S(1)}, bf16[1024,128]{1,0:T(8,128)(2,1)S(1)}, u32[]{:S(2)}, u32[]{:S(2)}) collective-permute-start(bf16[1024,128]{1,0:T(8,128)(2,1)S(1)} %collective-permute-done.1.refs_2_), channel_id=1, source_target_pairs={{0,4},{1,5},{2,6},{3,7},{4,0},{5,1},{6,2},{7,3},{8,12},{9,13},{10,... | collective-permute-start | bytes 786440 | tf_op jit(solution)/shard_map/ppermute | solution.py:413
  48.6 7.0 %all-to-all-done = bf16[64,16,512]{2,1,0:T(8,128)(2,1)} async-done(((bf16[64,16,512]{2,1,0:T(8,128)(2,1)}), bf16[64,16,512]{2,1,0:T(8,128)(2,1)}, u32[]{:S(2)}, u32[]{:S(2)}) %all-to-all-start) | async-done | bytes 1048608 | tf_op jit(solution)/shard_map/all_to_all | solution.py:445
  55.5 8.5 %conv.1 = bf16[32,16,512]{2,1,0:T(8,128)(2,1)} custom-call(bf16[32,2,16,512]{3,2,1,0:T(8,128)(2,1)} %bitcast.1.in_ref, bf16[1536,256]{1,0:T(8,128)(2,1)} %constant.37.clone.factor_ref, f32[128,256]{1,0:T(8,128)} %constant.38.clone.turn_ref), custom_call_target="tpu_custom_call" | custom-call | flops 5000000000 | bytes 2097152 | tf_op jit(solution)/shard_map/conv/pallas_call | solution.py:174
  64.0 5.0 %all-to-all-start.1 = ((bf16[32,16,512]{2,1,0:T(8,128)(2,1)}), bf16[32,16,512]{2,1,0:T(8,128)(2,1)}, u32[]{:S(2)}, u32[]{:S(2)}) async-start(bf16[32,16,512]{2,1,0:T(8,128)(2,1)} %conv.1), calls=%async_computation.1 | async-start | bytes 1048576 | tf_op jit(solution)/shard_map/all_to_all | solution.py:445
  69.1 17.4 %collective-permute-done.7.refs_4_ = bf16[1024,128]{1,0:T(8,128)(2,1)S(1)} collective-permute-done((bf16[1024,128]{1,0:T(8,128)(2,1)S(1)}, bf16[1024,128]{1,0:T(8,128)(2,1)S(1)}, u32[]{:S(2)}, u32[]{:S(2)}) %collective-permute-start.7) | collective-permute-done | bytes 262176 | tf_op jit(solution)/shard_map/ppermute | solution.py:413
  86.4 1.2 %copy-done.5 = f32[4,512,128]{2,1,0:T(8,128)S(1)} copy-done((f32[4,512,128]{2,1,0:T(8,128)S(1)}, f32[4,512,128]{2,1,0:T(8,128)}, u32[]{:S(2)}) %copy-start.5) | copy-done | bytes 1048600
  88.6 3.6 %back.3 = (bf16[512,512]{1,0:T(8,128)(2,1)S(1)}, f32[4,512]{1,0:T(4,128)S(1)}) custom-call(s32[3]{0:T(128)S(1)} %pad_add_fusion.where_ref.refs_0_, bf16[512,1024]{1,0:T(8,128)(2,1)S(1)} %collective-permute-done.2.other_ref.refs_1_, bf16[1024,128]{1,0:T(8,128)(2,1)S(1)} %collective-permute-done.1.refs_2_, ...), custom_call_target="tpu_custom_call" | custom-call | flops 99999997952 | bytes 4194304 | tf_op jit(solution)/shard_map/back/pallas_call | solution.py:361
  92.2 4.2 %collective-permute-start.10 = (f32[4,512]{1,0:T(4,128)S(1)}, f32[4,512]{1,0:T(4,128)S(1)}, u32[]{:S(2)}, u32[]{:S(2)}) collective-permute-start(f32[4,512]{1,0:T(4,128)S(1)} %get-tuple-element.32), channel_id=1, source_target_pairs={{0,1},{1,0},{2,3},{3,2},{4,5},{5,4},{6,7},{7,6},{8,9},{9,8},{10,11... | collective-permute-start | bytes 24584 | tf_op jit(solution)/shard_map/ppermute | solution.py:441
  96.5 3.6 %back.2 = (bf16[512,512]{1,0:T(8,128)(2,1)S(1)}, f32[4,512]{1,0:T(4,128)S(1)}) custom-call(s32[3]{0:T(128)S(1)} %pad_add_fusion.where_ref.refs_0_, bf16[512,1024]{1,0:T(8,128)(2,1)S(1)} %bitcast.12, bf16[1024,128]{1,0:T(8,128)(2,1)S(1)} %collective-permute-done.1.refs_2_, bf16[1024,128]{1,0:T(8,128)(2,1)S(1)} %collective-permute-done.6.refs_3_, ...), custom_call_target="tpu_custom_call" | custom-call | flops 99999997952 | bytes 4194304 | tf_op jit(solution)/shard_map/back/pallas_call | solution.py:361
  100.1 1.8 %merge.1 = (bf16[512,1024]{1,0:T(8,128)(2,1)}, f32[8,512]{1,0:T(8,128)}) custom-call(s32[3]{0:T(128)S(1)} %pad_add_fusion.where_ref.refs_0_, bf16[512,512]{1,0:T(8,128)(2,1)S(1)} %get-tuple-element.28.mine_ref, bf16[512,512]{1,0:T(8,128)(2,1)S(1)} %collective-permute-done.9.got_ref, f32[4,512]{1,0:T(4,128)S(1)} %get-tuple-element.31.mine_lse, ...), custom_call_target="tpu_custom_call" | custom-call | bytes 2097152 | tf_op jit(solution)/shard_map/merge/pallas_call | solution.py:397
  101.9 2.5 %gate.1 = bf16[512,512]{1,0:T(8,128)(2,1)} custom-call(bf16[512,512]{1,0:T(8,128)(2,1)} %bitcast.6.conv_ref, bf16[512,512]{1,0:T(8,128)(2,1)} %gate_ref.1, bf16[512,512]{1,0:T(8,128)(2,1)} %key_ref.5, bf16[512,512]{1,0:T(8,128)(2,1)} %value_ref.5, f32[1,512]{1,0:T(1,128)} %bitcast.14), custom_call_target="tpu_custom_call" | custom-call | flops 268435456 | bytes 2621440 | tf_op jit(solution)/shard_map/gate/pallas_call | solution.py:197
  (31 shorter events, 4.3 us)
Async XLA Ops:
  0.6 36.2 %collective-permute-start.2 = (bf16[512,1024]{1,0:T(8,128)(2,1)}, bf16[512,1024]{1,0:T(8,128)(2,1)S(1)}, u32[]{:S(2)}, u32[]{:S(2)}) collective-permute-start(bf16[512,1024]{1,0:T(8,128)(2,1)} %bitcast.10), channel_id=1, source_target_pairs={{0,1},{1,0},{2,3},{3,2},{4,5},{5,4},{6,7},{7,6},{8,9},{9,8},{10,11... | collective-permute-start | bytes 3145736 | tf_op jit(solution)/shard_map/ppermute | solution.py:441
  5.6 12.8 %collective-permute-start.1 = (bf16[1024,128]{1,0:T(8,128)(2,1)}, bf16[1024,128]{1,0:T(8,128)(2,1)S(1)}, u32[]{:S(2)}, u32[]{:S(2)}) collective-permute-start(bf16[1024,128]{1,0:T(8,128)(2,1)} %pack.1.after_ref.refs_0_), channel_id=1, source_target_pairs={{0,8},{1,9},{2,10},{3,11},{4,12},{5,13},{6,14},{7,15},{8,16},{9,17... | collective-permute-start | bytes 786440 | tf_op jit(solution)/shard_map/ppermute | solution.py:437
  7.1 15.4 %collective-permute-start = (bf16[1024,128]{1,0:T(8,128)(2,1)}, bf16[1024,128]{1,0:T(8,128)(2,1)S(1)}, u32[]{:S(2)}, u32[]{:S(2)}) collective-permute-start(bf16[1024,128]{1,0:T(8,128)(2,1)} %pack.1.after_ref.refs_0_), channel_id=1, source_target_pairs={{0,4},{1,5},{2,6},{3,7},{4,0},{5,1},{6,2},{7,3},{8,12},{9,13},{10,... | collective-permute-start | bytes 786440 | tf_op jit(solution)/shard_map/ppermute | solution.py:413
  10.2 26.6 %collective-permute-start.4 = (bf16[1024,128]{1,0:T(8,128)(2,1)}, bf16[1024,128]{1,0:T(8,128)(2,1)S(1)}, u32[]{:S(2)}, u32[]{:S(2)}) collective-permute-start(bf16[1024,128]{1,0:T(8,128)(2,1)} %pack.1.after_ref.refs_0_), channel_id=1, source_target_pairs={{2,0},{3,1},{4,2},{5,3},{6,4},{7,5},{10,8},{11,9},{12,10},{13,11},... | collective-permute-start | bytes 786440 | tf_op jit(solution)/shard_map/ppermute | solution.py:413
  11.5 25.4 %collective-permute-start.3 = (bf16[1024,128]{1,0:T(8,128)(2,1)}, bf16[1024,128]{1,0:T(8,128)(2,1)S(1)}, u32[]{:S(2)}, u32[]{:S(2)}) collective-permute-start(bf16[1024,128]{1,0:T(8,128)(2,1)} %pack.1.after_ref.refs_0_), channel_id=1, source_target_pairs={{0,2},{1,3},{2,4},{3,5},{4,6},{5,7},{8,10},{9,11},{10,12},{11,13},... | collective-permute-start | bytes 786440 | tf_op jit(solution)/shard_map/ppermute | solution.py:413
  22.5 14.3 %collective-permute-start.5 = (bf16[1024,128]{1,0:T(8,128)(2,1)S(1)}, bf16[1024,128]{1,0:T(8,128)(2,1)}, u32[]{:S(2)}, u32[]{:S(2)}) collective-permute-start(bf16[1024,128]{1,0:T(8,128)(2,1)S(1)} %collective-permute-done.refs_3_), channel_id=1, source_target_pairs={{4,6},{5,7},{2,0},{3,1},{12,14},{13,15},{10,8},{11,9},{20,22},{21,... | collective-permute-start | bytes 786440 | tf_op jit(solution)/shard_map/ppermute | solution.py:413
  23.8 13.0 %copy-start = (bf16[1024,128]{1,0:T(8,128)(2,1)S(1)}, bf16[1024,128]{1,0:T(8,128)(2,1)}, u32[]{:S(2)}) copy-start(bf16[1024,128]{1,0:T(8,128)(2,1)} %pack.1.after_ref.refs_0_) | copy-start | bytes 786436
  23.8 13.0 %copy-start.1 = (bf16[512,1,1024]{2,0,1:T(8,128)(2,1)S(1)}, bf16[512,1,1024]{2,0,1:T(8,128)(2,1)}, u32[]{:S(2)}) copy-start(bf16[512,1,1024]{2,0,1:T(8,128)(2,1)} %param.15) | copy-start | bytes 3145732
  23.9 31.7 %all-to-all-start = ((bf16[64,16,512]{2,1,0:T(8,128)(2,1)}), bf16[64,16,512]{2,1,0:T(8,128)(2,1)}, u32[]{:S(2)}, u32[]{:S(2)}) async-start(bf16[64,16,512]{2,1,0:T(8,128)(2,1)} %bitcast.13), calls=%async_computation | async-start | bytes 2097152 | tf_op jit(solution)/shard_map/all_to_all | solution.py:445
  40.5 1.0 copy-start.2
  41.4 1.0 copy-start.4
  42.4 0.7 copy-start.6
  43.2 0.7 copy-start.8
  43.9 25.2 %collective-permute-start.8 = (bf16[1024,128]{1,0:T(8,128)(2,1)S(1)}, bf16[1024,128]{1,0:T(8,128)(2,1)S(1)}, u32[]{:S(2)}, u32[]{:S(2)}) collective-permute-start(bf16[1024,128]{1,0:T(8,128)(2,1)S(1)} %collective-permute-done.1.refs_2_), channel_id=1, source_target_pairs={{0,6},{1,7},{2,0},{3,1},{4,2},{5,3},{6,4},{7,5},{8,14},{9,15},{10,... | collective-permute-start | bytes 786440 | tf_op jit(solution)/shard_map/ppermute | solution.py:413
  45.5 40.9 %collective-permute-start.7 = (bf16[1024,128]{1,0:T(8,128)(2,1)S(1)}, bf16[1024,128]{1,0:T(8,128)(2,1)S(1)}, u32[]{:S(2)}, u32[]{:S(2)}) collective-permute-start(bf16[1024,128]{1,0:T(8,128)(2,1)S(1)} %collective-permute-done.1.refs_2_), channel_id=1, source_target_pairs={{0,4},{1,5},{2,6},{3,7},{4,0},{5,1},{6,2},{7,3},{8,12},{9,13},{10,... | collective-permute-start | bytes 786440 | tf_op jit(solution)/shard_map/ppermute | solution.py:413
  47.8 38.6 %collective-permute-start.6 = (bf16[1024,128]{1,0:T(8,128)(2,1)S(1)}, bf16[1024,128]{1,0:T(8,128)(2,1)S(1)}, u32[]{:S(2)}, u32[]{:S(2)}) collective-permute-start(bf16[1024,128]{1,0:T(8,128)(2,1)S(1)} %collective-permute-done.1.refs_2_), channel_id=1, source_target_pairs={{0,2},{1,3},{2,4},{3,5},{4,6},{5,7},{6,0},{7,1},{8,10},{9,11},{10,... | collective-permute-start | bytes 786440 | tf_op jit(solution)/shard_map/ppermute | solution.py:413
  64.0 22.4 %copy-start.7 = (f32[512,128]{1,0:T(8,128)S(1)}, f32[512,128]{1,0:T(8,128)}, u32[]{:S(2)}) copy-start(f32[512,128]{1,0:T(8,128)} %copy-done.6) | copy-start | bytes 786436
  64.0 37.9 %all-to-all-start.1 = ((bf16[32,16,512]{2,1,0:T(8,128)(2,1)}), bf16[32,16,512]{2,1,0:T(8,128)(2,1)}, u32[]{:S(2)}, u32[]{:S(2)}) async-start(bf16[32,16,512]{2,1,0:T(8,128)(2,1)} %conv.1), calls=%async_computation.1 | async-start | bytes 1048576 | tf_op jit(solution)/shard_map/all_to_all | solution.py:445
  86.4 1.2 %copy-start.5 = (f32[4,512,128]{2,1,0:T(8,128)S(1)}, f32[4,512,128]{2,1,0:T(8,128)}, u32[]{:S(2)}) copy-start(f32[4,512,128]{2,1,0:T(8,128)} %copy-done.4) | copy-start | bytes 3145732
  87.6 0.9 copy-start.9
  88.6 7.9 %copy-start.3 = (f32[4,512,128]{2,1,0:T(8,128)S(1)}, f32[4,512,128]{2,1,0:T(8,128)}, u32[]{:S(2)}) copy-start(f32[4,512,128]{2,1,0:T(8,128)} %copy-done.2) | copy-start | bytes 3145732
  92.2 7.9 %collective-permute-start.10 = (f32[4,512]{1,0:T(4,128)S(1)}, f32[4,512]{1,0:T(4,128)S(1)}, u32[]{:S(2)}, u32[]{:S(2)}) collective-permute-start(f32[4,512]{1,0:T(4,128)S(1)} %get-tuple-element.32), channel_id=1, source_target_pairs={{0,1},{1,0},{2,3},{3,2},{4,5},{5,4},{6,7},{7,6},{8,9},{9,8},{10,11... | collective-permute-start | bytes 24584 | tf_op jit(solution)/shard_map/ppermute | solution.py:441
  96.4 3.7 %collective-permute-start.9 = (bf16[512,512]{1,0:T(8,128)(2,1)S(1)}, bf16[512,512]{1,0:T(8,128)(2,1)S(1)}, u32[]{:S(2)}, u32[]{:S(2)}) collective-permute-start(bf16[512,512]{1,0:T(8,128)(2,1)S(1)} %get-tuple-element.30), channel_id=1, source_target_pairs={{0,1},{1,0},{2,3},{3,2},{4,5},{5,4},{6,7},{7,6},{8,9},{9,8},{10,11... | collective-permute-start | bytes 1572872 | tf_op jit(solution)/shard_map/ppermute | solution.py:441

commit v5 on v4

--- a/solution.py
+++ b/solution.py
@@ -452,7 +452,8 @@
     where = jnp.stack([seq, chan // 2, chan % 2]).astype(jnp.int32)
     query = attn_query.reshape(TOK, KVH * HD)
     kv = pack_call(attn_keys, attn_values)
-    query_got = swap(query)
+    given_query, kv_ready = lax.optimization_barrier((query, kv))
+    query_got = swap(given_query)
     kv_behind = to_next(kv)
     own = gather_near(kv)
     turned = turn_call(hyena_key, hyena_value, long_filter, kv)

time: 105 us -> 105 us (level)
  transfers between devices with their start and end apart: 13 -> 13, of which waited for: 3 -> 3; matrix products, arithmetic and copies ran while one was open for 0% -> 0% of each run, Pallas kernels for 24% -> 23%
where the time goes in v5:
time: 105 us; the launch traced here: 104 us
  starting transfers between devices  41.5 us (40%)
  waiting for transfers between devices  28.4 us (27%)
  Pallas kernels  28 us (27%)
  local copies, waits for them, and re-layouts  5.56 us (5%)
    ppermute x7, waiting for transfers between devices, one_line(): return lax.ppermute(x, 'chan', pairs)  21.4 us
    all_to_all x2, starting transfers between devices, exchange(): return lax.all_to_all(x, 'seq', split_axis=0, concat_axis=0, tiled=True)  17.9 us
    ppermute x7, starting transfers between devices, one_line(): return lax.ppermute(x, 'chan', pairs)  14.5 us
    pallas_call x1, Pallas kernels, conv_call(): pl.pallas_call(conv_kernel, out_shape=jax.ShapeDtypeStruct((SEQ, MINE, TO...  8.46 us
    ppermute x3, starting transfers between devices, swap(): return lax.ppermute(x, 'chan', [(c, c ^ 1) for c in range(CHAN)])  7.59 us
    pallas_call x2, Pallas kernels, back_call(): pl.pallas_call(kernel, out_shape=(jax.ShapeDtypeStruct((TOK, 4 * HD), BF)...  7.1 us
    all_to_all x2, waiting for transfers between devices, exchange(): return lax.all_to_all(x, 'seq', split_axis=0, concat_axis=0, tiled=True)  6.97 us
    unnamed x20, local copies, waits for them, and re-layouts  5.56 us
  transfers between devices with their start and end apart: 13, of which 3 were waited for; matrix products, arithmetic and copies ran while one was open for 0% of the time, Pallas kernels for 23%

profile of v5, /device:TPU:1, one launch (start us, length us, event | category | flops | bytes accessed | tf_op | source)
XLA Modules:
  0.0 104.4 jit_solution(10043998686844843261)
XLA Ops:
  0.6 1.7 %pack.1.after_ref.refs_0_ = bf16[1024,128]{1,0:T(8,128)(2,1)} custom-call(bf16[512,128]{1,0:T(8,128)(2,1)} %key_ref.3, bf16[512,128]{1,0:T(8,128)(2,1)} %value_ref.3), custom_call_target="tpu_custom_call" | custom-call | bytes 524288 | tf_op jit(solution)/shard_map/pack/pallas_call | solution.py:221
  2.3 3.2 %collective-permute-start.2 = (bf16[512,1024]{1,0:T(8,128)(2,1)}, bf16[512,1024]{1,0:T(8,128)(2,1)S(1)}, u32[]{:S(2)}, u32[]{:S(2)}) collective-permute-start(bf16[512,1024]{1,0:T(8,128)(2,1)} %bitcast.10), channel_id=1, source_target_pairs={{0,1},{1,0},{2,3},{3,2},{4,5},{5,4},{6,7},{7,6},{8,9},{9,8},{10,11... | collective-permute-start | bytes 3145736 | tf_op jit(solution)/shard_map/ppermute | solution.py:441
  5.6 1.5 %collective-permute-start.1 = (bf16[1024,128]{1,0:T(8,128)(2,1)}, bf16[1024,128]{1,0:T(8,128)(2,1)S(1)}, u32[]{:S(2)}, u32[]{:S(2)}) collective-permute-start(bf16[1024,128]{1,0:T(8,128)(2,1)} %pack.1.after_ref.refs_0_), channel_id=1, source_target_pairs={{0,8},{1,9},{2,10},{3,11},{4,12},{5,13},{6,14},{7,15},{8,16},{9,17... | collective-permute-start | bytes 786440 | tf_op jit(solution)/shard_map/ppermute | solution.py:437
  7.0 3.1 %collective-permute-start = (bf16[1024,128]{1,0:T(8,128)(2,1)}, bf16[1024,128]{1,0:T(8,128)(2,1)S(1)}, u32[]{:S(2)}, u32[]{:S(2)}) collective-permute-start(bf16[1024,128]{1,0:T(8,128)(2,1)} %pack.1.after_ref.refs_0_), channel_id=1, source_target_pairs={{0,4},{1,5},{2,6},{3,7},{4,0},{5,1},{6,2},{7,3},{8,12},{9,13},{10,... | collective-permute-start | bytes 786440 | tf_op jit(solution)/shard_map/ppermute | solution.py:413
  10.1 1.3 %collective-permute-start.4 = (bf16[1024,128]{1,0:T(8,128)(2,1)}, bf16[1024,128]{1,0:T(8,128)(2,1)S(1)}, u32[]{:S(2)}, u32[]{:S(2)}) collective-permute-start(bf16[1024,128]{1,0:T(8,128)(2,1)} %pack.1.after_ref.refs_0_), channel_id=1, source_target_pairs={{2,0},{3,1},{4,2},{5,3},{6,4},{7,5},{10,8},{11,9},{12,10},{13,11},... | collective-permute-start | bytes 786440 | tf_op jit(solution)/shard_map/ppermute | solution.py:413
  11.4 4.2 %collective-permute-start.3 = (bf16[1024,128]{1,0:T(8,128)(2,1)}, bf16[1024,128]{1,0:T(8,128)(2,1)S(1)}, u32[]{:S(2)}, u32[]{:S(2)}) collective-permute-start(bf16[1024,128]{1,0:T(8,128)(2,1)} %pack.1.after_ref.refs_0_), channel_id=1, source_target_pairs={{0,2},{1,3},{2,4},{3,5},{4,6},{5,7},{8,10},{9,11},{10,12},{11,13},... | collective-permute-start | bytes 786440 | tf_op jit(solution)/shard_map/ppermute | solution.py:413
  15.6 2.8 %turn.1 = bf16[32,2,16,512]{3,2,1,0:T(8,128)(2,1)} custom-call(bf16[512,512]{1,0:T(8,128)(2,1)} %key_ref.5, bf16[512,512]{1,0:T(8,128)(2,1)} %value_ref.5, bf16[512,512]{1,0:T(8,128)(2,1)} %filter_ref.1, bf16[1024,128]{1,0:T(8,128)(2,1)} %pack.1.after_ref.refs_0_), custom_call_target="tpu_custom_call" | custom-call | flops 536870912 | bytes 2621440 | tf_op jit(solution)/shard_map/turn/pallas_call | solution.py:86
  18.4 4.1 %collective-permute-done.refs_3_ = bf16[1024,128]{1,0:T(8,128)(2,1)S(1)} collective-permute-done((bf16[1024,128]{1,0:T(8,128)(2,1)}, bf16[1024,128]{1,0:T(8,128)(2,1)S(1)}, u32[]{:S(2)}, u32[]{:S(2)}) %collective-permute-start) | collective-permute-done | bytes 262176 | tf_op jit(solution)/shard_map/ppermute | solution.py:413
  22.5 1.3 %collective-permute-start.5 = (bf16[1024,128]{1,0:T(8,128)(2,1)S(1)}, bf16[1024,128]{1,0:T(8,128)(2,1)}, u32[]{:S(2)}, u32[]{:S(2)}) collective-permute-start(bf16[1024,128]{1,0:T(8,128)(2,1)S(1)} %collective-permute-done.refs_3_), channel_id=1, source_target_pairs={{4,6},{5,7},{2,0},{3,1},{12,14},{13,15},{10,8},{11,9},{20,22},{21,... | collective-permute-start | bytes 786440 | tf_op jit(solution)/shard_map/ppermute | solution.py:413
  23.8 12.9 %all-to-all-start = ((bf16[64,16,512]{2,1,0:T(8,128)(2,1)}), bf16[64,16,512]{2,1,0:T(8,128)(2,1)}, u32[]{:S(2)}, u32[]{:S(2)}) async-start(bf16[64,16,512]{2,1,0:T(8,128)(2,1)} %bitcast.13), calls=%async_computation | async-start | bytes 2097152 | tf_op jit(solution)/shard_map/all_to_all | solution.py:445
  36.8 3.6 %own.1 = (f32[4,512,128]{2,1,0:T(8,128)S(1)}, f32[4,512,128]{2,1,0:T(8,128)S(1)}, f32[512,128]{1,0:T(8,128)S(1)}, f32[512,128]{1,0:T(8,128)S(1)}) custom-call(s32[3]{0:T(128)S(1)} %pad_add_fusion.where_ref.refs_0_, bf16[512,1024]{1,0:T(8,128)(2,1)S(1)} %bitcast.11, bf16[512,1024]{1,0:T(8,128)(2,1)S(1)} %collective-permute-done.2.other_ref.refs_1_, ...), custom_call_target="tpu_custom_call" | custom-call | flops 40000000000 | bytes 4194304 | tf_op jit(solution)/shard_map/own/pallas_call | solution.py:300
  41.4 1.0 copy-done.4
  43.8 1.7 %collective-permute-start.8 = (bf16[1024,128]{1,0:T(8,128)(2,1)S(1)}, bf16[1024,128]{1,0:T(8,128)(2,1)S(1)}, u32[]{:S(2)}, u32[]{:S(2)}) collective-permute-start(bf16[1024,128]{1,0:T(8,128)(2,1)S(1)} %collective-permute-done.1.refs_2_), channel_id=1, source_target_pairs={{0,6},{1,7},{2,0},{3,1},{4,2},{5,3},{6,4},{7,5},{8,14},{9,15},{10,... | collective-permute-start | bytes 786440 | tf_op jit(solution)/shard_map/ppermute | solution.py:413
  45.5 2.3 %collective-permute-start.7 = (bf16[1024,128]{1,0:T(8,128)(2,1)S(1)}, bf16[1024,128]{1,0:T(8,128)(2,1)S(1)}, u32[]{:S(2)}, u32[]{:S(2)}) collective-permute-start(bf16[1024,128]{1,0:T(8,128)(2,1)S(1)} %collective-permute-done.1.refs_2_), channel_id=1, source_target_pairs={{0,4},{1,5},{2,6},{3,7},{4,0},{5,1},{6,2},{7,3},{8,12},{9,13},{10,... | collective-permute-start | bytes 786440 | tf_op jit(solution)/shard_map/ppermute | solution.py:413
  48.5 7.0 %all-to-all-done = bf16[64,16,512]{2,1,0:T(8,128)(2,1)} async-done(((bf16[64,16,512]{2,1,0:T(8,128)(2,1)}), bf16[64,16,512]{2,1,0:T(8,128)(2,1)}, u32[]{:S(2)}, u32[]{:S(2)}) %all-to-all-start) | async-done | bytes 1048608 | tf_op jit(solution)/shard_map/all_to_all | solution.py:445
  55.4 8.5 %conv.1 = bf16[32,16,512]{2,1,0:T(8,128)(2,1)} custom-call(bf16[32,2,16,512]{3,2,1,0:T(8,128)(2,1)} %bitcast.1.in_ref, bf16[1536,256]{1,0:T(8,128)(2,1)} %constant.37.clone.factor_ref, f32[128,256]{1,0:T(8,128)} %constant.38.clone.turn_ref), custom_call_target="tpu_custom_call" | custom-call | flops 5000000000 | bytes 2097152 | tf_op jit(solution)/shard_map/conv/pallas_call | solution.py:174
  63.9 5.0 %all-to-all-start.1 = ((bf16[32,16,512]{2,1,0:T(8,128)(2,1)}), bf16[32,16,512]{2,1,0:T(8,128)(2,1)}, u32[]{:S(2)}, u32[]{:S(2)}) async-start(bf16[32,16,512]{2,1,0:T(8,128)(2,1)} %conv.1), calls=%async_computation.1 | async-start | bytes 1048576 | tf_op jit(solution)/shard_map/all_to_all | solution.py:445
  69.0 17.4 %collective-permute-done.7.refs_4_ = bf16[1024,128]{1,0:T(8,128)(2,1)S(1)} collective-permute-done((bf16[1024,128]{1,0:T(8,128)(2,1)S(1)}, bf16[1024,128]{1,0:T(8,128)(2,1)S(1)}, u32[]{:S(2)}, u32[]{:S(2)}) %collective-permute-start.7) | collective-permute-done | bytes 262176 | tf_op jit(solution)/shard_map/ppermute | solution.py:413
  86.3 1.2 %copy-done.5 = f32[4,512,128]{2,1,0:T(8,128)S(1)} copy-done((f32[4,512,128]{2,1,0:T(8,128)S(1)}, f32[4,512,128]{2,1,0:T(8,128)}, u32[]{:S(2)}) %copy-start.5) | copy-done | bytes 1048600
  88.5 3.5 %back.3 = (bf16[512,512]{1,0:T(8,128)(2,1)S(1)}, f32[4,512]{1,0:T(4,128)S(1)}) custom-call(s32[3]{0:T(128)S(1)} %pad_add_fusion.where_ref.refs_0_, bf16[512,1024]{1,0:T(8,128)(2,1)S(1)} %collective-permute-done.2.other_ref.refs_1_, bf16[1024,128]{1,0:T(8,128)(2,1)S(1)} %collective-permute-done.1.refs_2_, ...), custom_call_target="tpu_custom_call" | custom-call | flops 99999997952 | bytes 4194304 | tf_op jit(solution)/shard_map/back/pallas_call | solution.py:361
  92.1 4.2 %collective-permute-start.10 = (f32[4,512]{1,0:T(4,128)S(1)}, f32[4,512]{1,0:T(4,128)S(1)}, u32[]{:S(2)}, u32[]{:S(2)}) collective-permute-start(f32[4,512]{1,0:T(4,128)S(1)} %get-tuple-element.34), channel_id=1, source_target_pairs={{0,1},{1,0},{2,3},{3,2},{4,5},{5,4},{6,7},{7,6},{8,9},{9,8},{10,11... | collective-permute-start | bytes 24584 | tf_op jit(solution)/shard_map/ppermute | solution.py:441
  96.4 3.6 %back.2 = (bf16[512,512]{1,0:T(8,128)(2,1)S(1)}, f32[4,512]{1,0:T(4,128)S(1)}) custom-call(s32[3]{0:T(128)S(1)} %pad_add_fusion.where_ref.refs_0_, bf16[512,1024]{1,0:T(8,128)(2,1)S(1)} %bitcast.12, bf16[1024,128]{1,0:T(8,128)(2,1)S(1)} %collective-permute-done.1.refs_2_, bf16[1024,128]{1,0:T(8,128)(2,1)S(1)} %collective-permute-done.6.refs_3_, ...), custom_call_target="tpu_custom_call" | custom-call | flops 99999997952 | bytes 4194304 | tf_op jit(solution)/shard_map/back/pallas_call | solution.py:361
  100.0 1.8 %merge.1 = (bf16[512,1024]{1,0:T(8,128)(2,1)}, f32[8,512]{1,0:T(8,128)}) custom-call(s32[3]{0:T(128)S(1)} %pad_add_fusion.where_ref.refs_0_, bf16[512,512]{1,0:T(8,128)(2,1)S(1)} %get-tuple-element.30.mine_ref, bf16[512,512]{1,0:T(8,128)(2,1)S(1)} %collective-permute-done.9.got_ref, f32[4,512]{1,0:T(4,128)S(1)} %get-tuple-element.33.mine_lse, ...), custom_call_target="tpu_custom_call" | custom-call | bytes 2097152 | tf_op jit(solution)/shard_map/merge/pallas_call | solution.py:397
  101.9 2.5 %gate.1 = bf16[512,512]{1,0:T(8,128)(2,1)} custom-call(bf16[512,512]{1,0:T(8,128)(2,1)} %bitcast.6.conv_ref, bf16[512,512]{1,0:T(8,128)(2,1)} %gate_ref.1, bf16[512,512]{1,0:T(8,128)(2,1)} %key_ref.5, bf16[512,512]{1,0:T(8,128)(2,1)} %value_ref.5, f32[1,512]{1,0:T(1,128)} %bitcast.14), custom_call_target="tpu_custom_call" | custom-call | flops 268435456 | bytes 2621440 | tf_op jit(solution)/shard_map/gate/pallas_call | solution.py:197
  (31 shorter events, 4.3 us)
Async XLA Ops:
  2.3 34.5 %collective-permute-start.2 = (bf16[512,1024]{1,0:T(8,128)(2,1)}, bf16[512,1024]{1,0:T(8,128)(2,1)S(1)}, u32[]{:S(2)}, u32[]{:S(2)}) collective-permute-start(bf16[512,1024]{1,0:T(8,128)(2,1)} %bitcast.10), channel_id=1, source_target_pairs={{0,1},{1,0},{2,3},{3,2},{4,5},{5,4},{6,7},{7,6},{8,9},{9,8},{10,11... | collective-permute-start | bytes 3145736 | tf_op jit(solution)/shard_map/ppermute | solution.py:441
  5.6 12.8 %collective-permute-start.1 = (bf16[1024,128]{1,0:T(8,128)(2,1)}, bf16[1024,128]{1,0:T(8,128)(2,1)S(1)}, u32[]{:S(2)}, u32[]{:S(2)}) collective-permute-start(bf16[1024,128]{1,0:T(8,128)(2,1)} %pack.1.after_ref.refs_0_), channel_id=1, source_target_pairs={{0,8},{1,9},{2,10},{3,11},{4,12},{5,13},{6,14},{7,15},{8,16},{9,17... | collective-permute-start | bytes 786440 | tf_op jit(solution)/shard_map/ppermute | solution.py:437
  7.0 15.4 %collective-permute-start = (bf16[1024,128]{1,0:T(8,128)(2,1)}, bf16[1024,128]{1,0:T(8,128)(2,1)S(1)}, u32[]{:S(2)}, u32[]{:S(2)}) collective-permute-start(bf16[1024,128]{1,0:T(8,128)(2,1)} %pack.1.after_ref.refs_0_), channel_id=1, source_target_pairs={{0,4},{1,5},{2,6},{3,7},{4,0},{5,1},{6,2},{7,3},{8,12},{9,13},{10,... | collective-permute-start | bytes 786440 | tf_op jit(solution)/shard_map/ppermute | solution.py:413
  10.1 26.6 %collective-permute-start.4 = (bf16[1024,128]{1,0:T(8,128)(2,1)}, bf16[1024,128]{1,0:T(8,128)(2,1)S(1)}, u32[]{:S(2)}, u32[]{:S(2)}) collective-permute-start(bf16[1024,128]{1,0:T(8,128)(2,1)} %pack.1.after_ref.refs_0_), channel_id=1, source_target_pairs={{2,0},{3,1},{4,2},{5,3},{6,4},{7,5},{10,8},{11,9},{12,10},{13,11},... | collective-permute-start | bytes 786440 | tf_op jit(solution)/shard_map/ppermute | solution.py:413
  11.4 25.4 %collective-permute-start.3 = (bf16[1024,128]{1,0:T(8,128)(2,1)}, bf16[1024,128]{1,0:T(8,128)(2,1)S(1)}, u32[]{:S(2)}, u32[]{:S(2)}) collective-permute-start(bf16[1024,128]{1,0:T(8,128)(2,1)} %pack.1.after_ref.refs_0_), channel_id=1, source_target_pairs={{0,2},{1,3},{2,4},{3,5},{4,6},{5,7},{8,10},{9,11},{10,12},{11,13},... | collective-permute-start | bytes 786440 | tf_op jit(solution)/shard_map/ppermute | solution.py:413
  22.5 14.3 %collective-permute-start.5 = (bf16[1024,128]{1,0:T(8,128)(2,1)S(1)}, bf16[1024,128]{1,0:T(8,128)(2,1)}, u32[]{:S(2)}, u32[]{:S(2)}) collective-permute-start(bf16[1024,128]{1,0:T(8,128)(2,1)S(1)} %collective-permute-done.refs_3_), channel_id=1, source_target_pairs={{4,6},{5,7},{2,0},{3,1},{12,14},{13,15},{10,8},{11,9},{20,22},{21,... | collective-permute-start | bytes 786440 | tf_op jit(solution)/shard_map/ppermute | solution.py:413
  23.8 13.0 %copy-start = (bf16[1024,128]{1,0:T(8,128)(2,1)S(1)}, bf16[1024,128]{1,0:T(8,128)(2,1)}, u32[]{:S(2)}) copy-start(bf16[1024,128]{1,0:T(8,128)(2,1)} %pack.1.after_ref.refs_0_) | copy-start | bytes 786436
  23.8 13.0 %copy-start.1 = (bf16[512,1,1024]{2,0,1:T(8,128)(2,1)S(1)}, bf16[512,1,1024]{2,0,1:T(8,128)(2,1)}, u32[]{:S(2)}) copy-start(bf16[512,1,1024]{2,0,1:T(8,128)(2,1)} %param.15) | copy-start | bytes 3145732
  23.8 31.7 %all-to-all-start = ((bf16[64,16,512]{2,1,0:T(8,128)(2,1)}), bf16[64,16,512]{2,1,0:T(8,128)(2,1)}, u32[]{:S(2)}, u32[]{:S(2)}) async-start(bf16[64,16,512]{2,1,0:T(8,128)(2,1)} %bitcast.13), calls=%async_computation | async-start | bytes 2097152 | tf_op jit(solution)/shard_map/all_to_all | solution.py:445
  40.4 1.0 copy-start.2
  41.4 1.0 copy-start.4
  42.4 0.7 copy-start.6
  43.1 0.7 copy-start.8
  43.8 25.2 %collective-permute-start.8 = (bf16[1024,128]{1,0:T(8,128)(2,1)S(1)}, bf16[1024,128]{1,0:T(8,128)(2,1)S(1)}, u32[]{:S(2)}, u32[]{:S(2)}) collective-permute-start(bf16[1024,128]{1,0:T(8,128)(2,1)S(1)} %collective-permute-done.1.refs_2_), channel_id=1, source_target_pairs={{0,6},{1,7},{2,0},{3,1},{4,2},{5,3},{6,4},{7,5},{8,14},{9,15},{10,... | collective-permute-start | bytes 786440 | tf_op jit(solution)/shard_map/ppermute | solution.py:413
  45.5 40.9 %collective-permute-start.7 = (bf16[1024,128]{1,0:T(8,128)(2,1)S(1)}, bf16[1024,128]{1,0:T(8,128)(2,1)S(1)}, u32[]{:S(2)}, u32[]{:S(2)}) collective-permute-start(bf16[1024,128]{1,0:T(8,128)(2,1)S(1)} %collective-permute-done.1.refs_2_), channel_id=1, source_target_pairs={{0,4},{1,5},{2,6},{3,7},{4,0},{5,1},{6,2},{7,3},{8,12},{9,13},{10,... | collective-permute-start | bytes 786440 | tf_op jit(solution)/shard_map/ppermute | solution.py:413
  47.7 38.6 %collective-permute-start.6 = (bf16[1024,128]{1,0:T(8,128)(2,1)S(1)}, bf16[1024,128]{1,0:T(8,128)(2,1)S(1)}, u32[]{:S(2)}, u32[]{:S(2)}) collective-permute-start(bf16[1024,128]{1,0:T(8,128)(2,1)S(1)} %collective-permute-done.1.refs_2_), channel_id=1, source_target_pairs={{0,2},{1,3},{2,4},{3,5},{4,6},{5,7},{6,0},{7,1},{8,10},{9,11},{10,... | collective-permute-start | bytes 786440 | tf_op jit(solution)/shard_map/ppermute | solution.py:413
  63.9 22.4 %copy-start.7 = (f32[512,128]{1,0:T(8,128)S(1)}, f32[512,128]{1,0:T(8,128)}, u32[]{:S(2)}) copy-start(f32[512,128]{1,0:T(8,128)} %copy-done.6) | copy-start | bytes 786436
  63.9 37.9 %all-to-all-start.1 = ((bf16[32,16,512]{2,1,0:T(8,128)(2,1)}), bf16[32,16,512]{2,1,0:T(8,128)(2,1)}, u32[]{:S(2)}, u32[]{:S(2)}) async-start(bf16[32,16,512]{2,1,0:T(8,128)(2,1)} %conv.1), calls=%async_computation.1 | async-start | bytes 1048576 | tf_op jit(solution)/shard_map/all_to_all | solution.py:445
  86.3 1.2 %copy-start.5 = (f32[4,512,128]{2,1,0:T(8,128)S(1)}, f32[4,512,128]{2,1,0:T(8,128)}, u32[]{:S(2)}) copy-start(f32[4,512,128]{2,1,0:T(8,128)} %copy-done.4) | copy-start | bytes 3145732
  87.6 0.9 copy-start.9
  88.5 7.9 %copy-start.3 = (f32[4,512,128]{2,1,0:T(8,128)S(1)}, f32[4,512,128]{2,1,0:T(8,128)}, u32[]{:S(2)}) copy-start(f32[4,512,128]{2,1,0:T(8,128)} %copy-done.2) | copy-start | bytes 3145732
  92.1 7.9 %collective-permute-start.10 = (f32[4,512]{1,0:T(4,128)S(1)}, f32[4,512]{1,0:T(4,128)S(1)}, u32[]{:S(2)}, u32[]{:S(2)}) collective-permute-start(f32[4,512]{1,0:T(4,128)S(1)} %get-tuple-element.34), channel_id=1, source_target_pairs={{0,1},{1,0},{2,3},{3,2},{4,5},{5,4},{6,7},{7,6},{8,9},{9,8},{10,11... | collective-permute-start | bytes 24584 | tf_op jit(solution)/shard_map/ppermute | solution.py:441
  96.3 3.7 %collective-permute-start.9 = (bf16[512,512]{1,0:T(8,128)(2,1)S(1)}, bf16[512,512]{1,0:T(8,128)(2,1)S(1)}, u32[]{:S(2)}, u32[]{:S(2)}) collective-permute-start(bf16[512,512]{1,0:T(8,128)(2,1)S(1)} %get-tuple-element.32), channel_id=1, source_target_pairs={{0,1},{1,0},{2,3},{3,2},{4,5},{5,4},{6,7},{7,6},{8,9},{9,8},{10,11... | collective-permute-start | bytes 1572872 | tf_op jit(solution)/shard_map/ppermute | solution.py:441
